TPU v7x, 128 devices: a whole 4x4x4 slice. The times are simulated.
128 devices in a mesh: depth: 32 (over y, x, core), tile: 4 (over z).
Axes of the slice: x: 4, y: 4, z: 4, core: 2. Of those that a mesh axis runs over, the one named last changes fastest.
Arguments:
- scalar_field: float32 [512, 4, 512, 512], P('depth', 'tile'), may hold values from -12 to 12
- depth_rank: int32 [32, 4], P('depth', 'tile'), may hold values from 0 to 31, as said below
- palette: float32 [3, 2], replicated, may hold values from -1.5 to 1.5
- extinction: float32 [2], replicated, may hold values from 0.4 to 1.6
Outputs:
- scanline_image: float32 [4, 1, 512, 2048], P(None, None, ('depth', 'tile'))
Inputs may be any that keep to these rules, and one draw needn't show every extreme that they name: In every column of depth_rank each of 0 to 31 appears once, and for every k the depth indices that agree in their k lowest bits hold a contiguous range of ranks.
All inputs are finite; a program needn't handle non-finite values.
Results may differ from a plain program's by a relative error of at most 0.000034.
Values sent between devices are 32-bit elements; how exact they have to be, the bound alone decides.
No kernel may reach another device: no remote copies, remote signals or barrier semaphores. Data moves between devices by JAX's collectives and lax.ppermute only.
A program may use at most 256 MiB of HBM per device.

v0:
```python
import jax
import jax.numpy as jnp
from jax import lax
from jax.sharding import PartitionSpec as P

TILES_X = 4


def partner_2(x, axis, distance):
    return lax.ppermute(x, axis, [(i, i ^ 1 << distance) for i in range(lax.axis_size(axis))])


def composite_over(nearer, farther):
    return nearer + (1.0 - nearer[3:4]) * farther


def march_brick(samples_in, palette, extinction, depth_total):
    slope = palette[:, 0][:, None, None]
    offset = palette[:, 1][:, None, None]
    accumulated = jnp.zeros((4,) + samples_in.shape[1:], jnp.float32)
    for position in range(samples_in.shape[0]):
        sample_slice = samples_in[position]
        rate = extinction[0] * sample_slice * sample_slice + extinction[1]
        opacity = 1.0 - jnp.exp(-rate / depth_total)
        colour = jax.nn.sigmoid(slope * sample_slice[None] + offset)
        sample = jnp.concatenate([opacity[None] * colour, opacity[None]], axis=0)
        accumulated = composite_over(accumulated, sample)
    return accumulated


def body(scalar_field, depth_rank, palette, extinction):
    depth_count = lax.axis_size("depth")
    tile_count = lax.axis_size("tile")
    samples_in = scalar_field[:, 0]
    partial_value = march_brick(
        samples_in, palette, extinction, scalar_field.shape[0] * depth_count
    )
    width = partial_value.shape[2]
    tile_rows = tile_count // TILES_X
    tree_depth = depth_count.bit_length() - 1
    depth_place = lax.axis_index("depth")
    current = partial_value
    for tree_level in reversed(range(tree_depth)):
        half_rows = current.shape[1] // 2
        upper_half = depth_place >> tree_level & 1
        kept_rows = lax.dynamic_slice_in_dim(current, upper_half * half_rows, half_rows, 1)
        sent_rows = lax.dynamic_slice_in_dim(current, (1 - upper_half) * half_rows, half_rows, 1)
        partner, partner_rank = partner_2((sent_rows, depth_rank), "depth", tree_level)
        in_front = depth_rank[0, 0] < partner_rank[0, 0]
        nearer = jnp.where(in_front, kept_rows, partner)
        farther = jnp.where(in_front, partner, kept_rows)
        current = composite_over(nearer, farther)
    small_rows = current.shape[1] // tile_count
    outgoing = current.reshape(4, tile_count, small_rows, width)
    gathered = lax.all_to_all(outgoing, "tile", split_axis=1, concat_axis=1, tiled=True)
    small_rows = gathered.shape[2]
    arranged = gathered.reshape(4, tile_rows, TILES_X, small_rows, width).transpose(0, 1, 3, 2, 4)
    return arranged.reshape(4, tile_rows, small_rows, TILES_X * width)


def solution(mesh):
    in_specs = (P("depth", "tile", None, None), P("depth", "tile"), P(), P())
    out_specs = P(None, None, ("depth", "tile"), None)
    return jax.shard_map(body, mesh=mesh, in_specs=in_specs, out_specs=out_specs, check_vma=False)
```

profile of v0, /device:TPU:6, one launch (start us, length us, event | category | flops | bytes accessed | tf_op | source)
XLA Modules:
  0.0 244.0 jit_solution(5197604287231313510)
XLA Ops:
  1.4 13.3 %slice_bitcast_fusion = (f32[512,512]{1,0:T(8,128)}, f32[512,512]{1,0:T(8,128)}, f32[512,512]{1,0:T(8,128)}, f32[512,512]{1,0:T(8,128)}, f32[512,512]{1,0:T(8,12...) fusion(f32[16,1,512,512]{3,2,1,0:T(8,128)} %param.4), kind=kLoop, calls=%fused_computation.269 | loop fusion | bytes 33554432 | tf_op jit(solution)/shard_map/squeeze | solution.py:22
  16.7 8.1 %fusion.168 = (f32[512,512]{1,0:T(8,128)}, f32[512,512]{1,0:T(8,128)}, f32[512,512]{1,0:T(8,128)}, f32[512,512]{1,0:T(8,128)}, f32[512,512]{1,0:T(8,128)}, /*ind...) fusion(f32[]{:T(128)} %bitcast.7, f32[]{:T(128)} %bitcast.5, ...), kind=kLoop, calls=%fused_computation.234 | loop fusion | flops 25427968 | bytes 34603016 | tf_op jit(solution)/shard_map/sub | solution.py:24
  24.9 8.0 %fusion.173 = (f32[1,512,512]{2,1,0:T(8,128)}, f32[1,512,512]{2,1,0:T(8,128)}, f32[1,512,512]{2,1,0:T(8,128)}, f32[1,512,512]{2,1,0:T(8,128)}, f32[1,512,512]{2,...) fusion(f32[16,1,512,512]{3,2,1,0:T(8,128)S(1)} %bitcast.155, ...), kind=kLoop, calls=%fused_computation.239 | loop fusion | flops 25165824 | bytes 33554440 | tf_op jit(solution)/shard_map/sub | solution.py:24
  32.9 15.0 %divide_multiply_fusion = (f32[3,512,512]{2,1,0:T(8,128)S(1)}, f32[3,512,512]{2,1,0:T(8,128)}, f32[3,512,512]{2,1,0:T(8,128)}, f32[3,512,512]{2,1,0:T(8,128)}, f...) fusion(f32[512,512]{1,0:T(8,128)} %get-tuple-element.24, ...), kind=kLoop, calls=%fused_computation.30 | loop fusion | flops 37748736 | bytes 41943064 | tf_op jit(solution)/shard_map/mul | solution.py:26
  47.8 13.2 %divide_multiply_fusion.1 = (f32[3,512,512]{2,1,0:T(8,128)S(1)}, f32[3,512,512]{2,1,0:T(8,128)}, f32[3,512,512]{2,1,0:T(8,128)}, f32[3,512,512]{2,1,0:T(8,128)},...) fusion(f32[512,512]{1,0:T(8,128)} %get-tuple-element.39, ...), kind=kLoop, calls=%fused_computation.31 | loop fusion | flops 37748736 | bytes 41943064 | tf_op jit(solution)/shard_map/mul | solution.py:26
  61.0 4.8 %maximum_add_fusion = f32[4,512,512]{2,1,0:T(8,128)S(1)} fusion(f32[1,512,512]{2,1,0:T(8,128)} %get-tuple-element.41, f32[3,512,512]{2,1,0:T(8,128)} %get-tuple-element.71, f32[1,512,512]{2,1,0:T(8,128)} %get-tuple-element.42, f32[3,512,512]{2,1,0:T(8,128)} %get-tuple-element.57, f32[512,512]{1,0:T(8,128)} %get-tuple-element.22), kind=kLoop, calls=%fused_computation | loop fusion | flops 4194304 | bytes 13631488 | tf_op jit(solution)/shard_map/add | solution.py:14
  66.9 3.8 %fusion = f32[4,512,512]{2,1,0:T(8,128)S(1)} fusion(f32[4,512,512]{2,1,0:T(8,128)S(1)} %maximum_add_fusion, f32[1,512,512]{2,1,0:T(8,128)} %get-tuple-element.43, f32[3,512,512]{2,1,0:T(8,128)} %get-tuple-element.58, f32[512,512]{1,0:T(8,128)} %fusion.187), kind=kLoop, calls=%fused_computation.3 | loop fusion | flops 3145728 | bytes 13631488 | tf_op jit(solution)/shard_map/add | solution.py:14
  71.8 3.4 %fusion.1 = f32[4,512,512]{2,1,0:T(8,128)S(1)} fusion(f32[4,512,512]{2,1,0:T(8,128)S(1)} %fusion, f32[1,512,512]{2,1,0:T(8,128)S(1)} %copy-done.17, f32[3,512,512]{2,1,0:T(8,128)} %get-tuple-element.59, f32[512,512]{1,0:T(8,128)} %fusion.186), kind=kLoop, calls=%fused_computation.5 | loop fusion | flops 3145728 | bytes 13631488 | tf_op jit(solution)/shard_map/add | solution.py:14
  76.2 3.8 %fusion.2 = f32[4,512,512]{2,1,0:T(8,128)S(1)} fusion(f32[4,512,512]{2,1,0:T(8,128)S(1)} %fusion.1, f32[1,512,512]{2,1,0:T(8,128)} %get-tuple-element.45, f32[3,512,512]{2,1,0:T(8,128)} %get-tuple-element.60, f32[512,512]{1,0:T(8,128)} %fusion.185), kind=kLoop, calls=%fused_computation.7 | loop fusion | flops 3145728 | bytes 13631488 | tf_op jit(solution)/shard_map/add | solution.py:14
  81.0 3.4 %fusion.3 = f32[4,512,512]{2,1,0:T(8,128)S(1)} fusion(f32[4,512,512]{2,1,0:T(8,128)S(1)} %fusion.2, f32[1,512,512]{2,1,0:T(8,128)S(1)} %copy-done.16, f32[3,512,512]{2,1,0:T(8,128)} %get-tuple-element.61, f32[512,512]{1,0:T(8,128)} %fusion.184), kind=kLoop, calls=%fused_computation.9 | loop fusion | flops 3145728 | bytes 13631488 | tf_op jit(solution)/shard_map/add | solution.py:14
  85.5 3.8 %fusion.4 = f32[4,512,512]{2,1,0:T(8,128)S(1)} fusion(f32[4,512,512]{2,1,0:T(8,128)S(1)} %fusion.3, f32[1,512,512]{2,1,0:T(8,128)} %get-tuple-element.47, f32[3,512,512]{2,1,0:T(8,128)} %get-tuple-element.62, f32[512,512]{1,0:T(8,128)} %fusion.183), kind=kLoop, calls=%fused_computation.11 | loop fusion | flops 3145728 | bytes 13631488 | tf_op jit(solution)/shard_map/add | solution.py:14
  90.3 2.5 %fusion.5 = f32[4,512,512]{2,1,0:T(8,128)S(1)} fusion(f32[4,512,512]{2,1,0:T(8,128)S(1)} %fusion.4, f32[1,512,512]{2,1,0:T(8,128)S(1)} %copy-done.15, f32[3,512,512]{2,1,0:T(8,128)S(1)} %get-tuple-element.63, f32[512,512]{1,0:T(8,128)} %fusion.182), kind=kLoop, calls=%fused_computation.13 | loop fusion | flops 3145728 | bytes 13631488 | tf_op jit(solution)/shard_map/add | solution.py:14
  95.1 2.9 %fusion.6 = f32[4,512,512]{2,1,0:T(8,128)S(1)} fusion(f32[4,512,512]{2,1,0:T(8,128)S(1)} %fusion.5, f32[1,512,512]{2,1,0:T(8,128)} %get-tuple-element.49, f32[3,512,512]{2,1,0:T(8,128)S(1)} %copy-done.5, f32[512,512]{1,0:T(8,128)} %fusion.181), kind=kLoop, calls=%fused_computation.15 | loop fusion | flops 3145728 | bytes 13631488 | tf_op jit(solution)/shard_map/add | solution.py:14
  100.2 2.7 %fusion.7 = f32[4,512,512]{2,1,0:T(8,128)S(1)} fusion(f32[4,512,512]{2,1,0:T(8,128)S(1)} %fusion.6, f32[1,512,512]{2,1,0:T(8,128)S(1)} %copy-done.14, f32[3,512,512]{2,1,0:T(8,128)S(1)} %copy-done.4, f32[512,512]{1,0:T(8,128)} %fusion.180), kind=kLoop, calls=%fused_computation.17 | loop fusion | flops 3145728 | bytes 13631488 | tf_op jit(solution)/shard_map/add | solution.py:14
  105.2 2.9 %fusion.8 = f32[4,512,512]{2,1,0:T(8,128)S(1)} fusion(f32[4,512,512]{2,1,0:T(8,128)S(1)} %fusion.7, f32[1,512,512]{2,1,0:T(8,128)} %get-tuple-element.51, f32[3,512,512]{2,1,0:T(8,128)S(1)} %copy-done.3, f32[512,512]{1,0:T(8,128)} %fusion.179), kind=kLoop, calls=%fused_computation.19 | loop fusion | flops 3145728 | bytes 13631488 | tf_op jit(solution)/shard_map/add | solution.py:14
  116.9 4.0 %fusion.13 = f32[4,512,512]{2,1,0:T(8,128)S(1)} fusion(f32[4,512,512]{2,1,0:T(8,128)} %copy-done.2, f32[1,512,512]{2,1,0:T(8,128)} %get-tuple-element.40, f32[3,512,512]{2,1,0:T(8,128)S(1)} %get-tuple-element.56, f32[512,512]{1,0:T(8,128)} %fusion.174), kind=kLoop, calls=%fused_computation.29 | loop fusion | flops 3145728 | bytes 13631488 | tf_op jit(solution)/shard_map/add | solution.py:14
  124.4 3.2 %collective-permute-start.5 = (f32[4,256,512]{2,1,0:T(8,128)}, f32[4,256,512]{2,1,0:T(8,128)S(1)}, u32[]{:S(2)}, u32[]{:S(2)}) collective-permute-start(f32[4,256,512]{2,1,0:T(8,128)} %constant_dynamic-slice_fusion.4), channel_id=1, source_target_pairs={{0,64},{4,68},{8,72},{12,76},{16,80},{20,84},{24,88},{28,92},{32,9... | collective-permute-start | bytes 6291464 | tf_op jit(solution)/shard_map/ppermute | solution.py:10
  128.6 45.0 %collective-permute-done.4 = s32[1,1]{1,0:T(1,128)} collective-permute-done((s32[1,1]{1,0:T(1,128)}, s32[1,1]{1,0:T(1,128)}, u32[]{:S(2)}, u32[]{:S(2)}) %collective-permute-start.4) | collective-permute-done | bytes 36 | tf_op jit(solution)/shard_map/ppermute | solution.py:10
  174.2 2.9 %dynamic-slice_select_fusion = f32[4,256,512]{2,1,0:T(8,128)S(1)} fusion(f32[4,256,512]{2,1,0:T(8,128)S(1)} %collective-permute-done.5, f32[4,512,512]{2,1,0:T(8,128)} %copy-done, s32[]{:T(128)S(6)} %select_n.95, pred[]{:T(512)} %bitcast.4), kind=kLoop, calls=%fused_computation.47 | loop fusion | flops 524288 | bytes 6291461 | tf_op jit(solution)/shard_map/jit(_where)/select_n | solution.py:50
  177.8 2.2 multiply_add_fusion
  183.1 22.2 %collective-permute-done.3 = s32[1,1]{1,0:T(1,128)} collective-permute-done((s32[1,1]{1,0:T(1,128)}, s32[1,1]{1,0:T(1,128)}, u32[]{:S(2)}, u32[]{:S(2)}) %collective-permute-start.3) | collective-permute-done | bytes 36 | tf_op jit(solution)/shard_map/ppermute | solution.py:10
  212.1 9.5 %collective-permute-done.2 = s32[1,1]{1,0:T(1,128)} collective-permute-done((s32[1,1]{1,0:T(1,128)}, s32[1,1]{1,0:T(1,128)}, u32[]{:S(2)}, u32[]{:S(2)}) %collective-permute-start.2) | collective-permute-done | bytes 36 | tf_op jit(solution)/shard_map/ppermute | solution.py:10
  224.7 4.4 %collective-permute-done.1 = s32[1,1]{1,0:T(1,128)} collective-permute-done((s32[1,1]{1,0:T(1,128)}, s32[1,1]{1,0:T(1,128)}, u32[]{:S(2)}, u32[]{:S(2)}) %collective-permute-start.1) | collective-permute-done | bytes 36 | tf_op jit(solution)/shard_map/ppermute | solution.py:10
  232.3 11.1 %all_to_all.5 = f32[4,4,4,512]{3,2,0,1:T(4,128)S(1)} all-to-all(f32[4,4,4,512]{3,2,0,1:T(4,128)S(1)} %copy.7), channel_id=1, replica_groups=mesh['depth'=32,'tile'=4] {'tile'}, dimensions={1} | all-to-all | bytes 262144 | tf_op jit(solution)/shard_map/all_to_all | solution.py:55
  (103 shorter events, 44.0 us)
Async XLA Ops:
  0.0 14.7 %slice-start = ((s8[16777216]{0:T(1024)(128)(4,1)}), s8[4194304]{0:T(1024)(128)(4,1)S(1)}, s32[]{:S(2)}) async-start(s8[16777216]{0:T(1024)(128)(4,1)} %bitcast.154), calls=%async_computation.1 | async-start | bytes 8388608
  1.4 13.3 %slice-start.1 = ((s8[16777216]{0:T(1024)(128)(4,1)}), s8[4194304]{0:T(1024)(128)(4,1)S(1)}, s32[]{:S(2)}) async-start(s8[16777216]{0:T(1024)(128)(4,1)} %bitcast.154), calls=%async_computation.2 | async-start | bytes 8388608
  1.4 13.3 %slice-start.2 = ((s8[16777216]{0:T(1024)(128)(4,1)}), s8[4194304]{0:T(1024)(128)(4,1)S(1)}, s32[]{:S(2)}) async-start(s8[16777216]{0:T(1024)(128)(4,1)} %bitcast.154), calls=%async_computation.3 | async-start | bytes 8388608
  1.4 15.3 %slice-start.3 = ((s8[16777216]{0:T(1024)(128)(4,1)}), s8[4194304]{0:T(1024)(128)(4,1)S(1)}, s32[]{:S(2)}) async-start(s8[16777216]{0:T(1024)(128)(4,1)} %bitcast.154), calls=%async_computation.4 | async-start | bytes 8388608
  24.8 8.0 %copy-start.18 = (f32[3,2]{0,1:T(2,128)S(1)}, f32[3,2]{0,1:T(2,128)}, u32[]{:S(2)}) copy-start(f32[3,2]{0,1:T(2,128)} %param.6) | copy-start | bytes 76
  32.8 15.0 %copy-start.7 = (f32[512,512]{1,0:T(8,128)S(1)}, f32[512,512]{1,0:T(8,128)}, u32[]{:S(2)}) copy-start(f32[512,512]{1,0:T(8,128)} %get-tuple-element.25) | copy-start | bytes 3145732
  32.8 15.0 %copy-start.8 = (f32[512,512]{1,0:T(8,128)S(1)}, f32[512,512]{1,0:T(8,128)}, u32[]{:S(2)}) copy-start(f32[512,512]{1,0:T(8,128)} %get-tuple-element.26) | copy-start | bytes 3145732
  66.9 4.9 %copy-start.17 = (f32[1,512,512]{2,1,0:T(8,128)S(1)}, f32[1,512,512]{2,1,0:T(8,128)}, u32[]{:S(2)}) copy-start(f32[1,512,512]{2,1,0:T(8,128)} %get-tuple-element.44) | copy-start | bytes 3145732
  76.2 4.8 %copy-start.16 = (f32[1,512,512]{2,1,0:T(8,128)S(1)}, f32[1,512,512]{2,1,0:T(8,128)}, u32[]{:S(2)}) copy-start(f32[1,512,512]{2,1,0:T(8,128)} %get-tuple-element.46) | copy-start | bytes 3145732
  85.5 4.8 %copy-start.15 = (f32[1,512,512]{2,1,0:T(8,128)S(1)}, f32[1,512,512]{2,1,0:T(8,128)}, u32[]{:S(2)}) copy-start(f32[1,512,512]{2,1,0:T(8,128)} %get-tuple-element.48) | copy-start | bytes 3145732
  95.1 4.0 %copy-start.14 = (f32[1,512,512]{2,1,0:T(8,128)S(1)}, f32[1,512,512]{2,1,0:T(8,128)}, u32[]{:S(2)}) copy-start(f32[1,512,512]{2,1,0:T(8,128)} %get-tuple-element.50) | copy-start | bytes 3145732
  105.2 3.0 %copy-start.13 = (f32[1,512,512]{2,1,0:T(8,128)S(1)}, f32[1,512,512]{2,1,0:T(8,128)}, u32[]{:S(2)}) copy-start(f32[1,512,512]{2,1,0:T(8,128)} %get-tuple-element.52) | copy-start | bytes 3145732
  124.4 49.8 %collective-permute-start.5 = (f32[4,256,512]{2,1,0:T(8,128)}, f32[4,256,512]{2,1,0:T(8,128)S(1)}, u32[]{:S(2)}, u32[]{:S(2)}) collective-permute-start(f32[4,256,512]{2,1,0:T(8,128)} %constant_dynamic-slice_fusion.4), channel_id=1, source_target_pairs={{0,64},{4,68},{8,72},{12,76},{16,80},{20,84},{24,88},{28,92},{32,9... | collective-permute-start | bytes 6291464 | tf_op jit(solution)/shard_map/ppermute | solution.py:10
  127.6 46.1 %collective-permute-start.4 = (s32[1,1]{1,0:T(1,128)}, s32[1,1]{1,0:T(1,128)}, u32[]{:S(2)}, u32[]{:S(2)}) collective-permute-start(s32[1,1]{1,0:T(1,128)} %param.5), channel_id=1, source_target_pairs={{0,64},{4,68},{8,72},{12,76},{16,80},{20,84},{24,88},{28,92},{32,9... | collective-permute-start | bytes 20 | tf_op jit(solution)/shard_map/ppermute | solution.py:10
  174.2 2.9 %copy-start.6 = (f32[4,256,512]{2,1,0:T(8,128)}, f32[4,256,512]{2,1,0:T(8,128)S(1)}, u32[]{:S(2)}) copy-start(f32[4,256,512]{2,1,0:T(8,128)S(1)} %collective-permute-done.5) | copy-start | bytes 6291460
  174.2 3.6 %copy-start.1 = (f32[4,512,512]{2,1,0:T(8,128)S(1)}, f32[4,512,512]{2,1,0:T(8,128)}, u32[]{:S(2)}) copy-start(f32[4,512,512]{2,1,0:T(8,128)} %copy-done) | copy-start | bytes 12582916
  181.1 24.9 %collective-permute-start.6 = (f32[4,128,512]{2,1,0:T(8,128)}, f32[4,128,512]{2,1,0:T(8,128)S(1)}, u32[]{:S(2)}, u32[]{:S(2)}) collective-permute-start(f32[4,128,512]{2,1,0:T(8,128)} %constant_dynamic-slice_fusion.3), channel_id=1, source_target_pairs={{0,32},{4,36},{8,40},{12,44},{16,48},{20,52},{24,56},{28,60},{32,0... | collective-permute-start | bytes 3145736 | tf_op jit(solution)/shard_map/ppermute | solution.py:10
  182.6 22.7 %collective-permute-start.3 = (s32[1,1]{1,0:T(1,128)}, s32[1,1]{1,0:T(1,128)}, u32[]{:S(2)}, u32[]{:S(2)}) collective-permute-start(s32[1,1]{1,0:T(1,128)} %param.5), channel_id=1, source_target_pairs={{0,32},{4,36},{8,40},{12,44},{16,48},{20,52},{24,56},{28,60},{32,0... | collective-permute-start | bytes 20 | tf_op jit(solution)/shard_map/ppermute | solution.py:10
  208.5 13.8 %collective-permute-start.7 = (f32[4,64,512]{2,1,0:T(8,128)S(1)}, f32[4,64,512]{2,1,0:T(8,128)S(1)}, u32[]{:S(2)}, u32[]{:S(2)}) collective-permute-start(f32[4,64,512]{2,1,0:T(8,128)S(1)} %constant_dynamic-slice_fusion.2), channel_id=1, source_target_pairs={{0,16},{4,20},{8,24},{12,28},{16,0},{20,4},{24,8},{28,12},{32,48},... | collective-permute-start | bytes 1572872 | tf_op jit(solution)/shard_map/ppermute | solution.py:10
  210.0 11.6 %collective-permute-start.2 = (s32[1,1]{1,0:T(1,128)}, s32[1,1]{1,0:T(1,128)}, u32[]{:S(2)}, u32[]{:S(2)}) collective-permute-start(s32[1,1]{1,0:T(1,128)} %param.5), channel_id=1, source_target_pairs={{0,16},{4,20},{8,24},{12,28},{16,0},{20,4},{24,8},{28,12},{32,48},... | collective-permute-start | bytes 20 | tf_op jit(solution)/shard_map/ppermute | solution.py:10
  222.6 7.1 %collective-permute-start.8 = (f32[4,32,512]{2,1,0:T(8,128)S(1)}, f32[4,32,512]{2,1,0:T(8,128)S(1)}, u32[]{:S(2)}, u32[]{:S(2)}) collective-permute-start(f32[4,32,512]{2,1,0:T(8,128)S(1)} %constant_dynamic-slice_fusion.1), channel_id=1, source_target_pairs={{0,8},{4,12},{8,0},{12,4},{16,24},{20,28},{24,16},{28,20},{32,40},... | collective-permute-start | bytes 786440 | tf_op jit(solution)/shard_map/ppermute | solution.py:10
  223.5 5.6 %collective-permute-start.1 = (s32[1,1]{1,0:T(1,128)}, s32[1,1]{1,0:T(1,128)}, u32[]{:S(2)}, u32[]{:S(2)}) collective-permute-start(s32[1,1]{1,0:T(1,128)} %param.5), channel_id=1, source_target_pairs={{0,8},{4,12},{8,0},{12,4},{16,24},{20,28},{24,16},{28,20},{32,40},... | collective-permute-start | bytes 20 | tf_op jit(solution)/shard_map/ppermute | solution.py:10
  229.9 2.2 collective-permute-start.9
  229.9 1.5 collective-permute-start
  (9 other events, 16.0 us)
where the time goes:
time: 245 us; the launch traced here: 244 us
  other arithmetic  105 us (43%)
  waiting for transfers between devices  82.1 us (34%)
  local copies, waits for them, and re-layouts  29.2 us (12%)
  starting transfers between devices  11.9 us (5%)
  blocking collectives  11.1 us (5%)
  between operations  4.34 us (2%)
    ppermute x10, waiting for transfers between devices, partner_2(): lax.ppermute(x, axis, [(i, i ^ 1 << distance) for i in range(lax.axis_siz...  82.1 us
    add x20, other arithmetic, composite_over(): return nearer + (1.0 - nearer[3:4]) * farther  46.8 us
    mul x2, other arithmetic, march_brick(): sample = jnp.concatenate([opacity[None] * colour, opacity[None]], axis=0)  28.1 us
    sub x2, other arithmetic, march_brick(): opacity = 1.0 - jnp.exp(-rate / depth_total)  16.1 us
    squeeze x1, local copies, waits for them, and re-layouts, march_brick(): sample_slice = samples_in[position]  13.3 us
    ppermute x10, starting transfers between devices, partner_2(): lax.ppermute(x, axis, [(i, i ^ 1 << distance) for i in range(lax.axis_siz...  11.9 us
    mul x19, other arithmetic, composite_over(): return nearer + (1.0 - nearer[3:4]) * farther  11.2 us
    all_to_all x1, blocking collectives, body(): lax.all_to_all(outgoing, 'tile', split_axis=1, concat_axis=1, tiled=True)  11.1 us
  transfers between devices with their start and end apart: 10, of which 5 were waited for; matrix products, arithmetic and copies ran while one was open for 0% of the time, Pallas kernels for 0%

commit v1 on v0

v1 whole, which is shorter than its diff:
```python
import functools
import math

import jax
import jax.numpy as jnp
from jax import lax
from jax.experimental import pallas as pl
from jax.experimental.pallas import tpu as pltpu
from jax.sharding import PartitionSpec as P

N = 4
SAMPLES = 16
LANES = 128
BLOCKS = 4
CHANNELS = 4
SLAB = BLOCKS * 8
VMEM = 40 * 2**20


def merge_two(a, b, a_in_front):
    one = jnp.float32(1.0)
    weight_a = jnp.where(a_in_front, one, b[3])
    weight_b = jnp.where(a_in_front, a[3], one)
    return [a[k] * weight_a + b[k] * weight_b for k in range(3)] + [a[3] * b[3]]


def merge_four(parts, ranks):
    even = merge_two(parts[0], parts[2], (ranks[0] < ranks[2])[None])
    odd = merge_two(parts[1], parts[3], (ranks[1] < ranks[3])[None])
    return merge_two(even, odd, (ranks[0] < ranks[1])[None])


def read_slab(ref, start):
    return ref[pl.ds(pl.multiple_of(start, SLAB), SLAB), :].reshape(BLOCKS, 8, LANES)


def write_slab(ref, start, value):
    ref[pl.ds(start, SLAB), :] = value.reshape(SLAB, LANES)


def march_kernel(place, palette, extinction, rank, *refs, count, depth_total):
    fields, messages = refs[:count], refs[count:]
    x_block = pl.program_id(0)
    odd_z = (place[3] & 1) == 1
    scale = -1.0 / (depth_total * math.log(2.0))
    quadratic = extinction[0] * scale
    constant = extinction[1] * scale
    slopes = [palette[k, 0] * 0.5 for k in range(3)]
    offsets = [palette[k, 1] * 0.5 for k in range(3)]
    width = 2 * LANES
    low_half = lax.broadcasted_iota(jnp.int32, (8, width), 0) < 4

    for j in range(count):
        field, first, second = fields[j], messages[2 * j], messages[2 * j + 1]

        def columns(block, carry, field=field, first=first, second=second):
            lanes = pl.ds(pl.multiple_of(block * width, width), width)
            shape = (2, 8, width)
            squares = jnp.zeros(shape, jnp.float32)
            through = jnp.ones(shape, jnp.float32)
            totals = [jnp.zeros(shape, jnp.float32) for _ in range(3)]
            for i in range(SAMPLES):
                s = field[i, :, :, lanes]
                squares = squares + s * s
                after = jnp.exp2(squares * quadratic + constant * float(i + 1))
                weight = through - after
                through = after
                for k in range(3):
                    totals[k] = totals[k] + weight * jnp.tanh(s * slopes[k] + offsets[k])
            opacity = 1.0 - through
            channels = [0.5 * (opacity + totals[k]) for k in range(3)] + [through]
            for k in range(CHANNELS):
                near, far = channels[k][0], channels[k][1]
                low = jnp.where(low_half, near, pltpu.roll(far, 4, 0))
                high = jnp.where(low_half, pltpu.roll(near, 4, 0), far)
                for half in range(2):
                    part = slice(half * LANES, (half + 1) * LANES)
                    row = pl.multiple_of(((k * N + x_block) * BLOCKS + block * 2 + half) * 8, 8)
                    first[pl.ds(row, 8), :] = jnp.where(odd_z, high[:, part], low[:, part])
                    second[pl.ds(row, 8), :] = jnp.where(odd_z, low[:, part], high[:, part])
            return carry

        lax.fori_loop(0, BLOCKS // 2, columns, 0)

    @pl.when(x_block == 0)
    def _():
        own = jnp.full((8, LANES), rank[0, 0].astype(jnp.float32))
        for message in messages:
            message[pl.ds(CHANNELS * N * SLAB, 8), :] = own


def march(field, place, palette, extinction, rank, y_flips, z_pair, depth_total):
    count = len(y_flips)
    rows = CHANNELS * N * SLAB + 8

    def field_index(flip):
        return lambda x, where: (0, 0, where[0] ^ flip, x, 0, (where[3] >> 1) ^ z_pair, 0, 0)

    smem = pl.BlockSpec(memory_space=pltpu.SMEM)
    pixels = count * N * 2 * 8 * 512
    return pl.pallas_call(
        functools.partial(march_kernel, count=count, depth_total=depth_total),
        grid_spec=pltpu.PrefetchScalarGridSpec(
            num_scalar_prefetch=1,
            grid=(N,),
            in_specs=[smem, smem, smem]
            + [
                pl.BlockSpec((SAMPLES, None, None, None, 2, None, 8, 512), field_index(flip))
                for flip in y_flips
            ],
            out_specs=[pl.BlockSpec((rows, LANES), lambda x, where: (0, 0))] * (2 * count),
        ),
        out_shape=[jax.ShapeDtypeStruct((rows, LANES), jnp.float32)] * (2 * count),
        compiler_params=pltpu.CompilerParams(vmem_limit_bytes=VMEM),
        cost_estimate=pl.CostEstimate(
            flops=pixels * SAMPLES * 20,
            bytes_accessed=pixels * 4 * (SAMPLES + 4),
            transcendentals=pixels * SAMPLES * 4,
        ),
        name="march",
    )(place, palette, extinction, rank, *([field] * count))


def merge_y_kernel(place, *refs):
    inputs, outputs = refs[:8], refs[8:]
    for tile in range(2):
        group = inputs[tile * 4 : tile * 4 + 4]
        ranks = [m[pl.ds(CHANNELS * N * SLAB, 8), :] for m in group]
        for flip in range(N):
            x = place[1] ^ flip
            parts = [[read_slab(m, (k * N + x) * SLAB) for k in range(CHANNELS)] for m in group]
            merged = merge_four(parts, ranks)
            for k in range(CHANNELS):
                write_slab(outputs[flip], (tile * CHANNELS + k) * SLAB, merged[k])
            outputs[flip][pl.ds(2 * CHANNELS * SLAB + tile * 8, 8), :] = ranks[0]


def merge_y(place, messages):
    rows = 2 * CHANNELS * SLAB + 16
    vmem = pl.BlockSpec(memory_space=pltpu.VMEM)
    return pl.pallas_call(
        merge_y_kernel,
        in_specs=[pl.BlockSpec(memory_space=pltpu.SMEM)] + [vmem] * 8,
        out_specs=[vmem] * N,
        out_shape=[jax.ShapeDtypeStruct((rows, LANES), jnp.float32)] * N,
        compiler_params=pltpu.CompilerParams(vmem_limit_bytes=VMEM),
        cost_estimate=pl.CostEstimate(flops=2**21, bytes_accessed=3 * 2**20, transcendentals=0),
        name="merge_y",
    )(place, *messages)


def merge_x_kernel(*refs):
    inputs, out = refs[:-1], refs[-1]
    for pair in range(2):
        group = inputs[pair * 4 : pair * 4 + 4]
        for tile in range(2):
            slot = pair * 2 + tile
            ranks = [m[pl.ds(2 * CHANNELS * SLAB + tile * 8, 8), :] for m in group]
            parts = [[read_slab(m, (tile * CHANNELS + k) * SLAB) for k in range(CHANNELS)] for m in group]
            merged = merge_four(parts, ranks)
            for k in range(CHANNELS):
                write_slab(out, (slot * CHANNELS + k) * SLAB, merged[k])
            out[pl.ds(N * CHANNELS * SLAB + slot * 8, 8), :] = ranks[0]


def merge_x(messages):
    rows = N * CHANNELS * SLAB + N * 8
    vmem = pl.BlockSpec(memory_space=pltpu.VMEM)
    return pl.pallas_call(
        merge_x_kernel,
        in_specs=[vmem] * 8,
        out_specs=vmem,
        out_shape=jax.ShapeDtypeStruct((rows, LANES), jnp.float32),
        compiler_params=pltpu.CompilerParams(vmem_limit_bytes=VMEM),
        cost_estimate=pl.CostEstimate(flops=2**20, bytes_accessed=2**20, transcendentals=0),
        name="merge_x",
    )(*messages)


def merge_core_kernel(place, mine, other, out):
    core, z = place[2], place[3]
    for slot in range(N):
        where = N * CHANNELS * SLAB + slot * 8
        in_front = (mine[pl.ds(where, 8), :] < other[pl.ds(where, 8), :])[None]
        parts = [[read_slab(m, (slot * CHANNELS + k) * SLAB) for k in range(CHANNELS)] for m in (mine, other)]
        merged = merge_two(parts[0], parts[1], in_front)
        merged[3] = 1.0 - merged[3]
        tile = z ^ slot
        for k in range(CHANNELS):
            for block in range(BLOCKS):
                value = merged[k][block]
                value = jnp.where(core == 1, pltpu.roll(value, 4, 0), value)[:4]
                lanes = pl.ds(pl.multiple_of(tile * 512 + block * LANES, LANES), LANES)
                out[k, 0, :, lanes] = value


def merge_core(place, mine, other):
    vmem = pl.BlockSpec(memory_space=pltpu.VMEM)
    return pl.pallas_call(
        merge_core_kernel,
        in_specs=[pl.BlockSpec(memory_space=pltpu.SMEM), vmem, vmem],
        out_specs=vmem,
        out_shape=jax.ShapeDtypeStruct((CHANNELS, 1, 4, N * 512), jnp.float32),
        compiler_params=pltpu.CompilerParams(vmem_limit_bytes=VMEM),
        cost_estimate=pl.CostEstimate(flops=2**19, bytes_accessed=2**19, transcendentals=0),
        name="merge_core",
    )(place, mine, other)


def exchange(value, y=0, x=0, core=0, z=0):
    flip = ((y * N + x) * 2 + core) * N + z
    return lax.ppermute(value, ("depth", "tile"), [(i, i ^ flip) for i in range(N * N * 2 * N)])


def body(scalar_field, depth_rank, palette, extinction):
    depth = lax.axis_index("depth")
    place = jnp.stack([depth >> 3, (depth >> 1) & 3, depth & 1, lax.axis_index("tile")]).astype(jnp.int32)
    depth_total = scalar_field.shape[0] * lax.axis_size("depth")
    field = scalar_field.reshape(SAMPLES, 1, N, N, 2, 2, 8, 512)
    by_x = [None, None]
    for z_pair in (1, 0):
        received = {}
        for y_flips in ((2, 1), (3, 0)):
            sent = march(field, place, palette, extinction, depth_rank, y_flips, z_pair, depth_total)
            for j, flip in enumerate(y_flips):
                for tile in range(2):
                    z_flip = z_pair * 2 + tile
                    message = sent[j * 2 + tile]
                    received[tile, flip] = message if flip == z_flip == 0 else exchange(message, y=flip, z=z_flip)
        parts = merge_y(place, [received[tile, flip] for tile in range(2) for flip in range(N)])
        by_x[z_pair] = [parts[0]] + [exchange(parts[flip], x=flip) for flip in range(1, N)]
    mine = merge_x(by_x[0] + by_x[1])
    return merge_core(place, mine, exchange(mine, core=1))


def solution(mesh):
    in_specs = (P("depth", "tile", None, None), P("depth", "tile"), P(), P())
    out_specs = P(None, None, ("depth", "tile"), None)
    return jax.shard_map(body, mesh=mesh, in_specs=in_specs, out_specs=out_specs, check_vma=False)
```

time: 245 us -> 104 us (0.42)
  the two profiles are of different devices: /device:TPU:6 before, /device:TPU:25 now
where the time goes in v1:
time: 104 us
  starting transfers between devices  48.4 us (47%)
  waiting for transfers between devices  28.1 us (27%)
  Pallas kernels  25.1 us (24%)
  local copies, waits for them, and re-layouts  1.42 us (1%)
    ppermute x22, starting transfers between devices, exchange(): lax.ppermute(value, ('depth', 'tile'), [(i, i ^ flip) for i in range(N *...  48.4 us
    ppermute x22, waiting for transfers between devices, exchange(): lax.ppermute(value, ('depth', 'tile'), [(i, i ^ flip) for i in range(N *...  28.1 us
    pallas_call x4, Pallas kernels, march(): pl.pallas_call(functools.partial(march_kernel, count=count, depth_total=d...  22.3 us
  transfers between devices with their start and end apart: 22, of which 10 were waited for; matrix products, arithmetic and copies ran while one was open for 0% of the time, Pallas kernels for 18%

profile of v1, /device:TPU:25, one launch (start us, length us, event | category | flops | bytes accessed | tf_op | source)
XLA Modules:
  0.0 103.9 jit_solution(6561051748710116730)
XLA Ops:
  2.2 5.6 %march.7 = (f32[520,128]{1,0:T(8,128)S(1)}, f32[520,128]{1,0:T(8,128)S(1)}, f32[520,128]{1,0:T(8,128)S(1)}, f32[520,128]{1,0:T(8,128)S(1)}) custom-call(s32[4]{0:T(128)S(1)} %pad_add_fusion.place, f32[3,2]{1,0:T(4,128)S(1)} %copy.5.palette, f32[2]{0:T(128)S(1)} %copy-done, s32[1,1]{1,0:T(1,128)S(6)} %copy.9.rank, f32[16,1,4,4,2,2,8,512]{7,6,5,4,3,2,1,0:T(8,128)} %bitcast.5, ...), custom_call_target="tpu_custom_call" | custom-call | flops 20971520 | bytes 5242880 | tf_op jit(solution)/shard_map/march/pallas_call | solution.py:101
  7.7 3.9 %collective-permute-start.11 = (f32[520,128]{1,0:T(8,128)S(1)}, f32[520,128]{1,0:T(8,128)S(1)}, u32[]{:S(2)}, u32[]{:S(2)}) collective-permute-start(f32[520,128]{1,0:T(8,128)S(1)} %get-tuple-element.42), channel_id=1, source_target_pairs={{0,34},{1,35},{2,32},{3,33},{4,38},{5,39},{6,36},{7,37},{8,42},{9,... | collective-permute-start | bytes 798728 | tf_op jit(solution)/shard_map/ppermute | solution.py:212
  12.2 3.3 %collective-permute-start.15 = (f32[520,128]{1,0:T(8,128)S(1)}, f32[520,128]{1,0:T(8,128)S(1)}, u32[]{:S(2)}, u32[]{:S(2)}) collective-permute-start(f32[520,128]{1,0:T(8,128)S(1)} %get-tuple-element.46), channel_id=1, source_target_pairs={{0,35},{1,34},{2,33},{3,32},{4,39},{5,38},{6,37},{7,36},{8,43},{9,... | collective-permute-start | bytes 798728 | tf_op jit(solution)/shard_map/ppermute | solution.py:212
  15.5 1.9 %collective-permute-start.16 = (f32[520,128]{1,0:T(8,128)S(1)}, f32[520,128]{1,0:T(8,128)S(1)}, u32[]{:S(2)}, u32[]{:S(2)}) collective-permute-start(f32[520,128]{1,0:T(8,128)S(1)} %get-tuple-element.47), channel_id=1, source_target_pairs={{0,67},{1,66},{2,65},{3,64},{4,71},{5,70},{6,69},{7,68},{8,75},{9,... | collective-permute-start | bytes 798728 | tf_op jit(solution)/shard_map/ppermute | solution.py:212
  17.4 5.6 %march.6 = (f32[520,128]{1,0:T(8,128)S(1)}, f32[520,128]{1,0:T(8,128)S(1)}, f32[520,128]{1,0:T(8,128)S(1)}, f32[520,128]{1,0:T(8,128)S(1)}) custom-call(s32[4]{0:T(128)S(1)} %pad_add_fusion.place, f32[3,2]{1,0:T(4,128)S(1)} %copy.5.palette, f32[2]{0:T(128)S(1)} %copy-done, s32[1,1]{1,0:T(1,128)S(6)} %copy.9.rank, f32[16,1,4,4,2,2,8,512]{7,6,5,4,3,2,1,0:T(8,128)} %bitcast.7, ...), custom_call_target="tpu_custom_call" | custom-call | flops 20971520 | bytes 5242880 | tf_op jit(solution)/shard_map/march/pallas_call | solution.py:101
  23.0 2.5 %collective-permute-start.10 = (f32[520,128]{1,0:T(8,128)S(1)}, f32[520,128]{1,0:T(8,128)S(1)}, u32[]{:S(2)}, u32[]{:S(2)}) collective-permute-start(f32[520,128]{1,0:T(8,128)S(1)} %get-tuple-element.41), channel_id=1, source_target_pairs={{0,2},{1,3},{2,0},{3,1},{4,6},{5,7},{6,4},{7,5},{8,10},{9,11},{10,... | collective-permute-start | bytes 798728 | tf_op jit(solution)/shard_map/ppermute | solution.py:212
  26.5 5.6 %march.5 = (f32[520,128]{1,0:T(8,128)S(1)}, f32[520,128]{1,0:T(8,128)S(1)}, f32[520,128]{1,0:T(8,128)S(1)}, f32[520,128]{1,0:T(8,128)S(1)}) custom-call(s32[4]{0:T(128)S(1)} %pad_add_fusion.place, f32[3,2]{1,0:T(4,128)S(1)} %copy.5.palette, f32[2]{0:T(128)S(1)} %copy-done, s32[1,1]{1,0:T(1,128)S(6)} %copy.9.rank, f32[16,1,4,4,2,2,8,512]{7,6,5,4,3,2,1,0:T(8,128)} %bitcast.9, ...), custom_call_target="tpu_custom_call" | custom-call | flops 20971520 | bytes 5242880 | tf_op jit(solution)/shard_map/march/pallas_call | solution.py:101
  32.1 3.0 %collective-permute-start.14 = (f32[520,128]{1,0:T(8,128)S(1)}, f32[520,128]{1,0:T(8,128)S(1)}, u32[]{:S(2)}, u32[]{:S(2)}) collective-permute-start(f32[520,128]{1,0:T(8,128)S(1)} %get-tuple-element.45), channel_id=1, source_target_pairs={{0,3},{1,2},{2,1},{3,0},{4,7},{5,6},{6,5},{7,4},{8,11},{9,10},{10,... | collective-permute-start | bytes 798728 | tf_op jit(solution)/shard_map/ppermute | solution.py:212
  35.1 2.6 %collective-permute-start.17 = (f32[520,128]{1,0:T(8,128)S(1)}, f32[520,128]{1,0:T(8,128)S(1)}, u32[]{:S(2)}, u32[]{:S(2)}) collective-permute-start(f32[520,128]{1,0:T(8,128)S(1)} %get-tuple-element.48), channel_id=1, source_target_pairs={{0,99},{1,98},{2,97},{3,96},{4,103},{5,102},{6,101},{7,100},{8,107... | collective-permute-start | bytes 798728 | tf_op jit(solution)/shard_map/ppermute | solution.py:212
  37.7 5.4 %collective-permute-done.16.refs_6_ = f32[520,128]{1,0:T(8,128)S(1)} collective-permute-done((f32[520,128]{1,0:T(8,128)S(1)}, f32[520,128]{1,0:T(8,128)S(1)}, u32[]{:S(2)}, u32[]{:S(2)}) %collective-permute-start.16) | collective-permute-done | bytes 266272 | tf_op jit(solution)/shard_map/ppermute | solution.py:212
  43.0 2.3 %collective-permute-start = (f32[520,128]{1,0:T(8,128)S(1)}, f32[520,128]{1,0:T(8,128)S(1)}, u32[]{:S(2)}, u32[]{:S(2)}) collective-permute-start(f32[520,128]{1,0:T(8,128)S(1)} %get-tuple-element.30), channel_id=1, source_target_pairs={{0,32},{1,33},{2,34},{3,35},{4,36},{5,37},{6,38},{7,39},{8,40},{9,... | collective-permute-start | bytes 798728 | tf_op jit(solution)/shard_map/ppermute | solution.py:212
  45.8 7.5 %collective-permute-start.1 = (f32[520,128]{1,0:T(8,128)S(1)}, f32[520,128]{1,0:T(8,128)S(1)}, u32[]{:S(2)}, u32[]{:S(2)}) collective-permute-start(f32[520,128]{1,0:T(8,128)S(1)} %get-tuple-element.31), channel_id=1, source_target_pairs={{0,64},{1,65},{2,66},{3,67},{4,68},{5,69},{6,70},{7,71},{8,72},{9,... | collective-permute-start | bytes 798728 | tf_op jit(solution)/shard_map/ppermute | solution.py:212
  53.3 3.9 %collective-permute-start.4 = (f32[520,128]{1,0:T(8,128)S(1)}, f32[520,128]{1,0:T(8,128)S(1)}, u32[]{:S(2)}, u32[]{:S(2)}) collective-permute-start(f32[520,128]{1,0:T(8,128)S(1)} %get-tuple-element.34), channel_id=1, source_target_pairs={{0,33},{1,32},{2,35},{3,34},{4,37},{5,36},{6,39},{7,38},{8,41},{9,... | collective-permute-start | bytes 798728 | tf_op jit(solution)/shard_map/ppermute | solution.py:212
  57.1 5.6 %march.4 = (f32[520,128]{1,0:T(8,128)S(1)}, f32[520,128]{1,0:T(8,128)S(1)}, f32[520,128]{1,0:T(8,128)S(1)}, f32[520,128]{1,0:T(8,128)S(1)}) custom-call(s32[4]{0:T(128)S(1)} %pad_add_fusion.place, f32[3,2]{1,0:T(4,128)S(1)} %copy.5.palette, f32[2]{0:T(128)S(1)} %copy-done, s32[1,1]{1,0:T(1,128)S(6)} %copy.9.rank, f32[16,1,4,4,2,2,8,512]{7,6,5,4,3,2,1,0:T(8,128)} %bitcast.11, ...), custom_call_target="tpu_custom_call" | custom-call | flops 20971520 | bytes 5242880 | tf_op jit(solution)/shard_map/march/pallas_call | solution.py:101
  62.8 2.4 %collective-permute-start.2 = (f32[520,128]{1,0:T(8,128)S(1)}, f32[520,128]{1,0:T(8,128)S(1)}, u32[]{:S(2)}, u32[]{:S(2)}) collective-permute-start(f32[520,128]{1,0:T(8,128)S(1)} %get-tuple-element.32), channel_id=1, source_target_pairs={{0,96},{1,97},{2,98},{3,99},{4,100},{5,101},{6,102},{7,103},{8,104... | collective-permute-start | bytes 798728 | tf_op jit(solution)/shard_map/ppermute | solution.py:212
  67.8 1.4 %collective-permute-done.4.refs_5_ = f32[520,128]{1,0:T(8,128)S(1)} collective-permute-done((f32[520,128]{1,0:T(8,128)S(1)}, f32[520,128]{1,0:T(8,128)S(1)}, u32[]{:S(2)}, u32[]{:S(2)}) %collective-permute-start.4) | collective-permute-done | bytes 266272 | tf_op jit(solution)/shard_map/ppermute | solution.py:212
  70.5 3.3 %collective-permute-done.5.refs_6_ = f32[520,128]{1,0:T(8,128)S(1)} collective-permute-done((f32[520,128]{1,0:T(8,128)S(1)}, f32[520,128]{1,0:T(8,128)S(1)}, u32[]{:S(2)}, u32[]{:S(2)}) %collective-permute-start.5) | collective-permute-done | bytes 266272 | tf_op jit(solution)/shard_map/ppermute | solution.py:212
  73.8 2.7 %collective-permute-start.19 = (f32[272,128]{1,0:T(8,128)S(1)}, f32[272,128]{1,0:T(8,128)S(1)}, u32[]{:S(2)}, u32[]{:S(2)}) collective-permute-start(f32[272,128]{1,0:T(8,128)S(1)} %get-tuple-element.51), channel_id=1, source_target_pairs={{0,16},{1,17},{2,18},{3,19},{4,20},{5,21},{6,22},{7,23},{8,24},{9,... | collective-permute-start | bytes 417800 | tf_op jit(solution)/shard_map/ppermute | solution.py:212
  77.4 2.5 %collective-permute-start.20 = (f32[272,128]{1,0:T(8,128)S(1)}, f32[272,128]{1,0:T(8,128)S(1)}, u32[]{:S(2)}, u32[]{:S(2)}) collective-permute-start(f32[272,128]{1,0:T(8,128)S(1)} %get-tuple-element.52), channel_id=1, source_target_pairs={{0,24},{1,25},{2,26},{3,27},{4,28},{5,29},{6,30},{7,31},{8,16},{9,... | collective-permute-start | bytes 417800 | tf_op jit(solution)/shard_map/ppermute | solution.py:212
  79.9 6.9 %collective-permute-done.3.refs_4_ = f32[520,128]{1,0:T(8,128)S(1)} collective-permute-done((f32[520,128]{1,0:T(8,128)S(1)}, f32[520,128]{1,0:T(8,128)S(1)}, u32[]{:S(2)}, u32[]{:S(2)}) %collective-permute-start.3) | collective-permute-done | bytes 266272 | tf_op jit(solution)/shard_map/ppermute | solution.py:212
  87.6 1.3 %collective-permute-start.7 = (f32[272,128]{1,0:T(8,128)S(1)}, f32[272,128]{1,0:T(8,128)S(1)}, u32[]{:S(2)}, u32[]{:S(2)}) collective-permute-start(f32[272,128]{1,0:T(8,128)S(1)} %get-tuple-element.38), channel_id=1, source_target_pairs={{0,8},{1,9},{2,10},{3,11},{4,12},{5,13},{6,14},{7,15},{8,0},{9,1},... | collective-permute-start | bytes 417800 | tf_op jit(solution)/shard_map/ppermute | solution.py:212
  88.8 2.5 %collective-permute-start.8 = (f32[272,128]{1,0:T(8,128)S(1)}, f32[272,128]{1,0:T(8,128)S(1)}, u32[]{:S(2)}, u32[]{:S(2)}) collective-permute-start(f32[272,128]{1,0:T(8,128)S(1)} %get-tuple-element.39), channel_id=1, source_target_pairs={{0,16},{1,17},{2,18},{3,19},{4,20},{5,21},{6,22},{7,23},{8,24},{9,... | collective-permute-start | bytes 417800 | tf_op jit(solution)/shard_map/ppermute | solution.py:212
  92.4 5.2 %collective-permute-done.8.refs_2_ = f32[272,128]{1,0:T(8,128)S(1)} collective-permute-done((f32[272,128]{1,0:T(8,128)S(1)}, f32[272,128]{1,0:T(8,128)S(1)}, u32[]{:S(2)}, u32[]{:S(2)}) %collective-permute-start.8) | collective-permute-done | bytes 139296 | tf_op jit(solution)/shard_map/ppermute | solution.py:212
  97.6 2.5 %collective-permute-done.9.refs_3_ = f32[272,128]{1,0:T(8,128)S(1)} collective-permute-done((f32[272,128]{1,0:T(8,128)S(1)}, f32[272,128]{1,0:T(8,128)S(1)}, u32[]{:S(2)}, u32[]{:S(2)}) %collective-permute-start.9) | collective-permute-done | bytes 139296 | tf_op jit(solution)/shard_map/ppermute | solution.py:212
  (32 shorter events, 14.0 us)
Async XLA Ops:
  1.5 0.7 copy-start
  7.7 17.7 %collective-permute-start.11 = (f32[520,128]{1,0:T(8,128)S(1)}, f32[520,128]{1,0:T(8,128)S(1)}, u32[]{:S(2)}, u32[]{:S(2)}) collective-permute-start(f32[520,128]{1,0:T(8,128)S(1)} %get-tuple-element.42), channel_id=1, source_target_pairs={{0,34},{1,35},{2,32},{3,33},{4,38},{5,39},{6,36},{7,37},{8,42},{9,... | collective-permute-start | bytes 798728 | tf_op jit(solution)/shard_map/ppermute | solution.py:212
  11.6 20.5 %collective-permute-start.12 = (f32[520,128]{1,0:T(8,128)S(1)}, f32[520,128]{1,0:T(8,128)S(1)}, u32[]{:S(2)}, u32[]{:S(2)}) collective-permute-start(f32[520,128]{1,0:T(8,128)S(1)} %get-tuple-element.43), channel_id=1, source_target_pairs={{0,66},{1,67},{2,64},{3,65},{4,70},{5,71},{6,68},{7,69},{8,74},{9,... | collective-permute-start | bytes 798728 | tf_op jit(solution)/shard_map/ppermute | solution.py:212
  12.2 22.9 %collective-permute-start.15 = (f32[520,128]{1,0:T(8,128)S(1)}, f32[520,128]{1,0:T(8,128)S(1)}, u32[]{:S(2)}, u32[]{:S(2)}) collective-permute-start(f32[520,128]{1,0:T(8,128)S(1)} %get-tuple-element.46), channel_id=1, source_target_pairs={{0,35},{1,34},{2,33},{3,32},{4,39},{5,38},{6,37},{7,36},{8,43},{9,... | collective-permute-start | bytes 798728 | tf_op jit(solution)/shard_map/ppermute | solution.py:212
  15.5 27.5 %collective-permute-start.16 = (f32[520,128]{1,0:T(8,128)S(1)}, f32[520,128]{1,0:T(8,128)S(1)}, u32[]{:S(2)}, u32[]{:S(2)}) collective-permute-start(f32[520,128]{1,0:T(8,128)S(1)} %get-tuple-element.47), channel_id=1, source_target_pairs={{0,67},{1,66},{2,65},{3,64},{4,71},{5,70},{6,69},{7,68},{8,75},{9,... | collective-permute-start | bytes 798728 | tf_op jit(solution)/shard_map/ppermute | solution.py:212
  23.0 22.8 %collective-permute-start.10 = (f32[520,128]{1,0:T(8,128)S(1)}, f32[520,128]{1,0:T(8,128)S(1)}, u32[]{:S(2)}, u32[]{:S(2)}) collective-permute-start(f32[520,128]{1,0:T(8,128)S(1)} %get-tuple-element.41), channel_id=1, source_target_pairs={{0,2},{1,3},{2,0},{3,1},{4,6},{5,7},{6,4},{7,5},{8,10},{9,11},{10,... | collective-permute-start | bytes 798728 | tf_op jit(solution)/shard_map/ppermute | solution.py:212
  25.4 27.8 %collective-permute-start.13 = (f32[520,128]{1,0:T(8,128)S(1)}, f32[520,128]{1,0:T(8,128)S(1)}, u32[]{:S(2)}, u32[]{:S(2)}) collective-permute-start(f32[520,128]{1,0:T(8,128)S(1)} %get-tuple-element.44), channel_id=1, source_target_pairs={{0,98},{1,99},{2,96},{3,97},{4,102},{5,103},{6,100},{7,101},{8,106... | collective-permute-start | bytes 798728 | tf_op jit(solution)/shard_map/ppermute | solution.py:212
  32.1 30.6 %collective-permute-start.14 = (f32[520,128]{1,0:T(8,128)S(1)}, f32[520,128]{1,0:T(8,128)S(1)}, u32[]{:S(2)}, u32[]{:S(2)}) collective-permute-start(f32[520,128]{1,0:T(8,128)S(1)} %get-tuple-element.45), channel_id=1, source_target_pairs={{0,3},{1,2},{2,1},{3,0},{4,7},{5,6},{6,5},{7,4},{8,11},{9,10},{10,... | collective-permute-start | bytes 798728 | tf_op jit(solution)/shard_map/ppermute | solution.py:212
  35.1 27.7 %collective-permute-start.17 = (f32[520,128]{1,0:T(8,128)S(1)}, f32[520,128]{1,0:T(8,128)S(1)}, u32[]{:S(2)}, u32[]{:S(2)}) collective-permute-start(f32[520,128]{1,0:T(8,128)S(1)} %get-tuple-element.48), channel_id=1, source_target_pairs={{0,99},{1,98},{2,97},{3,96},{4,103},{5,102},{6,101},{7,100},{8,107... | collective-permute-start | bytes 798728 | tf_op jit(solution)/shard_map/ppermute | solution.py:212
  43.0 22.2 %collective-permute-start = (f32[520,128]{1,0:T(8,128)S(1)}, f32[520,128]{1,0:T(8,128)S(1)}, u32[]{:S(2)}, u32[]{:S(2)}) collective-permute-start(f32[520,128]{1,0:T(8,128)S(1)} %get-tuple-element.30), channel_id=1, source_target_pairs={{0,32},{1,33},{2,34},{3,35},{4,36},{5,37},{6,38},{7,39},{8,40},{9,... | collective-permute-start | bytes 798728 | tf_op jit(solution)/shard_map/ppermute | solution.py:212
  45.8 20.4 %collective-permute-start.1 = (f32[520,128]{1,0:T(8,128)S(1)}, f32[520,128]{1,0:T(8,128)S(1)}, u32[]{:S(2)}, u32[]{:S(2)}) collective-permute-start(f32[520,128]{1,0:T(8,128)S(1)} %get-tuple-element.31), channel_id=1, source_target_pairs={{0,64},{1,65},{2,66},{3,67},{4,68},{5,69},{6,70},{7,71},{8,72},{9,... | collective-permute-start | bytes 798728 | tf_op jit(solution)/shard_map/ppermute | solution.py:212
  53.3 16.0 %collective-permute-start.4 = (f32[520,128]{1,0:T(8,128)S(1)}, f32[520,128]{1,0:T(8,128)S(1)}, u32[]{:S(2)}, u32[]{:S(2)}) collective-permute-start(f32[520,128]{1,0:T(8,128)S(1)} %get-tuple-element.34), channel_id=1, source_target_pairs={{0,33},{1,32},{2,35},{3,34},{4,37},{5,36},{6,39},{7,38},{8,41},{9,... | collective-permute-start | bytes 798728 | tf_op jit(solution)/shard_map/ppermute | solution.py:212
  62.7 11.1 %collective-permute-start.5 = (f32[520,128]{1,0:T(8,128)S(1)}, f32[520,128]{1,0:T(8,128)S(1)}, u32[]{:S(2)}, u32[]{:S(2)}) collective-permute-start(f32[520,128]{1,0:T(8,128)S(1)} %get-tuple-element.35), channel_id=1, source_target_pairs={{0,65},{1,64},{2,67},{3,66},{4,69},{5,68},{6,71},{7,70},{8,73},{9,... | collective-permute-start | bytes 798728 | tf_op jit(solution)/shard_map/ppermute | solution.py:212
  62.8 14.6 %collective-permute-start.2 = (f32[520,128]{1,0:T(8,128)S(1)}, f32[520,128]{1,0:T(8,128)S(1)}, u32[]{:S(2)}, u32[]{:S(2)}) collective-permute-start(f32[520,128]{1,0:T(8,128)S(1)} %get-tuple-element.32), channel_id=1, source_target_pairs={{0,96},{1,97},{2,98},{3,99},{4,100},{5,101},{6,102},{7,103},{8,104... | collective-permute-start | bytes 798728 | tf_op jit(solution)/shard_map/ppermute | solution.py:212
  65.2 21.6 %collective-permute-start.3 = (f32[520,128]{1,0:T(8,128)S(1)}, f32[520,128]{1,0:T(8,128)S(1)}, u32[]{:S(2)}, u32[]{:S(2)}) collective-permute-start(f32[520,128]{1,0:T(8,128)S(1)} %get-tuple-element.33), channel_id=1, source_target_pairs={{0,1},{1,0},{2,3},{3,2},{4,5},{5,4},{6,7},{7,6},{8,9},{9,8},{10,11... | collective-permute-start | bytes 798728 | tf_op jit(solution)/shard_map/ppermute | solution.py:212
  66.2 20.7 %collective-permute-start.6 = (f32[520,128]{1,0:T(8,128)S(1)}, f32[520,128]{1,0:T(8,128)S(1)}, u32[]{:S(2)}, u32[]{:S(2)}) collective-permute-start(f32[520,128]{1,0:T(8,128)S(1)} %get-tuple-element.36), channel_id=1, source_target_pairs={{0,97},{1,96},{2,99},{3,98},{4,101},{5,100},{6,103},{7,102},{8,105... | collective-permute-start | bytes 798728 | tf_op jit(solution)/shard_map/ppermute | solution.py:212
  69.3 22.0 %collective-permute-start.18 = (f32[272,128]{1,0:T(8,128)S(1)}, f32[272,128]{1,0:T(8,128)S(1)}, u32[]{:S(2)}, u32[]{:S(2)}) collective-permute-start(f32[272,128]{1,0:T(8,128)S(1)} %get-tuple-element.50), channel_id=1, source_target_pairs={{0,8},{1,9},{2,10},{3,11},{4,12},{5,13},{6,14},{7,15},{8,0},{9,1},... | collective-permute-start | bytes 417800 | tf_op jit(solution)/shard_map/ppermute | solution.py:212
  73.8 17.7 %collective-permute-start.19 = (f32[272,128]{1,0:T(8,128)S(1)}, f32[272,128]{1,0:T(8,128)S(1)}, u32[]{:S(2)}, u32[]{:S(2)}) collective-permute-start(f32[272,128]{1,0:T(8,128)S(1)} %get-tuple-element.51), channel_id=1, source_target_pairs={{0,16},{1,17},{2,18},{3,19},{4,20},{5,21},{6,22},{7,23},{8,24},{9,... | collective-permute-start | bytes 417800 | tf_op jit(solution)/shard_map/ppermute | solution.py:212
  77.4 14.1 %collective-permute-start.20 = (f32[272,128]{1,0:T(8,128)S(1)}, f32[272,128]{1,0:T(8,128)S(1)}, u32[]{:S(2)}, u32[]{:S(2)}) collective-permute-start(f32[272,128]{1,0:T(8,128)S(1)} %get-tuple-element.52), channel_id=1, source_target_pairs={{0,24},{1,25},{2,26},{3,27},{4,28},{5,29},{6,30},{7,31},{8,16},{9,... | collective-permute-start | bytes 417800 | tf_op jit(solution)/shard_map/ppermute | solution.py:212
  87.6 4.8 %collective-permute-start.7 = (f32[272,128]{1,0:T(8,128)S(1)}, f32[272,128]{1,0:T(8,128)S(1)}, u32[]{:S(2)}, u32[]{:S(2)}) collective-permute-start(f32[272,128]{1,0:T(8,128)S(1)} %get-tuple-element.38), channel_id=1, source_target_pairs={{0,8},{1,9},{2,10},{3,11},{4,12},{5,13},{6,14},{7,15},{8,0},{9,1},... | collective-permute-start | bytes 417800 | tf_op jit(solution)/shard_map/ppermute | solution.py:212
  88.8 8.8 %collective-permute-start.8 = (f32[272,128]{1,0:T(8,128)S(1)}, f32[272,128]{1,0:T(8,128)S(1)}, u32[]{:S(2)}, u32[]{:S(2)}) collective-permute-start(f32[272,128]{1,0:T(8,128)S(1)} %get-tuple-element.39), channel_id=1, source_target_pairs={{0,16},{1,17},{2,18},{3,19},{4,20},{5,21},{6,22},{7,23},{8,24},{9,... | collective-permute-start | bytes 417800 | tf_op jit(solution)/shard_map/ppermute | solution.py:212
  91.3 8.8 %collective-permute-start.9 = (f32[272,128]{1,0:T(8,128)S(1)}, f32[272,128]{1,0:T(8,128)S(1)}, u32[]{:S(2)}, u32[]{:S(2)}) collective-permute-start(f32[272,128]{1,0:T(8,128)S(1)} %get-tuple-element.40), channel_id=1, source_target_pairs={{0,24},{1,25},{2,26},{3,27},{4,28},{5,29},{6,30},{7,31},{8,16},{9,... | collective-permute-start | bytes 417800 | tf_op jit(solution)/shard_map/ppermute | solution.py:212
  100.2 2.5 %collective-permute-start.21 = (f32[544,128]{1,0:T(8,128)S(1)}, f32[544,128]{1,0:T(8,128)S(1)}, u32[]{:S(2)}, u32[]{:S(2)}) collective-permute-start(f32[544,128]{1,0:T(8,128)S(1)} %merge_x.1.mine), channel_id=1, source_target_pairs={{0,4},{1,5},{2,6},{3,7},{4,0},{5,1},{6,2},{7,3},{8,12},{9,13},{10,... | collective-permute-start | bytes 835592 | tf_op jit(solution)/shard_map/ppermute | solution.py:212

commit v2 on v0

v2 whole, which is shorter than its diff:
```python
import functools
import math

import jax
import jax.numpy as jnp
from jax import lax
from jax.experimental import pallas as pl
from jax.experimental.pallas import tpu as pltpu
from jax.sharding import PartitionSpec as P

N = 4
SAMPLES = 16
LANES = 128
CHANNELS = 4
X_ROWS = 32
CORE_ROWS = 16
CHUNKS = ((0, 1), (2, 2), (1, 1))
GROUPS = ((0, 1), (2,))
VMEM = 40 * 2**20


def merge_two(a, b, a_in_front):
    one = jnp.float32(1.0)
    weight_a = jnp.where(a_in_front, one, b[3])
    weight_b = jnp.where(a_in_front, a[3], one)
    return [a[k] * weight_a + b[k] * weight_b for k in range(3)] + [a[3] * b[3]]


def merge_four(parts, ranks):
    even = merge_two(parts[0], parts[2], (ranks[0] < ranks[2])[None])
    odd = merge_two(parts[1], parts[3], (ranks[1] < ranks[3])[None])
    return merge_two(even, odd, (ranks[0] < ranks[1])[None])


def read(ref, start, rows):
    return ref[pl.ds(pl.multiple_of(start, 8), rows), :].reshape(rows // 8, 8, LANES)


def write(ref, start, value):
    ref[pl.ds(start, value.shape[0] * 8), :] = value.reshape(value.shape[0] * 8, LANES)


def vmem_specs(count):
    return [pl.BlockSpec(memory_space=pltpu.VMEM)] * count


def smem_specs(count):
    return [pl.BlockSpec(memory_space=pltpu.SMEM)] * count


def rows_of(*counts):
    return [jax.ShapeDtypeStruct((rows, LANES), jnp.float32) for rows in counts]


def cost(microseconds):
    return pl.CostEstimate(flops=int(microseconds * 1e9), bytes_accessed=1, transcendentals=0)


def march_kernel(place, slopes, extinction, rank, *refs, blocks, depth_total):
    fields, messages = refs[:N], refs[-N:]
    x = pl.program_id(0)
    scale = -1.0 / (depth_total * math.log(2.0))
    quadratic = extinction[0] * scale
    constant = extinction[1] * scale
    slope = [slopes[0, k] * 0.5 for k in range(3)]
    offset = [slopes[1, k] * 0.5 for k in range(3)]

    for field, message in zip(fields, messages):
        for block in range(blocks):
            shape = (X_ROWS, LANES)
            squares = jnp.zeros(shape, jnp.float32)
            through = jnp.ones(shape, jnp.float32)
            totals = [jnp.zeros(shape, jnp.float32) for _ in range(3)]
            for i in range(SAMPLES):
                s = field[i, :, block * LANES : (block + 1) * LANES]
                squares = squares + s * s
                after = jnp.exp2(squares * quadratic + constant * float(i + 1))
                weight = through - after
                through = after
                for k in range(3):
                    totals[k] = totals[k] + weight * jnp.tanh(s * slope[k] + offset[k])
            opacity = 1.0 - through
            channels = [0.5 * (opacity + totals[k]) for k in range(3)] + [through]
            for k in range(CHANNELS):
                row = ((k * N + x) * blocks + block) * X_ROWS
                message[pl.ds(pl.multiple_of(row, X_ROWS), X_ROWS), :] = channels[k]

    @pl.when(x == 0)
    def _():
        own = jnp.full((8, LANES), rank[0, 0].astype(jnp.float32))
        for message in messages:
            message[pl.ds(CHANNELS * N * blocks * X_ROWS, 8), :] = own


def march(field, place, palette, extinction, rank, first, blocks, depth_total, after=()):
    rows = CHANNELS * N * blocks * X_ROWS + 8

    def field_index(flip):
        return lambda x, where: (0, 0, (where[0] ^ flip) * N + x, first // blocks)

    return pl.pallas_call(
        functools.partial(march_kernel, blocks=blocks, depth_total=depth_total),
        grid_spec=pltpu.PrefetchScalarGridSpec(
            num_scalar_prefetch=1,
            grid=(N,),
            in_specs=smem_specs(3)
            + [pl.BlockSpec((SAMPLES, None, X_ROWS, blocks * LANES), field_index(flip)) for flip in range(N)]
            + [pl.BlockSpec(memory_space=pl.ANY)] * len(after),
            out_specs=[pl.BlockSpec((rows, LANES), lambda x, where: (0, 0))] * N,
        ),
        out_shape=rows_of(*[rows] * N),
        compiler_params=pltpu.CompilerParams(vmem_limit_bytes=VMEM),
        cost_estimate=cost(1.5 + 4.1 * blocks),
        name="march",
    )(place, palette.T, extinction, rank, *([field] * N), *after)


def merge_y_kernel(place, *refs, sizes):
    inputs, outputs = refs[:-N], refs[-N:]
    total = sum(sizes) * X_ROWS
    base = 0
    for c, blocks in enumerate(sizes):
        group = inputs[c * N : c * N + N]
        slab = blocks * X_ROWS
        ranks = [m[pl.ds(CHANNELS * N * slab, 8), :] for m in group]
        for flip in range(N):
            x = place[1] ^ flip
            parts = [[read(m, (k * N + x) * slab, slab) for k in range(CHANNELS)] for m in group]
            merged = merge_four(parts, ranks)
            for k in range(CHANNELS):
                write(outputs[flip], k * total + base, merged[k])
            outputs[flip][pl.ds(CHANNELS * total, 8), :] = ranks[0]
        base += slab


def merge_y(place, messages, sizes):
    return pl.pallas_call(
        functools.partial(merge_y_kernel, sizes=sizes),
        in_specs=smem_specs(1) + vmem_specs(len(messages)),
        out_specs=vmem_specs(N),
        out_shape=rows_of(*[CHANNELS * sum(sizes) * X_ROWS + 8] * N),
        compiler_params=pltpu.CompilerParams(vmem_limit_bytes=VMEM),
        cost_estimate=cost(0.3 * sum(sizes)),
        name="merge_y",
    )(place, *messages)


def merge_x_kernel(place, *refs):
    inputs, outputs = refs[:-2], refs[-2:]
    for g, chunks in enumerate(GROUPS):
        columns = [first + block for first, count in (CHUNKS[c] for c in chunks) for block in range(count)]
        group = inputs[g * N : g * N + N]
        blocks = len(columns)
        ranks = [m[pl.ds(CHANNELS * blocks * X_ROWS, 8), :] for m in group]
        for flip in range(2):
            core = place[2] ^ flip
            for block, column in enumerate(columns):
                parts = [
                    [read(m, (k * blocks + block) * X_ROWS + core * CORE_ROWS, CORE_ROWS) for k in range(CHANNELS)]
                    for m in group
                ]
                merged = merge_four(parts, ranks)
                for k in range(CHANNELS):
                    write(outputs[flip], (k * N + column) * CORE_ROWS, merged[k])
            outputs[flip][pl.ds(CHANNELS * N * CORE_ROWS, 8), :] = ranks[0]


def merge_x(place, messages):
    return pl.pallas_call(
        merge_x_kernel,
        in_specs=smem_specs(1) + vmem_specs(len(messages)),
        out_specs=vmem_specs(2),
        out_shape=rows_of(*[CHANNELS * N * CORE_ROWS + 8] * 2),
        compiler_params=pltpu.CompilerParams(vmem_limit_bytes=VMEM),
        cost_estimate=cost(0.5),
        name="merge_x",
    )(place, *messages)


def merge_core_kernel(place, mine, other, *targets):
    where = CHANNELS * N * CORE_ROWS
    in_front = (mine[pl.ds(where, 8), :] < other[pl.ds(where, 8), :])[None]
    for block in range(N):
        parts = [[read(m, (k * N + block) * CORE_ROWS, CORE_ROWS) for k in range(CHANNELS)] for m in (mine, other)]
        merged = merge_two(parts[0], parts[1], in_front)
        merged[3] = 1.0 - merged[3]
        for k in range(CHANNELS):
            for flip, target in enumerate(targets):
                z = place[3] ^ flip
                value = jnp.where(z >= 2, merged[k][1], merged[k][0])
                value = jnp.where((z & 1) == 1, pltpu.roll(value, 4, 0), value)
                target[pl.ds((k * N + block) * 4, 4), :] = value[:4]


def merge_core(place, mine, other):
    rows = CHANNELS * N * 4
    return pl.pallas_call(
        merge_core_kernel,
        in_specs=smem_specs(1) + vmem_specs(2),
        out_specs=vmem_specs(N),
        out_shape=rows_of(*[rows] * N),
        compiler_params=pltpu.CompilerParams(vmem_limit_bytes=VMEM),
        cost_estimate=cost(0.5),
        name="merge_core",
    )(place, mine, other)


def assemble_kernel(place, *refs):
    sources, out = refs[:N], refs[N]
    for flip, source in enumerate(sources):
        tile = place[3] ^ flip
        for k in range(CHANNELS):
            for block in range(N):
                lanes = pl.ds(pl.multiple_of((tile * N + block) * LANES, LANES), LANES)
                out[k, 0, :, lanes] = source[pl.ds((k * N + block) * 4, 4), :]


def assemble(place, pieces):
    return pl.pallas_call(
        assemble_kernel,
        in_specs=smem_specs(1) + vmem_specs(4),
        out_specs=pl.BlockSpec(memory_space=pltpu.VMEM),
        out_shape=jax.ShapeDtypeStruct((CHANNELS, 1, 4, N * N * LANES), jnp.float32),
        compiler_params=pltpu.CompilerParams(vmem_limit_bytes=VMEM),
        cost_estimate=cost(1.0),
        name="assemble",
    )(place, *pieces)


def exchange(value, y=0, x=0, core=0, z=0):
    flip = ((y * N + x) * 2 + core) * N + z
    return lax.ppermute(value, ("depth", "tile"), [(i, i ^ flip) for i in range(N * N * 2 * N)])


def all_flips(pieces, axis):
    moved = {flip: exchange(pieces[flip], **{axis: flip}) for flip in (2, 1, 3)}
    return [pieces[0], moved[1], moved[2], moved[3]]


def body(scalar_field, depth_rank, palette, extinction):
    depth = lax.axis_index("depth")
    place = jnp.stack([depth >> 3, (depth >> 1) & 3, depth & 1, lax.axis_index("tile")]).astype(jnp.int32)
    depth_total = scalar_field.shape[0] * lax.axis_size("depth")
    received, after = [], ()
    for c, (first, blocks) in enumerate(CHUNKS):
        sent = march(scalar_field, place, palette, extinction, depth_rank, first, blocks, depth_total, after)
        received.append(all_flips(sent, "y"))
        after = (sent[0],) if c == 0 else received[c - 1][1:]
    by_x = []
    for chunks in GROUPS:
        merged = merge_y(place, [m for c in chunks for m in received[c]], [CHUNKS[c][1] for c in chunks])
        by_x += all_flips(merged, "x")
    mine, send = merge_x(place, by_x)
    pieces = merge_core(place, mine, exchange(send, core=1))
    return assemble(place, all_flips(pieces, "z"))


def solution(mesh):
    in_specs = (P("depth", "tile", None, None), P("depth", "tile"), P(), P())
    out_specs = P(None, None, ("depth", "tile"), None)
    return jax.shard_map(body, mesh=mesh, in_specs=in_specs, out_specs=out_specs, check_vma=False)
```

time: 245 us -> 87 us (0.36)
  other arithmetic: 105 us -> 0.08 us
  waiting for transfers between devices: 82.1 us -> 32.5 us
  local copies, waits for them, and re-layouts: 29.2 us -> 1.34 us
  Pallas kernels: 0 us -> 23.1 us
  starting transfers between devices: 11.9 us -> 28.8 us
  blocking collectives: 11.1 us -> 0 us
  between operations: 4.34 us -> 0.73 us
    ppermute x10 -> x19, waiting for transfers between devices: 82.1 us -> 32.5 us  [exchange(): lax.ppermute(value, ('depth', 'tile'), [(i, i ^ flip) for i in range(N *...]
    add x20 -> x0, other arithmetic: 46.8 us -> none  [composite_over(): return nearer + (1.0 - nearer[3:4]) * farther]
    mul x21 -> x0, other arithmetic: 39.3 us -> none  [the longest x2 28.1 us: march_brick(): sample = jnp.concatenate([opacity[None] * colour, opacity[None]], axis=0)]
    pallas_call x0 -> x8, Pallas kernels: none -> 23.1 us  [the longest x3 19.2 us: march(): pl.pallas_call(functools.partial(march_kernel, blocks=blocks, depth_total...]
    ppermute x10 -> x19, starting transfers between devices: 11.9 us -> 28.8 us  [exchange(): lax.ppermute(value, ('depth', 'tile'), [(i, i ^ flip) for i in range(N *...]
    sub x2 -> x0, other arithmetic: 16.1 us -> none  [march_brick(): opacity = 1.0 - jnp.exp(-rate / depth_total)]
    squeeze x1 -> x0, local copies, waits for them, and re-layouts: 13.3 us -> none  [march_brick(): sample_slice = samples_in[position]]
    all_to_all x1 -> x0, blocking collectives: 11.1 us -> none  [body(): lax.all_to_all(outgoing, 'tile', split_axis=1, concat_axis=1, tiled=True)]
  transfers between devices with their start and end apart: 10 -> 19, of which waited for: 5 -> 11; matrix products, arithmetic and copies ran while one was open for 0% -> 0% of each run, Pallas kernels for 0% -> 18%
where the time goes in v2:
time: 87 us; the launch traced here: 86.6 us
  waiting for transfers between devices  32.5 us (37%)
  starting transfers between devices  28.8 us (33%)
  Pallas kernels  23.1 us (27%)
  local copies, waits for them, and re-layouts  1.34 us (2%)
    ppermute x19, waiting for transfers between devices, exchange(): lax.ppermute(value, ('depth', 'tile'), [(i, i ^ flip) for i in range(N *...  32.5 us
    ppermute x19, starting transfers between devices, exchange(): lax.ppermute(value, ('depth', 'tile'), [(i, i ^ flip) for i in range(N *...  28.8 us
    pallas_call x3, Pallas kernels, march(): pl.pallas_call(functools.partial(march_kernel, blocks=blocks, depth_total...  19.2 us
  transfers between devices with their start and end apart: 19, of which 11 were waited for; matrix products, arithmetic and copies ran while one was open for 0% of the time, Pallas kernels for 18%

profile of v2, /device:TPU:6, one launch (start us, length us, event | category | flops | bytes accessed | tf_op | source)
XLA Modules:
  0.0 86.6 jit_solution(9007786695573601546)
XLA Ops:
  2.1 5.5 %march.3 = (f32[520,128]{1,0:T(8,128)S(1)}, f32[520,128]{1,0:T(8,128)S(1)}, f32[520,128]{1,0:T(8,128)S(1)}, f32[520,128]{1,0:T(8,128)S(1)}) custom-call(s32[4]{0:T(128)S(1)} %pad_add_fusion.place, f32[2,3]{1,0:T(2,128)S(1)} %bitcast.5, f32[2]{0:T(128)S(1)} %copy-done.1, s32[1,1]{1,0:T(1,128)S(6)} %copy.5.rank, f32[16,1,512,512]{3,2,1,0:T(8,128)} %refs_3_.5, ...), custom_call_target="tpu_custom_call" | custom-call | flops 5600000000 | bytes 1 | tf_op jit(solution)/shard_map/march/pallas_call | solution.py:101
  7.5 1.7 %collective-permute-start = (f32[520,128]{1,0:T(8,128)S(1)}, f32[520,128]{1,0:T(8,128)S(1)}, u32[]{:S(2)}, u32[]{:S(2)}) collective-permute-start(f32[520,128]{1,0:T(8,128)S(1)} %get-tuple-element.32), channel_id=1, source_target_pairs={{0,32},{1,33},{2,34},{3,35},{4,36},{5,37},{6,38},{7,39},{8,40},{9,... | collective-permute-start | bytes 798728 | tf_op jit(solution)/shard_map/ppermute | solution.py:232
  9.2 2.9 %collective-permute-start.1 = (f32[520,128]{1,0:T(8,128)S(1)}, f32[520,128]{1,0:T(8,128)S(1)}, u32[]{:S(2)}, u32[]{:S(2)}) collective-permute-start(f32[520,128]{1,0:T(8,128)S(1)} %get-tuple-element.33), channel_id=1, source_target_pairs={{0,64},{1,65},{2,66},{3,67},{4,68},{5,69},{6,70},{7,71},{8,72},{9,... | collective-permute-start | bytes 798728 | tf_op jit(solution)/shard_map/ppermute | solution.py:232
  12.3 8.2 %march.4 = (f32[1032,128]{1,0:T(8,128)S(1)}, f32[1032,128]{1,0:T(8,128)S(1)}, f32[1032,128]{1,0:T(8,128)S(1)}, f32[1032,128]{1,0:T(8,128)S(1)}) custom-call(s32[4]{0:T(128)S(1)} %pad_add_fusion.place, f32[2,3]{1,0:T(2,128)S(1)} %bitcast.6, f32[2]{0:T(128)S(1)} %copy-done.1, s32[1,1]{1,0:T(1,128)S(6)} %copy.5.rank, f32[16,1,512,512]{3,2,1,0:T(8,128)} %refs_3_.5, ...), custom_call_target="tpu_custom_call" | custom-call | flops 9699999744 | bytes 1 | tf_op jit(solution)/shard_map/march/pallas_call | solution.py:101
  21.0 4.1 %collective-permute-start.4 = (f32[1032,128]{1,0:T(8,128)S(1)}, f32[1032,128]{1,0:T(8,128)S(1)}, u32[]{:S(2)}, u32[]{:S(2)}) collective-permute-start(f32[1032,128]{1,0:T(8,128)S(1)} %get-tuple-element.37), channel_id=1, source_target_pairs={{0,64},{1,65},{2,66},{3,67},{4,68},{5,69},{6,70},{7,71},{8,72},{9,... | collective-permute-start | bytes 1585160 | tf_op jit(solution)/shard_map/ppermute | solution.py:232
  25.3 1.2 %collective-permute-done.2.refs_3_.refs_6_ = f32[520,128]{1,0:T(8,128)S(1)} collective-permute-done((f32[520,128]{1,0:T(8,128)S(1)}, f32[520,128]{1,0:T(8,128)S(1)}, u32[]{:S(2)}, u32[]{:S(2)}) %collective-permute-start.2) | collective-permute-done | bytes 266272 | tf_op jit(solution)/shard_map/ppermute | solution.py:232
  26.6 5.5 %march.5 = (f32[520,128]{1,0:T(8,128)S(1)}, f32[520,128]{1,0:T(8,128)S(1)}, f32[520,128]{1,0:T(8,128)S(1)}, f32[520,128]{1,0:T(8,128)S(1)}) custom-call(s32[4]{0:T(128)S(1)} %pad_add_fusion.place, f32[2,3]{1,0:T(2,128)S(1)} %bitcast.7, f32[2]{0:T(128)S(1)} %copy-done.1, s32[1,1]{1,0:T(1,128)S(6)} %copy.5.rank, f32[16,1,512,512]{3,2,1,0:T(8,128)} %refs_3_.5, ...), custom_call_target="tpu_custom_call" | custom-call | flops 5600000000 | bytes 1 | tf_op jit(solution)/shard_map/march/pallas_call | solution.py:101
  32.2 3.2 %collective-permute-start.10 = (f32[520,128]{1,0:T(8,128)S(1)}, f32[520,128]{1,0:T(8,128)S(1)}, u32[]{:S(2)}, u32[]{:S(2)}) collective-permute-start(f32[520,128]{1,0:T(8,128)S(1)} %get-tuple-element.45), channel_id=1, source_target_pairs={{0,64},{1,65},{2,66},{3,67},{4,68},{5,69},{6,70},{7,71},{8,72},{9,... | collective-permute-start | bytes 798728 | tf_op jit(solution)/shard_map/ppermute | solution.py:232
  35.6 3.0 %collective-permute-start.11 = (f32[520,128]{1,0:T(8,128)S(1)}, f32[520,128]{1,0:T(8,128)S(1)}, u32[]{:S(2)}, u32[]{:S(2)}) collective-permute-start(f32[520,128]{1,0:T(8,128)S(1)} %get-tuple-element.46), channel_id=1, source_target_pairs={{0,96},{1,97},{2,98},{3,99},{4,100},{5,101},{6,102},{7,103},{8,104... | collective-permute-start | bytes 798728 | tf_op jit(solution)/shard_map/ppermute | solution.py:232
  38.6 10.8 %collective-permute-done.4.refs_6_ = f32[1032,128]{1,0:T(8,128)S(1)} collective-permute-done((f32[1032,128]{1,0:T(8,128)S(1)}, f32[1032,128]{1,0:T(8,128)S(1)}, u32[]{:S(2)}, u32[]{:S(2)}) %collective-permute-start.4) | collective-permute-done | bytes 528416 | tf_op jit(solution)/shard_map/ppermute | solution.py:232
  49.4 4.8 %collective-permute-done.5.refs_7_ = f32[1032,128]{1,0:T(8,128)S(1)} collective-permute-done((f32[1032,128]{1,0:T(8,128)S(1)}, f32[1032,128]{1,0:T(8,128)S(1)}, u32[]{:S(2)}, u32[]{:S(2)}) %collective-permute-start.5) | collective-permute-done | bytes 528416 | tf_op jit(solution)/shard_map/ppermute | solution.py:232
  55.9 1.1 %collective-permute-start.7 = (f32[392,128]{1,0:T(8,128)S(1)}, f32[392,128]{1,0:T(8,128)S(1)}, u32[]{:S(2)}, u32[]{:S(2)}) collective-permute-start(f32[392,128]{1,0:T(8,128)S(1)} %get-tuple-element.41), channel_id=1, source_target_pairs={{0,16},{1,17},{2,18},{3,19},{4,20},{5,21},{6,22},{7,23},{8,24},{9,... | collective-permute-start | bytes 602120 | tf_op jit(solution)/shard_map/ppermute | solution.py:232
  57.1 2.8 %collective-permute-start.8 = (f32[392,128]{1,0:T(8,128)S(1)}, f32[392,128]{1,0:T(8,128)S(1)}, u32[]{:S(2)}, u32[]{:S(2)}) collective-permute-start(f32[392,128]{1,0:T(8,128)S(1)} %get-tuple-element.42), channel_id=1, source_target_pairs={{0,24},{1,25},{2,26},{3,27},{4,28},{5,29},{6,30},{7,31},{8,16},{9,... | collective-permute-start | bytes 602120 | tf_op jit(solution)/shard_map/ppermute | solution.py:232
  59.8 1.6 %collective-permute-done.11.refs_3_ = f32[520,128]{1,0:T(8,128)S(1)} collective-permute-done((f32[520,128]{1,0:T(8,128)S(1)}, f32[520,128]{1,0:T(8,128)S(1)}, u32[]{:S(2)}, u32[]{:S(2)}) %collective-permute-start.11) | collective-permute-done | bytes 266272 | tf_op jit(solution)/shard_map/ppermute | solution.py:232
  63.0 1.1 %collective-permute-start.13 = (f32[136,128]{1,0:T(8,128)S(1)}, f32[136,128]{1,0:T(8,128)S(1)}, u32[]{:S(2)}, u32[]{:S(2)}) collective-permute-start(f32[136,128]{1,0:T(8,128)S(1)} %get-tuple-element.49), channel_id=1, source_target_pairs={{0,16},{1,17},{2,18},{3,19},{4,20},{5,21},{6,22},{7,23},{8,24},{9,... | collective-permute-start | bytes 208904 | tf_op jit(solution)/shard_map/ppermute | solution.py:232
  64.1 2.4 %collective-permute-done.12.refs_5_ = f32[136,128]{1,0:T(8,128)S(1)} collective-permute-done((f32[136,128]{1,0:T(8,128)S(1)}, f32[136,128]{1,0:T(8,128)S(1)}, u32[]{:S(2)}, u32[]{:S(2)}) %collective-permute-start.12) | collective-permute-done | bytes 69664 | tf_op jit(solution)/shard_map/ppermute | solution.py:232
  66.9 1.9 %collective-permute-done.13.refs_6_ = f32[136,128]{1,0:T(8,128)S(1)} collective-permute-done((f32[136,128]{1,0:T(8,128)S(1)}, f32[136,128]{1,0:T(8,128)S(1)}, u32[]{:S(2)}, u32[]{:S(2)}) %collective-permute-start.13) | collective-permute-done | bytes 69664 | tf_op jit(solution)/shard_map/ppermute | solution.py:232
  68.8 3.2 %collective-permute-done.14.refs_7_ = f32[136,128]{1,0:T(8,128)S(1)} collective-permute-done((f32[136,128]{1,0:T(8,128)S(1)}, f32[136,128]{1,0:T(8,128)S(1)}, u32[]{:S(2)}, u32[]{:S(2)}) %collective-permute-start.14) | collective-permute-done | bytes 69664 | tf_op jit(solution)/shard_map/ppermute | solution.py:232
  72.7 1.3 %collective-permute-done.15.other = f32[264,128]{1,0:T(8,128)S(1)} collective-permute-done((f32[264,128]{1,0:T(8,128)S(1)}, f32[264,128]{1,0:T(8,128)S(1)}, u32[]{:S(2)}, u32[]{:S(2)}) %collective-permute-start.15) | collective-permute-done | bytes 135200 | tf_op jit(solution)/shard_map/ppermute | solution.py:232
  74.7 2.0 %collective-permute-start.16 = (f32[64,128]{1,0:T(8,128)S(1)}, f32[64,128]{1,0:T(8,128)S(1)}, u32[]{:S(2)}, u32[]{:S(2)}) collective-permute-start(f32[64,128]{1,0:T(8,128)S(1)} %get-tuple-element.54), channel_id=1, source_target_pairs={{0,1},{1,0},{2,3},{3,2},{4,5},{5,4},{6,7},{7,6},{8,9},{9,8},{10,11... | collective-permute-start | bytes 98312 | tf_op jit(solution)/shard_map/ppermute | solution.py:232
  76.7 3.6 %collective-permute-start.17 = (f32[64,128]{1,0:T(8,128)S(1)}, f32[64,128]{1,0:T(8,128)S(1)}, u32[]{:S(2)}, u32[]{:S(2)}) collective-permute-start(f32[64,128]{1,0:T(8,128)S(1)} %get-tuple-element.55), channel_id=1, source_target_pairs={{0,2},{1,3},{2,0},{3,1},{4,6},{5,7},{6,4},{7,5},{8,10},{9,11},{10,... | collective-permute-start | bytes 98312 | tf_op jit(solution)/shard_map/ppermute | solution.py:232
  80.2 2.2 %collective-permute-done.17.refs_2_ = f32[64,128]{1,0:T(8,128)S(1)} collective-permute-done((f32[64,128]{1,0:T(8,128)S(1)}, f32[64,128]{1,0:T(8,128)S(1)}, u32[]{:S(2)}, u32[]{:S(2)}) %collective-permute-start.17) | collective-permute-done | bytes 32800 | tf_op jit(solution)/shard_map/ppermute | solution.py:232
  82.5 2.9 %collective-permute-done.18.refs_3_ = f32[64,128]{1,0:T(8,128)S(1)} collective-permute-done((f32[64,128]{1,0:T(8,128)S(1)}, f32[64,128]{1,0:T(8,128)S(1)}, u32[]{:S(2)}, u32[]{:S(2)}) %collective-permute-start.18) | collective-permute-done | bytes 32800 | tf_op jit(solution)/shard_map/ppermute | solution.py:232
  85.4 1.2 %assemble.1 = f32[4,1,4,2048]{3,2,1,0:T(4,128)} custom-call(s32[4]{0:T(128)S(1)} %pad_add_fusion.place, f32[64,128]{1,0:T(8,128)S(1)} %get-tuple-element.53.refs_0_, f32[64,128]{1,0:T(8,128)S(1)} %collective-permute-done.16.refs_1_, f32[64,128]{1,0:T(8,128)S(1)} %collective-permute-done.17.refs_2_, f32[64,128]{1,0:T(8,128)S(1)} %collective-permute-done.18.refs_3_), custom_call_target="tpu_custom_call" | custom-call | flops 1000000000 | bytes 1 | tf_op jit(solution)/shard_map/assemble/pallas_call | solution.py:219
  (27 shorter events, 7.7 us)
Async XLA Ops:
  0.7 0.7 copy-start
  1.4 0.7 copy-start.1
  7.5 17.6 %collective-permute-start = (f32[520,128]{1,0:T(8,128)S(1)}, f32[520,128]{1,0:T(8,128)S(1)}, u32[]{:S(2)}, u32[]{:S(2)}) collective-permute-start(f32[520,128]{1,0:T(8,128)S(1)} %get-tuple-element.32), channel_id=1, source_target_pairs={{0,32},{1,33},{2,34},{3,35},{4,36},{5,37},{6,38},{7,39},{8,40},{9,... | collective-permute-start | bytes 798728 | tf_op jit(solution)/shard_map/ppermute | solution.py:232
  9.2 16.1 %collective-permute-start.1 = (f32[520,128]{1,0:T(8,128)S(1)}, f32[520,128]{1,0:T(8,128)S(1)}, u32[]{:S(2)}, u32[]{:S(2)}) collective-permute-start(f32[520,128]{1,0:T(8,128)S(1)} %get-tuple-element.33), channel_id=1, source_target_pairs={{0,64},{1,65},{2,66},{3,67},{4,68},{5,69},{6,70},{7,71},{8,72},{9,... | collective-permute-start | bytes 798728 | tf_op jit(solution)/shard_map/ppermute | solution.py:232
  12.1 14.5 %collective-permute-start.2 = (f32[520,128]{1,0:T(8,128)S(1)}, f32[520,128]{1,0:T(8,128)S(1)}, u32[]{:S(2)}, u32[]{:S(2)}) collective-permute-start(f32[520,128]{1,0:T(8,128)S(1)} %get-tuple-element.34), channel_id=1, source_target_pairs={{0,96},{1,97},{2,98},{3,99},{4,100},{5,101},{6,102},{7,103},{8,104... | collective-permute-start | bytes 798728 | tf_op jit(solution)/shard_map/ppermute | solution.py:232
  20.6 15.0 %collective-permute-start.3 = (f32[1032,128]{1,0:T(8,128)S(1)}, f32[1032,128]{1,0:T(8,128)S(1)}, u32[]{:S(2)}, u32[]{:S(2)}) collective-permute-start(f32[1032,128]{1,0:T(8,128)S(1)} %get-tuple-element.36), channel_id=1, source_target_pairs={{0,32},{1,33},{2,34},{3,35},{4,36},{5,37},{6,38},{7,39},{8,40},{9,... | collective-permute-start | bytes 1585160 | tf_op jit(solution)/shard_map/ppermute | solution.py:232
  21.0 28.4 %collective-permute-start.4 = (f32[1032,128]{1,0:T(8,128)S(1)}, f32[1032,128]{1,0:T(8,128)S(1)}, u32[]{:S(2)}, u32[]{:S(2)}) collective-permute-start(f32[1032,128]{1,0:T(8,128)S(1)} %get-tuple-element.37), channel_id=1, source_target_pairs={{0,64},{1,65},{2,66},{3,67},{4,68},{5,69},{6,70},{7,71},{8,72},{9,... | collective-permute-start | bytes 1585160 | tf_op jit(solution)/shard_map/ppermute | solution.py:232
  25.1 29.1 %collective-permute-start.5 = (f32[1032,128]{1,0:T(8,128)S(1)}, f32[1032,128]{1,0:T(8,128)S(1)}, u32[]{:S(2)}, u32[]{:S(2)}) collective-permute-start(f32[1032,128]{1,0:T(8,128)S(1)} %get-tuple-element.38), channel_id=1, source_target_pairs={{0,96},{1,97},{2,98},{3,99},{4,100},{5,101},{6,102},{7,103},{8,104... | collective-permute-start | bytes 1585160 | tf_op jit(solution)/shard_map/ppermute | solution.py:232
  32.1 25.0 %collective-permute-start.9 = (f32[520,128]{1,0:T(8,128)S(1)}, f32[520,128]{1,0:T(8,128)S(1)}, u32[]{:S(2)}, u32[]{:S(2)}) collective-permute-start(f32[520,128]{1,0:T(8,128)S(1)} %get-tuple-element.44), channel_id=1, source_target_pairs={{0,32},{1,33},{2,34},{3,35},{4,36},{5,37},{6,38},{7,39},{8,40},{9,... | collective-permute-start | bytes 798728 | tf_op jit(solution)/shard_map/ppermute | solution.py:232
  32.2 27.7 %collective-permute-start.10 = (f32[520,128]{1,0:T(8,128)S(1)}, f32[520,128]{1,0:T(8,128)S(1)}, u32[]{:S(2)}, u32[]{:S(2)}) collective-permute-start(f32[520,128]{1,0:T(8,128)S(1)} %get-tuple-element.45), channel_id=1, source_target_pairs={{0,64},{1,65},{2,66},{3,67},{4,68},{5,69},{6,70},{7,71},{8,72},{9,... | collective-permute-start | bytes 798728 | tf_op jit(solution)/shard_map/ppermute | solution.py:232
  35.6 25.8 %collective-permute-start.11 = (f32[520,128]{1,0:T(8,128)S(1)}, f32[520,128]{1,0:T(8,128)S(1)}, u32[]{:S(2)}, u32[]{:S(2)}) collective-permute-start(f32[520,128]{1,0:T(8,128)S(1)} %get-tuple-element.46), channel_id=1, source_target_pairs={{0,96},{1,97},{2,98},{3,99},{4,100},{5,101},{6,102},{7,103},{8,104... | collective-permute-start | bytes 798728 | tf_op jit(solution)/shard_map/ppermute | solution.py:232
  55.0 16.9 %collective-permute-start.6 = (f32[392,128]{1,0:T(8,128)S(1)}, f32[392,128]{1,0:T(8,128)S(1)}, u32[]{:S(2)}, u32[]{:S(2)}) collective-permute-start(f32[392,128]{1,0:T(8,128)S(1)} %get-tuple-element.40), channel_id=1, source_target_pairs={{0,8},{1,9},{2,10},{3,11},{4,12},{5,13},{6,14},{7,15},{8,0},{9,1},... | collective-permute-start | bytes 602120 | tf_op jit(solution)/shard_map/ppermute | solution.py:232
  55.9 16.0 %collective-permute-start.7 = (f32[392,128]{1,0:T(8,128)S(1)}, f32[392,128]{1,0:T(8,128)S(1)}, u32[]{:S(2)}, u32[]{:S(2)}) collective-permute-start(f32[392,128]{1,0:T(8,128)S(1)} %get-tuple-element.41), channel_id=1, source_target_pairs={{0,16},{1,17},{2,18},{3,19},{4,20},{5,21},{6,22},{7,23},{8,24},{9,... | collective-permute-start | bytes 602120 | tf_op jit(solution)/shard_map/ppermute | solution.py:232
  57.1 14.9 %collective-permute-start.8 = (f32[392,128]{1,0:T(8,128)S(1)}, f32[392,128]{1,0:T(8,128)S(1)}, u32[]{:S(2)}, u32[]{:S(2)}) collective-permute-start(f32[392,128]{1,0:T(8,128)S(1)} %get-tuple-element.42), channel_id=1, source_target_pairs={{0,24},{1,25},{2,26},{3,27},{4,28},{5,29},{6,30},{7,31},{8,16},{9,... | collective-permute-start | bytes 602120 | tf_op jit(solution)/shard_map/ppermute | solution.py:232
  62.1 4.4 %collective-permute-start.12 = (f32[136,128]{1,0:T(8,128)S(1)}, f32[136,128]{1,0:T(8,128)S(1)}, u32[]{:S(2)}, u32[]{:S(2)}) collective-permute-start(f32[136,128]{1,0:T(8,128)S(1)} %get-tuple-element.48), channel_id=1, source_target_pairs={{0,8},{1,9},{2,10},{3,11},{4,12},{5,13},{6,14},{7,15},{8,0},{9,1},... | collective-permute-start | bytes 208904 | tf_op jit(solution)/shard_map/ppermute | solution.py:232
  63.0 5.8 %collective-permute-start.13 = (f32[136,128]{1,0:T(8,128)S(1)}, f32[136,128]{1,0:T(8,128)S(1)}, u32[]{:S(2)}, u32[]{:S(2)}) collective-permute-start(f32[136,128]{1,0:T(8,128)S(1)} %get-tuple-element.49), channel_id=1, source_target_pairs={{0,16},{1,17},{2,18},{3,19},{4,20},{5,21},{6,22},{7,23},{8,24},{9,... | collective-permute-start | bytes 208904 | tf_op jit(solution)/shard_map/ppermute | solution.py:232
  66.5 5.5 %collective-permute-start.14 = (f32[136,128]{1,0:T(8,128)S(1)}, f32[136,128]{1,0:T(8,128)S(1)}, u32[]{:S(2)}, u32[]{:S(2)}) collective-permute-start(f32[136,128]{1,0:T(8,128)S(1)} %get-tuple-element.50), channel_id=1, source_target_pairs={{0,24},{1,25},{2,26},{3,27},{4,28},{5,29},{6,30},{7,31},{8,16},{9,... | collective-permute-start | bytes 208904 | tf_op jit(solution)/shard_map/ppermute | solution.py:232
  72.6 1.4 %collective-permute-start.15 = (f32[264,128]{1,0:T(8,128)S(1)}, f32[264,128]{1,0:T(8,128)S(1)}, u32[]{:S(2)}, u32[]{:S(2)}) collective-permute-start(f32[264,128]{1,0:T(8,128)S(1)} %get-tuple-element.52), channel_id=1, source_target_pairs={{0,4},{1,5},{2,6},{3,7},{4,0},{5,1},{6,2},{7,3},{8,12},{9,13},{10,... | collective-permute-start | bytes 405512 | tf_op jit(solution)/shard_map/ppermute | solution.py:232
  74.7 5.6 %collective-permute-start.16 = (f32[64,128]{1,0:T(8,128)S(1)}, f32[64,128]{1,0:T(8,128)S(1)}, u32[]{:S(2)}, u32[]{:S(2)}) collective-permute-start(f32[64,128]{1,0:T(8,128)S(1)} %get-tuple-element.54), channel_id=1, source_target_pairs={{0,1},{1,0},{2,3},{3,2},{4,5},{5,4},{6,7},{7,6},{8,9},{9,8},{10,11... | collective-permute-start | bytes 98312 | tf_op jit(solution)/shard_map/ppermute | solution.py:232
  76.7 5.8 %collective-permute-start.17 = (f32[64,128]{1,0:T(8,128)S(1)}, f32[64,128]{1,0:T(8,128)S(1)}, u32[]{:S(2)}, u32[]{:S(2)}) collective-permute-start(f32[64,128]{1,0:T(8,128)S(1)} %get-tuple-element.55), channel_id=1, source_target_pairs={{0,2},{1,3},{2,0},{3,1},{4,6},{5,7},{6,4},{7,5},{8,10},{9,11},{10,... | collective-permute-start | bytes 98312 | tf_op jit(solution)/shard_map/ppermute | solution.py:232
  80.2 5.1 %collective-permute-start.18 = (f32[64,128]{1,0:T(8,128)S(1)}, f32[64,128]{1,0:T(8,128)S(1)}, u32[]{:S(2)}, u32[]{:S(2)}) collective-permute-start(f32[64,128]{1,0:T(8,128)S(1)} %get-tuple-element.56), channel_id=1, source_target_pairs={{0,3},{1,2},{2,1},{3,0},{4,7},{5,6},{6,5},{7,4},{8,11},{9,10},{10,... | collective-permute-start | bytes 98312 | tf_op jit(solution)/shard_map/ppermute | solution.py:232

commit v3 on v2

v3 whole, which is shorter than its diff:
```python
import functools
import math

import jax
import jax.numpy as jnp
from jax import lax
from jax.experimental import pallas as pl
from jax.experimental.pallas import tpu as pltpu
from jax.sharding import PartitionSpec as P

N = 4
SAMPLES = 16
LANES = 128
CHANNELS = 4
X_ROWS = 32
CORE_ROWS = 16
EARLY = 3
VMEM = 40 * 2**20


def merge_two(a, b, a_in_front):
    one = jnp.float32(1.0)
    weight_a = jnp.where(a_in_front, one, b[3])
    weight_b = jnp.where(a_in_front, a[3], one)
    return [a[k] * weight_a + b[k] * weight_b for k in range(3)] + [a[3] * b[3]]


def merge_four(parts, ranks):
    even = merge_two(parts[0], parts[2], (ranks[0] < ranks[2])[None])
    odd = merge_two(parts[1], parts[3], (ranks[1] < ranks[3])[None])
    return merge_two(even, odd, (ranks[0] < ranks[1])[None])


def read(ref, start, rows):
    return ref[pl.ds(pl.multiple_of(start, 8), rows), :].reshape(rows // 8, 8, LANES)


def write(ref, start, value):
    ref[pl.ds(start, value.shape[0] * 8), :] = value.reshape(value.shape[0] * 8, LANES)


def vmem_specs(count):
    return [pl.BlockSpec(memory_space=pltpu.VMEM)] * count


def smem_specs(count):
    return [pl.BlockSpec(memory_space=pltpu.SMEM)] * count


def rows_of(*counts):
    return [jax.ShapeDtypeStruct((rows, LANES), jnp.float32) for rows in counts]


def cost(microseconds):
    return pl.CostEstimate(flops=int(microseconds * 1e8), bytes_accessed=1, transcendentals=0)


def march_kernel(place, numbers, *refs, sizes, depth_total):
    fields, messages = refs[: len(sizes)], refs[-len(sizes) :]
    group = pl.program_id(0)
    scale = -1.0 / (depth_total * math.log(2.0))
    slope = [numbers[0, k] * 0.5 for k in range(3)]
    offset = [numbers[0, 3 + k] * 0.5 for k in range(3)]
    quadratic = numbers[0, 6] * scale
    constant = numbers[0, 7] * scale

    for field, message, blocks in zip(fields, messages, sizes):
        for block in range(blocks):
            shape = (X_ROWS, LANES)
            squares = jnp.zeros(shape, jnp.float32)
            through = jnp.ones(shape, jnp.float32)
            totals = [jnp.zeros(shape, jnp.float32) for _ in range(3)]
            for i in range(SAMPLES):
                s = field[i, :, block * LANES : (block + 1) * LANES]
                squares = squares + s * s
                after = jnp.exp2(squares * quadratic + constant * float(i + 1))
                weight = through - after
                through = after
                for k in range(3):
                    totals[k] = totals[k] + weight * jnp.tanh(s * slope[k] + offset[k])
            opacity = 1.0 - through
            channels = [0.5 * (opacity + totals[k]) for k in range(3)] + [through]
            for k in range(CHANNELS):
                row = ((k * N + group) * blocks + block) * X_ROWS
                message[pl.ds(pl.multiple_of(row, X_ROWS), X_ROWS), :] = channels[k]

    @pl.when(group == 0)
    def _():
        own = jnp.full((8, LANES), numbers[0, 8])
        for message, blocks in zip(messages, sizes):
            message[pl.ds(CHANNELS * N * blocks * X_ROWS, 8), :] = own


def march(field, place, numbers, parts, depth_total, after=()):
    def field_spec(axis, step, first, blocks):
        def index(group, where):
            y, x = (where[0] ^ step, group) if axis == "y" else (group, (where[1] + step) & 3)
            return 0, 0, y * N + x, first // blocks

        return pl.BlockSpec((SAMPLES, None, X_ROWS, blocks * LANES), index)

    sizes = [blocks for *_, blocks in parts]
    rows = [CHANNELS * N * blocks * X_ROWS + 8 for blocks in sizes]
    return pl.pallas_call(
        functools.partial(march_kernel, sizes=sizes, depth_total=depth_total),
        grid_spec=pltpu.PrefetchScalarGridSpec(
            num_scalar_prefetch=1,
            grid=(N,),
            in_specs=smem_specs(1)
            + [field_spec(*part) for part in parts]
            + [pl.BlockSpec(memory_space=pl.ANY)] * len(after),
            out_specs=[pl.BlockSpec((count, LANES), lambda group, where: (0, 0)) for count in rows],
        ),
        out_shape=rows_of(*rows),
        compiler_params=pltpu.CompilerParams(vmem_limit_bytes=VMEM),
        cost_estimate=cost(1.2 + 1.0 * sum(sizes)),
        name="march",
    )(place, numbers, *([field] * len(parts)), *after)


def turn_kernel(place, *refs):
    inputs, outputs = refs[:N], refs[N:]
    for brick, message in enumerate(inputs):
        for step in range(N):
            y = place[0] ^ step
            for k in range(CHANNELS):
                rows = message[pl.ds(pl.multiple_of((k * N + y) * X_ROWS, X_ROWS), X_ROWS), :]
                outputs[step][pl.ds((brick * CHANNELS + k) * X_ROWS, X_ROWS), :] = rows
            rank = message[pl.ds(CHANNELS * N * X_ROWS, 8), :]
            outputs[step][pl.ds(N * CHANNELS * X_ROWS + brick * 8, 8), :] = rank


def turn(place, messages):
    return pl.pallas_call(
        turn_kernel,
        in_specs=smem_specs(1) + vmem_specs(N),
        out_specs=vmem_specs(N),
        out_shape=rows_of(*[N * (CHANNELS * X_ROWS + 8)] * N),
        compiler_params=pltpu.CompilerParams(vmem_limit_bytes=VMEM),
        cost_estimate=cost(0.8),
        name="turn",
    )(place, *messages)


def merge_y_kernel(place, *refs):
    inputs, outputs = refs[:N], refs[-N:]
    slab = EARLY * X_ROWS
    ranks = [m[pl.ds(CHANNELS * N * slab, 8), :] for m in inputs]
    for step in range(N):
        x = (place[1] + step) & 3
        parts = [[read(m, (k * N + x) * slab, slab) for k in range(CHANNELS)] for m in inputs]
        merged = merge_four(parts, ranks)
        for k in range(CHANNELS):
            write(outputs[step], k * slab, merged[k])
        outputs[step][pl.ds(CHANNELS * slab, 8), :] = ranks[0]


def merge_y(place, messages, after=()):
    return pl.pallas_call(
        merge_y_kernel,
        in_specs=smem_specs(1) + vmem_specs(N) + [pl.BlockSpec(memory_space=pl.ANY)] * len(after),
        out_specs=vmem_specs(N),
        out_shape=rows_of(*[CHANNELS * EARLY * X_ROWS + 8] * N),
        compiler_params=pltpu.CompilerParams(vmem_limit_bytes=VMEM),
        cost_estimate=cost(0.9),
        name="merge_y",
    )(place, *messages, *after)


def merge_x_kernel(place, *refs):
    by_x, by_y, outputs = refs[:N], refs[N : 2 * N], refs[2 * N :]
    ranks = [m[pl.ds(CHANNELS * EARLY * X_ROWS, 8), :] for m in by_x]
    late_ranks = [[m[pl.ds(N * CHANNELS * X_ROWS + x * 8, 8), :] for m in by_y] for x in range(N)]
    for flip in range(2):
        core = place[2] ^ flip
        for block in range(EARLY):
            starts = [(k * EARLY + block) * X_ROWS + core * CORE_ROWS for k in range(CHANNELS)]
            merged = merge_four([[read(m, start, CORE_ROWS) for start in starts] for m in by_x], ranks)
            for k in range(CHANNELS):
                write(outputs[flip], (k * N + block) * CORE_ROWS, merged[k])
        bricks = []
        for x in range(N):
            starts = [(x * CHANNELS + k) * X_ROWS + core * CORE_ROWS for k in range(CHANNELS)]
            bricks.append(merge_four([[read(m, start, CORE_ROWS) for start in starts] for m in by_y], late_ranks[x]))
        merged = merge_four(bricks, [late_ranks[x][0] for x in range(N)])
        for k in range(CHANNELS):
            write(outputs[flip], (k * N + EARLY) * CORE_ROWS, merged[k])
        outputs[flip][pl.ds(CHANNELS * N * CORE_ROWS, 8), :] = ranks[0]


def merge_x(place, by_x, by_y):
    return pl.pallas_call(
        merge_x_kernel,
        in_specs=smem_specs(1) + vmem_specs(2 * N),
        out_specs=vmem_specs(2),
        out_shape=rows_of(*[CHANNELS * N * CORE_ROWS + 8] * 2),
        compiler_params=pltpu.CompilerParams(vmem_limit_bytes=VMEM),
        cost_estimate=cost(0.5),
        name="merge_x",
    )(place, *by_x, *by_y)


def merge_core_kernel(place, mine, other, *targets):
    where = CHANNELS * N * CORE_ROWS
    in_front = (mine[pl.ds(where, 8), :] < other[pl.ds(where, 8), :])[None]
    for block in range(N):
        parts = [[read(m, (k * N + block) * CORE_ROWS, CORE_ROWS) for k in range(CHANNELS)] for m in (mine, other)]
        merged = merge_two(parts[0], parts[1], in_front)
        merged[3] = 1.0 - merged[3]
        for k in range(CHANNELS):
            for step, target in enumerate(targets):
                z = (place[3] + step) & 3
                value = jnp.where(z >= 2, merged[k][1], merged[k][0])
                value = jnp.where((z & 1) == 1, pltpu.roll(value, 4, 0), value)
                target[pl.ds((k * N + block) * 4, 4), :] = value[:4]


def merge_core(place, mine, other):
    rows = CHANNELS * N * 4
    return pl.pallas_call(
        merge_core_kernel,
        in_specs=smem_specs(1) + vmem_specs(2),
        out_specs=vmem_specs(N),
        out_shape=rows_of(*[rows] * N),
        compiler_params=pltpu.CompilerParams(vmem_limit_bytes=VMEM),
        cost_estimate=cost(0.5),
        name="merge_core",
    )(place, mine, other)


def assemble_kernel(place, *refs):
    sources, out = refs[:N], refs[N]
    for step, source in enumerate(sources):
        tile = (place[3] - step) & 3
        for k in range(CHANNELS):
            for block in range(N):
                lanes = pl.ds(pl.multiple_of((tile * N + block) * LANES, LANES), LANES)
                out[k, 0, :, lanes] = source[pl.ds((k * N + block) * 4, 4), :]


def assemble(place, pieces):
    return pl.pallas_call(
        assemble_kernel,
        in_specs=smem_specs(1) + vmem_specs(4),
        out_specs=pl.BlockSpec(memory_space=pltpu.VMEM),
        out_shape=jax.ShapeDtypeStruct((CHANNELS, 1, 4, N * N * LANES), jnp.float32),
        compiler_params=pltpu.CompilerParams(vmem_limit_bytes=VMEM),
        cost_estimate=cost(1.0),
        name="assemble",
    )(place, *pieces)


def exchange(value, axis, step):
    def target(device):
        y, x, core, z = device // (2 * N * N), device // (2 * N) % N, device // N % 2, device % N
        if axis == "y":
            y ^= step
        elif axis == "x":
            x = (x + step) % N
        elif axis == "core":
            core ^= step
        else:
            z = (z + step) % N
        return ((y * N + x) * 2 + core) * N + z

    return lax.ppermute(value, ("depth", "tile"), [(i, target(i)) for i in range(2 * N * N * N)])


def all_steps(pieces, axis, order):
    moved = {step: exchange(pieces[step], axis, step) for step in order}
    return [pieces[0], moved[1], moved[2], moved[3]]


def body(scalar_field, depth_rank, palette, extinction):
    depth = lax.axis_index("depth")
    place = jnp.stack([depth >> 3, (depth >> 1) & 3, depth & 1, lax.axis_index("tile")]).astype(jnp.int32)
    slopes = palette.T
    rank = depth_rank.astype(jnp.float32)
    numbers = jnp.concatenate([slopes[0:1], slopes[1:2], extinction[None], rank], axis=1)
    depth_total = scalar_field.shape[0] * lax.axis_size("depth")
    (far,) = march(scalar_field, place, numbers, [("y", 2, 0, EARLY)], depth_total)
    parts = [("y", step, 0, EARLY) for step in (0, 1, 3)] + [("x", step, EARLY, 1) for step in range(N)]
    own, *near = march(scalar_field, place, numbers, parts, depth_total, [far])
    early = all_steps([own, near[0], far, near[1]], "y", (2, 1, 3))
    turned = turn(place, all_steps(near[2:], "x", (1, 2, 3)))
    by_x = all_steps(merge_y(place, early, turned[:1]), "x", (1, 2, 3))
    mine, send = merge_x(place, by_x, all_steps(turned, "y", (2, 1, 3)))
    pieces = merge_core(place, mine, exchange(send, "core", 1))
    return assemble(place, all_steps(pieces, "z", (2, 1, 3)))


def solution(mesh):
    in_specs = (P("depth", "tile", None, None), P("depth", "tile"), P(), P())
    out_specs = P(None, None, ("depth", "tile"), None)
    return jax.shard_map(body, mesh=mesh, in_specs=in_specs, out_specs=out_specs, check_vma=False)
```

time: 87 us -> 73.5 us (0.84)
  waiting for transfers between devices: 32.5 us -> 26.5 us
  starting transfers between devices: 28.8 us -> 23.3 us
  Pallas kernels: 23.1 us -> 21.2 us
    ppermute x19 -> x16, waiting for transfers between devices: 32.5 us -> 26.5 us  [exchange(): lax.ppermute(value, ('depth', 'tile'), [(i, target(i)) for i in range(2 *...]
    ppermute x19 -> x16, starting transfers between devices: 28.8 us -> 23.3 us  [exchange(): lax.ppermute(value, ('depth', 'tile'), [(i, target(i)) for i in range(2 *...]
    pallas_call x6 -> x5, Pallas kernels: 21.3 us -> 19.4 us  [the longest x2 17.1 us: march(): pl.pallas_call(functools.partial(march_kernel, sizes=sizes, depth_total=d...]
    unnamed x4 -> x0, local copies, waits for them, and re-layouts: 1.34 us -> none
  transfers between devices with their start and end apart: 19 -> 16, of which waited for: 11 -> 11; matrix products, arithmetic and copies ran while one was open for 0% -> 0% of each run, Pallas kernels for 18% -> 19%
where the time goes in v3:
time: 73.5 us; the launch traced here: 73.3 us
  waiting for transfers between devices  26.5 us (36%)
  starting transfers between devices  23.3 us (32%)
  Pallas kernels  21.2 us (29%)
  other arithmetic  0.81 us (1%)
  local copies, waits for them, and re-layouts  0.76 us (1%)
    ppermute x16, waiting for transfers between devices, exchange(): lax.ppermute(value, ('depth', 'tile'), [(i, target(i)) for i in range(2 *...  26.5 us
    ppermute x16, starting transfers between devices, exchange(): lax.ppermute(value, ('depth', 'tile'), [(i, target(i)) for i in range(2 *...  23.3 us
    pallas_call x2, Pallas kernels, march(): pl.pallas_call(functools.partial(march_kernel, sizes=sizes, depth_total=d...  17.1 us
  transfers between devices with their start and end apart: 16, of which 11 were waited for; matrix products, arithmetic and copies ran while one was open for 0% of the time, Pallas kernels for 19%

profile of v3, /device:TPU:6, one launch (start us, length us, event | category | flops | bytes accessed | tf_op | source)
XLA Modules:
  0.0 73.3 jit_solution(12514461987819052787)
XLA Ops:
  0.7 0.8 %fusion = (f32[1,3]{1,0:T(1,128)S(1)}, f32[1,3]{1,0:T(1,128)S(1)}) fusion(f32[2,3]{1,0:T(2,128)} %bitcast.6), kind=kLoop, calls=%fused_computation.2 | loop fusion | bytes 48 | tf_op jit(solution)/shard_map/slice | solution.py:279
  2.2 4.7 %march.2.refs_7_ = f32[1544,128]{1,0:T(8,128)S(1)} custom-call(s32[4]{0:T(128)S(1)} %pad_add_fusion.place, f32[1,9]{1,0:T(1,128)S(1)} %pad_maximum_fusion.numbers, f32[16,1,512,512]{3,2,1,0:T(8,128)} %refs_6_.1), custom_call_target="tpu_custom_call" | custom-call | flops 420000000 | bytes 1 | tf_op jit(solution)/shard_map/march/pallas_call | solution.py:104
  6.9 3.3 %collective-permute-start.1 = (f32[1544,128]{1,0:T(8,128)S(1)}, f32[1544,128]{1,0:T(8,128)S(1)}, u32[]{:S(2)}, u32[]{:S(2)}) collective-permute-start(f32[1544,128]{1,0:T(8,128)S(1)} %march.2.refs_7_), channel_id=1, source_target_pairs={{0,64},{1,65},{2,66},{3,67},{4,68},{5,69},{6,70},{7,71},{8,72},{9,... | collective-permute-start | bytes 2371592 | tf_op jit(solution)/shard_map/ppermute | solution.py:266
  10.2 12.5 %march.3 = (f32[1544,128]{1,0:T(8,128)S(1)}, f32[1544,128]{1,0:T(8,128)S(1)}, f32[1544,128]{1,0:T(8,128)S(1)}, f32[520,128]{1,0:T(8,128)S(1)}, f32[520,128]{1,0:...) custom-call(s32[4]{0:T(128)S(1)} %pad_add_fusion.place, f32[1,9]{1,0:T(1,128)S(1)} %pad_maximum_fusion.numbers, ...), custom_call_target="tpu_custom_call" | custom-call | flops 1420000000 | bytes 1 | tf_op jit(solution)/shard_map/march/pallas_call | solution.py:104
  24.2 2.4 %collective-permute-start.4 = (f32[520,128]{1,0:T(8,128)S(1)}, f32[520,128]{1,0:T(8,128)S(1)}, u32[]{:S(2)}, u32[]{:S(2)}) collective-permute-start(f32[520,128]{1,0:T(8,128)S(1)} %get-tuple-element.31), channel_id=1, source_target_pairs={{0,16},{1,17},{2,18},{3,19},{4,20},{5,21},{6,22},{7,23},{8,24},{9,... | collective-permute-start | bytes 798728 | tf_op jit(solution)/shard_map/ppermute | solution.py:266
  26.6 5.4 %collective-permute-done.3.refs_1_ = f32[520,128]{1,0:T(8,128)S(1)} collective-permute-done((f32[520,128]{1,0:T(8,128)S(1)}, f32[520,128]{1,0:T(8,128)S(1)}, u32[]{:S(2)}, u32[]{:S(2)}) %collective-permute-start.3) | collective-permute-done | bytes 266272 | tf_op jit(solution)/shard_map/ppermute | solution.py:266
  32.0 0.8 %collective-permute-start.5 = (f32[520,128]{1,0:T(8,128)S(1)}, f32[520,128]{1,0:T(8,128)S(1)}, u32[]{:S(2)}, u32[]{:S(2)}) collective-permute-start(f32[520,128]{1,0:T(8,128)S(1)} %get-tuple-element.32), channel_id=1, source_target_pairs={{0,24},{1,25},{2,26},{3,27},{4,28},{5,29},{6,30},{7,31},{8,0},{9,1... | collective-permute-start | bytes 798728 | tf_op jit(solution)/shard_map/ppermute | solution.py:266
  33.1 6.6 %collective-permute-done.5.refs_3_ = f32[520,128]{1,0:T(8,128)S(1)} collective-permute-done((f32[520,128]{1,0:T(8,128)S(1)}, f32[520,128]{1,0:T(8,128)S(1)}, u32[]{:S(2)}, u32[]{:S(2)}) %collective-permute-start.5) | collective-permute-done | bytes 266272 | tf_op jit(solution)/shard_map/ppermute | solution.py:266
  41.0 2.5 %collective-permute-start.10 = (f32[544,128]{1,0:T(8,128)S(1)}, f32[544,128]{1,0:T(8,128)S(1)}, u32[]{:S(2)}, u32[]{:S(2)}) collective-permute-start(f32[544,128]{1,0:T(8,128)S(1)} %get-tuple-element.39), channel_id=1, source_target_pairs={{0,64},{1,65},{2,66},{3,67},{4,68},{5,69},{6,70},{7,71},{8,72},{9,... | collective-permute-start | bytes 835592 | tf_op jit(solution)/shard_map/ppermute | solution.py:266
  43.5 1.6 %collective-permute-start.11 = (f32[544,128]{1,0:T(8,128)S(1)}, f32[544,128]{1,0:T(8,128)S(1)}, u32[]{:S(2)}, u32[]{:S(2)}) collective-permute-start(f32[544,128]{1,0:T(8,128)S(1)} %get-tuple-element.40), channel_id=1, source_target_pairs={{0,96},{1,97},{2,98},{3,99},{4,100},{5,101},{6,102},{7,103},{8,104... | collective-permute-start | bytes 835592 | tf_op jit(solution)/shard_map/ppermute | solution.py:266
  45.0 1.3 %collective-permute-done.refs_1_ = f32[1544,128]{1,0:T(8,128)S(1)} collective-permute-done((f32[1544,128]{1,0:T(8,128)S(1)}, f32[1544,128]{1,0:T(8,128)S(1)}, u32[]{:S(2)}, u32[]{:S(2)}) %collective-permute-start) | collective-permute-done | bytes 790560 | tf_op jit(solution)/shard_map/ppermute | solution.py:266
  46.3 0.9 %merge_y.1 = (f32[392,128]{1,0:T(8,128)S(1)}, f32[392,128]{1,0:T(8,128)S(1)}, f32[392,128]{1,0:T(8,128)S(1)}, f32[392,128]{1,0:T(8,128)S(1)}) custom-call(s32[4]{0:T(128)S(1)} %pad_add_fusion.place, f32[1544,128]{1,0:T(8,128)S(1)} %get-tuple-element.26.refs_0_, f32[1544,128]{1,0:T(8,128)S(1)} %collective-permute-done.refs_1_, ...), custom_call_target="tpu_custom_call" | custom-call | flops 90000000 | bytes 1 | tf_op jit(solution)/shard_map/merge_y/pallas_call | solution.py:159
  47.7 2.4 %collective-permute-start.7 = (f32[392,128]{1,0:T(8,128)S(1)}, f32[392,128]{1,0:T(8,128)S(1)}, u32[]{:S(2)}, u32[]{:S(2)}) collective-permute-start(f32[392,128]{1,0:T(8,128)S(1)} %get-tuple-element.36), channel_id=1, source_target_pairs={{0,16},{1,17},{2,18},{3,19},{4,20},{5,21},{6,22},{7,23},{8,24},{9,... | collective-permute-start | bytes 602120 | tf_op jit(solution)/shard_map/ppermute | solution.py:266
  50.2 2.1 %collective-permute-done.9.refs_5_ = f32[544,128]{1,0:T(8,128)S(1)} collective-permute-done((f32[544,128]{1,0:T(8,128)S(1)}, f32[544,128]{1,0:T(8,128)S(1)}, u32[]{:S(2)}, u32[]{:S(2)}) %collective-permute-start.9) | collective-permute-done | bytes 278560 | tf_op jit(solution)/shard_map/ppermute | solution.py:266
  52.3 0.8 %collective-permute-start.8 = (f32[392,128]{1,0:T(8,128)S(1)}, f32[392,128]{1,0:T(8,128)S(1)}, u32[]{:S(2)}, u32[]{:S(2)}) collective-permute-start(f32[392,128]{1,0:T(8,128)S(1)} %get-tuple-element.37), channel_id=1, source_target_pairs={{0,24},{1,25},{2,26},{3,27},{4,28},{5,29},{6,30},{7,31},{8,0},{9,1... | collective-permute-start | bytes 602120 | tf_op jit(solution)/shard_map/ppermute | solution.py:266
  53.1 3.7 %collective-permute-done.10.refs_6_ = f32[544,128]{1,0:T(8,128)S(1)} collective-permute-done((f32[544,128]{1,0:T(8,128)S(1)}, f32[544,128]{1,0:T(8,128)S(1)}, u32[]{:S(2)}, u32[]{:S(2)}) %collective-permute-start.10) | collective-permute-done | bytes 278560 | tf_op jit(solution)/shard_map/ppermute | solution.py:266
  57.2 2.6 %collective-permute-done.8.refs_3_ = f32[392,128]{1,0:T(8,128)S(1)} collective-permute-done((f32[392,128]{1,0:T(8,128)S(1)}, f32[392,128]{1,0:T(8,128)S(1)}, u32[]{:S(2)}, u32[]{:S(2)}) %collective-permute-start.8) | collective-permute-done | bytes 200736 | tf_op jit(solution)/shard_map/ppermute | solution.py:266
  60.6 1.3 %collective-permute-done.12.other = f32[264,128]{1,0:T(8,128)S(1)} collective-permute-done((f32[264,128]{1,0:T(8,128)S(1)}, f32[264,128]{1,0:T(8,128)S(1)}, u32[]{:S(2)}, u32[]{:S(2)}) %collective-permute-start.12) | collective-permute-done | bytes 135200 | tf_op jit(solution)/shard_map/ppermute | solution.py:266
  62.6 2.0 %collective-permute-start.13 = (f32[64,128]{1,0:T(8,128)S(1)}, f32[64,128]{1,0:T(8,128)S(1)}, u32[]{:S(2)}, u32[]{:S(2)}) collective-permute-start(f32[64,128]{1,0:T(8,128)S(1)} %get-tuple-element.44), channel_id=1, source_target_pairs={{0,1},{1,2},{2,3},{3,0},{4,5},{5,6},{6,7},{7,4},{8,9},{9,10},{10,1... | collective-permute-start | bytes 98312 | tf_op jit(solution)/shard_map/ppermute | solution.py:266
  64.6 3.6 %collective-permute-start.14 = (f32[64,128]{1,0:T(8,128)S(1)}, f32[64,128]{1,0:T(8,128)S(1)}, u32[]{:S(2)}, u32[]{:S(2)}) collective-permute-start(f32[64,128]{1,0:T(8,128)S(1)} %get-tuple-element.45), channel_id=1, source_target_pairs={{0,2},{1,3},{2,0},{3,1},{4,6},{5,7},{6,4},{7,5},{8,10},{9,11},{10,... | collective-permute-start | bytes 98312 | tf_op jit(solution)/shard_map/ppermute | solution.py:266
  68.1 1.0 %collective-permute-start.15 = (f32[64,128]{1,0:T(8,128)S(1)}, f32[64,128]{1,0:T(8,128)S(1)}, u32[]{:S(2)}, u32[]{:S(2)}) collective-permute-start(f32[64,128]{1,0:T(8,128)S(1)} %get-tuple-element.46), channel_id=1, source_target_pairs={{0,3},{1,0},{2,1},{3,2},{4,7},{5,4},{6,5},{7,6},{8,11},{9,8},{10,9... | collective-permute-start | bytes 98312 | tf_op jit(solution)/shard_map/ppermute | solution.py:266
  69.2 1.2 %collective-permute-done.14.refs_2_ = f32[64,128]{1,0:T(8,128)S(1)} collective-permute-done((f32[64,128]{1,0:T(8,128)S(1)}, f32[64,128]{1,0:T(8,128)S(1)}, u32[]{:S(2)}, u32[]{:S(2)}) %collective-permute-start.14) | collective-permute-done | bytes 32800 | tf_op jit(solution)/shard_map/ppermute | solution.py:266
  70.4 1.7 %collective-permute-done.15.refs_3_ = f32[64,128]{1,0:T(8,128)S(1)} collective-permute-done((f32[64,128]{1,0:T(8,128)S(1)}, f32[64,128]{1,0:T(8,128)S(1)}, u32[]{:S(2)}, u32[]{:S(2)}) %collective-permute-start.15) | collective-permute-done | bytes 32800 | tf_op jit(solution)/shard_map/ppermute | solution.py:266
  72.1 1.2 %assemble.1 = f32[4,1,4,2048]{3,2,1,0:T(4,128)} custom-call(s32[4]{0:T(128)S(1)} %pad_add_fusion.place, f32[64,128]{1,0:T(8,128)S(1)} %get-tuple-element.43.refs_0_, f32[64,128]{1,0:T(8,128)S(1)} %collective-permute-done.13.refs_1_, f32[64,128]{1,0:T(8,128)S(1)} %collective-permute-done.14.refs_2_, f32[64,128]{1,0:T(8,128)S(1)} %collective-permute-done.15.refs_3_), custom_call_target="tpu_custom_call" | custom-call | flops 100000000 | bytes 1 | tf_op jit(solution)/shard_map/assemble/pallas_call | solution.py:242
  (18 shorter events, 6.3 us)
Async XLA Ops:
  6.9 36.6 %collective-permute-start.1 = (f32[1544,128]{1,0:T(8,128)S(1)}, f32[1544,128]{1,0:T(8,128)S(1)}, u32[]{:S(2)}, u32[]{:S(2)}) collective-permute-start(f32[1544,128]{1,0:T(8,128)S(1)} %march.2.refs_7_), channel_id=1, source_target_pairs={{0,64},{1,65},{2,66},{3,67},{4,68},{5,69},{6,70},{7,71},{8,72},{9,... | collective-permute-start | bytes 2371592 | tf_op jit(solution)/shard_map/ppermute | solution.py:266
  22.6 9.4 %collective-permute-start.3 = (f32[520,128]{1,0:T(8,128)S(1)}, f32[520,128]{1,0:T(8,128)S(1)}, u32[]{:S(2)}, u32[]{:S(2)}) collective-permute-start(f32[520,128]{1,0:T(8,128)S(1)} %get-tuple-element.30), channel_id=1, source_target_pairs={{0,8},{1,9},{2,10},{3,11},{4,12},{5,13},{6,14},{7,15},{8,16},{9,17... | collective-permute-start | bytes 798728 | tf_op jit(solution)/shard_map/ppermute | solution.py:266
  23.2 23.1 %collective-permute-start = (f32[1544,128]{1,0:T(8,128)S(1)}, f32[1544,128]{1,0:T(8,128)S(1)}, u32[]{:S(2)}, u32[]{:S(2)}) collective-permute-start(f32[1544,128]{1,0:T(8,128)S(1)} %get-tuple-element.27), channel_id=1, source_target_pairs={{0,32},{1,33},{2,34},{3,35},{4,36},{5,37},{6,38},{7,39},{8,40},{9,... | collective-permute-start | bytes 2371592 | tf_op jit(solution)/shard_map/ppermute | solution.py:266
  23.8 22.5 %collective-permute-start.2 = (f32[1544,128]{1,0:T(8,128)S(1)}, f32[1544,128]{1,0:T(8,128)S(1)}, u32[]{:S(2)}, u32[]{:S(2)}) collective-permute-start(f32[1544,128]{1,0:T(8,128)S(1)} %get-tuple-element.28), channel_id=1, source_target_pairs={{0,96},{1,97},{2,98},{3,99},{4,100},{5,101},{6,102},{7,103},{8,104... | collective-permute-start | bytes 2371592 | tf_op jit(solution)/shard_map/ppermute | solution.py:266
  24.2 8.8 %collective-permute-start.4 = (f32[520,128]{1,0:T(8,128)S(1)}, f32[520,128]{1,0:T(8,128)S(1)}, u32[]{:S(2)}, u32[]{:S(2)}) collective-permute-start(f32[520,128]{1,0:T(8,128)S(1)} %get-tuple-element.31), channel_id=1, source_target_pairs={{0,16},{1,17},{2,18},{3,19},{4,20},{5,21},{6,22},{7,23},{8,24},{9,... | collective-permute-start | bytes 798728 | tf_op jit(solution)/shard_map/ppermute | solution.py:266
  32.0 7.6 %collective-permute-start.5 = (f32[520,128]{1,0:T(8,128)S(1)}, f32[520,128]{1,0:T(8,128)S(1)}, u32[]{:S(2)}, u32[]{:S(2)}) collective-permute-start(f32[520,128]{1,0:T(8,128)S(1)} %get-tuple-element.32), channel_id=1, source_target_pairs={{0,24},{1,25},{2,26},{3,27},{4,28},{5,29},{6,30},{7,31},{8,0},{9,1... | collective-permute-start | bytes 798728 | tf_op jit(solution)/shard_map/ppermute | solution.py:266
  40.3 12.0 %collective-permute-start.9 = (f32[544,128]{1,0:T(8,128)S(1)}, f32[544,128]{1,0:T(8,128)S(1)}, u32[]{:S(2)}, u32[]{:S(2)}) collective-permute-start(f32[544,128]{1,0:T(8,128)S(1)} %get-tuple-element.38), channel_id=1, source_target_pairs={{0,32},{1,33},{2,34},{3,35},{4,36},{5,37},{6,38},{7,39},{8,40},{9,... | collective-permute-start | bytes 835592 | tf_op jit(solution)/shard_map/ppermute | solution.py:266
  41.0 15.8 %collective-permute-start.10 = (f32[544,128]{1,0:T(8,128)S(1)}, f32[544,128]{1,0:T(8,128)S(1)}, u32[]{:S(2)}, u32[]{:S(2)}) collective-permute-start(f32[544,128]{1,0:T(8,128)S(1)} %get-tuple-element.39), channel_id=1, source_target_pairs={{0,64},{1,65},{2,66},{3,67},{4,68},{5,69},{6,70},{7,71},{8,72},{9,... | collective-permute-start | bytes 835592 | tf_op jit(solution)/shard_map/ppermute | solution.py:266
  43.5 13.7 %collective-permute-start.11 = (f32[544,128]{1,0:T(8,128)S(1)}, f32[544,128]{1,0:T(8,128)S(1)}, u32[]{:S(2)}, u32[]{:S(2)}) collective-permute-start(f32[544,128]{1,0:T(8,128)S(1)} %get-tuple-element.40), channel_id=1, source_target_pairs={{0,96},{1,97},{2,98},{3,99},{4,100},{5,101},{6,102},{7,103},{8,104... | collective-permute-start | bytes 835592 | tf_op jit(solution)/shard_map/ppermute | solution.py:266
  47.2 10.0 %collective-permute-start.6 = (f32[392,128]{1,0:T(8,128)S(1)}, f32[392,128]{1,0:T(8,128)S(1)}, u32[]{:S(2)}, u32[]{:S(2)}) collective-permute-start(f32[392,128]{1,0:T(8,128)S(1)} %get-tuple-element.35), channel_id=1, source_target_pairs={{0,8},{1,9},{2,10},{3,11},{4,12},{5,13},{6,14},{7,15},{8,16},{9,17... | collective-permute-start | bytes 602120 | tf_op jit(solution)/shard_map/ppermute | solution.py:266
  47.7 9.5 %collective-permute-start.7 = (f32[392,128]{1,0:T(8,128)S(1)}, f32[392,128]{1,0:T(8,128)S(1)}, u32[]{:S(2)}, u32[]{:S(2)}) collective-permute-start(f32[392,128]{1,0:T(8,128)S(1)} %get-tuple-element.36), channel_id=1, source_target_pairs={{0,16},{1,17},{2,18},{3,19},{4,20},{5,21},{6,22},{7,23},{8,24},{9,... | collective-permute-start | bytes 602120 | tf_op jit(solution)/shard_map/ppermute | solution.py:266
  52.3 7.5 %collective-permute-start.8 = (f32[392,128]{1,0:T(8,128)S(1)}, f32[392,128]{1,0:T(8,128)S(1)}, u32[]{:S(2)}, u32[]{:S(2)}) collective-permute-start(f32[392,128]{1,0:T(8,128)S(1)} %get-tuple-element.37), channel_id=1, source_target_pairs={{0,24},{1,25},{2,26},{3,27},{4,28},{5,29},{6,30},{7,31},{8,0},{9,1... | collective-permute-start | bytes 602120 | tf_op jit(solution)/shard_map/ppermute | solution.py:266
  60.5 1.4 %collective-permute-start.12 = (f32[264,128]{1,0:T(8,128)S(1)}, f32[264,128]{1,0:T(8,128)S(1)}, u32[]{:S(2)}, u32[]{:S(2)}) collective-permute-start(f32[264,128]{1,0:T(8,128)S(1)} %get-tuple-element.42), channel_id=1, source_target_pairs={{0,4},{1,5},{2,6},{3,7},{4,0},{5,1},{6,2},{7,3},{8,12},{9,13},{10,... | collective-permute-start | bytes 405512 | tf_op jit(solution)/shard_map/ppermute | solution.py:266
  62.6 6.6 %collective-permute-start.13 = (f32[64,128]{1,0:T(8,128)S(1)}, f32[64,128]{1,0:T(8,128)S(1)}, u32[]{:S(2)}, u32[]{:S(2)}) collective-permute-start(f32[64,128]{1,0:T(8,128)S(1)} %get-tuple-element.44), channel_id=1, source_target_pairs={{0,1},{1,2},{2,3},{3,0},{4,5},{5,6},{6,7},{7,4},{8,9},{9,10},{10,1... | collective-permute-start | bytes 98312 | tf_op jit(solution)/shard_map/ppermute | solution.py:266
  64.6 5.8 %collective-permute-start.14 = (f32[64,128]{1,0:T(8,128)S(1)}, f32[64,128]{1,0:T(8,128)S(1)}, u32[]{:S(2)}, u32[]{:S(2)}) collective-permute-start(f32[64,128]{1,0:T(8,128)S(1)} %get-tuple-element.45), channel_id=1, source_target_pairs={{0,2},{1,3},{2,0},{3,1},{4,6},{5,7},{6,4},{7,5},{8,10},{9,11},{10,... | collective-permute-start | bytes 98312 | tf_op jit(solution)/shard_map/ppermute | solution.py:266
  68.1 3.9 %collective-permute-start.15 = (f32[64,128]{1,0:T(8,128)S(1)}, f32[64,128]{1,0:T(8,128)S(1)}, u32[]{:S(2)}, u32[]{:S(2)}) collective-permute-start(f32[64,128]{1,0:T(8,128)S(1)} %get-tuple-element.46), channel_id=1, source_target_pairs={{0,3},{1,0},{2,1},{3,2},{4,7},{5,4},{6,5},{7,6},{8,11},{9,8},{10,9... | collective-permute-start | bytes 98312 | tf_op jit(solution)/shard_map/ppermute | solution.py:266

commit v4 on v3

--- a/solution.py
+++ b/solution.py
@@ -55,14 +55,14 @@
     return pl.CostEstimate(flops=int(microseconds * 1e8), bytes_accessed=1, transcendentals=0)
 
 
-def march_kernel(place, numbers, *refs, sizes, depth_total):
+def march_kernel(place, numbers, own_rank, *refs, sizes, depth_total):
     fields, messages = refs[: len(sizes)], refs[-len(sizes) :]
     group = pl.program_id(0)
     scale = -1.0 / (depth_total * math.log(2.0))
-    slope = [numbers[0, k] * 0.5 for k in range(3)]
-    offset = [numbers[0, 3 + k] * 0.5 for k in range(3)]
-    quadratic = numbers[0, 6] * scale
-    constant = numbers[0, 7] * scale
+    slope = [numbers[0, 0, k] * 0.5 for k in range(3)]
+    offset = [numbers[0, 1, k] * 0.5 for k in range(3)]
+    quadratic = numbers[1, 0, 0] * scale
+    constant = numbers[1, 1, 0] * scale
 
     for field, message, blocks in zip(fields, messages, sizes):
         for block in range(blocks):
@@ -86,12 +86,12 @@
 
     @pl.when(group == 0)
     def _():
-        own = jnp.full((8, LANES), numbers[0, 8])
+        own = jnp.full((8, LANES), own_rank[0, 0].astype(jnp.float32))
         for message, blocks in zip(messages, sizes):
             message[pl.ds(CHANNELS * N * blocks * X_ROWS, 8), :] = own
 
 
-def march(field, place, numbers, parts, depth_total, after=()):
+def march(field, place, parameters, parts, depth_total, after=()):
     def field_spec(axis, step, first, blocks):
         def index(group, where):
             y, x = (where[0] ^ step, group) if axis == "y" else (group, (where[1] + step) & 3)
@@ -106,7 +106,9 @@
         grid_spec=pltpu.PrefetchScalarGridSpec(
             num_scalar_prefetch=1,
             grid=(N,),
-            in_specs=smem_specs(1)
+            in_specs=[
+                pl.BlockSpec(v.shape, lambda group, where, v=v: (0,) * v.ndim, memory_space=pltpu.SMEM) for v in parameters
+            ]
             + [field_spec(*part) for part in parts]
             + [pl.BlockSpec(memory_space=pl.ANY)] * len(after),
             out_specs=[pl.BlockSpec((count, LANES), lambda group, where: (0, 0)) for count in rows],
@@ -115,7 +117,7 @@
         compiler_params=pltpu.CompilerParams(vmem_limit_bytes=VMEM),
         cost_estimate=cost(1.2 + 1.0 * sum(sizes)),
         name="march",
-    )(place, numbers, *([field] * len(parts)), *after)
+    )(place, *parameters, *([field] * len(parts)), *after)
 
 
 def turn_kernel(place, *refs):
@@ -274,13 +276,12 @@
 def body(scalar_field, depth_rank, palette, extinction):
     depth = lax.axis_index("depth")
     place = jnp.stack([depth >> 3, (depth >> 1) & 3, depth & 1, lax.axis_index("tile")]).astype(jnp.int32)
-    slopes = palette.T
-    rank = depth_rank.astype(jnp.float32)
-    numbers = jnp.concatenate([slopes[0:1], slopes[1:2], extinction[None], rank], axis=1)
+    which = lax.broadcasted_iota(jnp.int32, (2, 2, 3), 0)
+    parameters = (jnp.where(which == 0, palette.T[None], extinction[None, :, None]), depth_rank)
     depth_total = scalar_field.shape[0] * lax.axis_size("depth")
-    (far,) = march(scalar_field, place, numbers, [("y", 2, 0, EARLY)], depth_total)
+    (far,) = march(scalar_field, place, parameters, [("y", 2, 0, EARLY)], depth_total)
     parts = [("y", step, 0, EARLY) for step in (0, 1, 3)] + [("x", step, EARLY, 1) for step in range(N)]
-    own, *near = march(scalar_field, place, numbers, parts, depth_total, [far])
+    own, *near = march(scalar_field, place, parameters, parts, depth_total, [far])
     early = all_steps([own, near[0], far, near[1]], "y", (2, 1, 3))
     turned = turn(place, all_steps(near[2:], "x", (1, 2, 3)))
     by_x = all_steps(merge_y(place, early, turned[:1]), "x", (1, 2, 3))

time: 73.5 us -> 72.7 us (0.989)
  local copies, waits for them, and re-layouts: 0.76 us -> 0 us
    slice x1 -> x0, local copies, waits for them, and re-layouts: 0.76 us -> none  [body(): slopes[0:1]]
    select_n x0 -> x1, other arithmetic: none -> 0.75 us  [body(): jnp.where(which == 0, palette.T[None], extinction[None, :, None])]
where the time goes in v4:
time: 72.7 us; the launch traced here: 72.6 us
  waiting for transfers between devices  26.5 us (36%)
  starting transfers between devices  23.3 us (32%)
  Pallas kernels  21.2 us (29%)
  other arithmetic  0.84 us (1%)
    ppermute x16, waiting for transfers between devices, exchange(): lax.ppermute(value, ('depth', 'tile'), [(i, target(i)) for i in range(2 *...  26.5 us
    ppermute x16, starting transfers between devices, exchange(): lax.ppermute(value, ('depth', 'tile'), [(i, target(i)) for i in range(2 *...  23.3 us
    pallas_call x2, Pallas kernels, march(): pl.pallas_call(functools.partial(march_kernel, sizes=sizes, depth_total=d...  17.1 us
  transfers between devices with their start and end apart: 16, of which 11 were waited for; matrix products, arithmetic and copies ran while one was open for 0% of the time, Pallas kernels for 19%

profile of v4, /device:TPU:6, one launch (start us, length us, event | category | flops | bytes accessed | tf_op | source)
XLA Modules:
  0.0 72.6 jit_solution(10418702213320109570)
XLA Ops:
  1.5 4.7 %march.2.refs_7_ = f32[1544,128]{1,0:T(8,128)S(1)} custom-call(s32[4]{0:T(128)S(1)} %pad_add_fusion.place, f32[2,2,3]{2,1,0:T(2,128)S(1)} %broadcast_select_fusion.numbers, s32[1,1]{1,0:T(1,128)S(6)} %copy.5.own_rank, f32[16,1,512,512]{3,2,1,0:T(8,128)} %refs_6_.1), custom_call_target="tpu_custom_call" | custom-call | flops 420000000 | bytes 1 | tf_op jit(solution)/shard_map/march/pallas_call | solution.py:104
  6.2 3.3 %collective-permute-start.1 = (f32[1544,128]{1,0:T(8,128)S(1)}, f32[1544,128]{1,0:T(8,128)S(1)}, u32[]{:S(2)}, u32[]{:S(2)}) collective-permute-start(f32[1544,128]{1,0:T(8,128)S(1)} %march.2.refs_7_), channel_id=1, source_target_pairs={{0,64},{1,65},{2,66},{3,67},{4,68},{5,69},{6,70},{7,71},{8,72},{9,... | collective-permute-start | bytes 2371592 | tf_op jit(solution)/shard_map/ppermute | solution.py:268
  9.4 12.5 %march.3 = (f32[1544,128]{1,0:T(8,128)S(1)}, f32[1544,128]{1,0:T(8,128)S(1)}, f32[1544,128]{1,0:T(8,128)S(1)}, f32[520,128]{1,0:T(8,128)S(1)}, f32[520,128]{1,0:...) custom-call(s32[4]{0:T(128)S(1)} %pad_add_fusion.place, f32[2,2,3]{2,1,0:T(2,128)S(1)} %broadcast_select_fusion.numbers, ...), custom_call_target="tpu_custom_call" | custom-call | flops 1420000000 | bytes 1 | tf_op jit(solution)/shard_map/march/pallas_call | solution.py:104
  23.5 2.4 %collective-permute-start.4 = (f32[520,128]{1,0:T(8,128)S(1)}, f32[520,128]{1,0:T(8,128)S(1)}, u32[]{:S(2)}, u32[]{:S(2)}) collective-permute-start(f32[520,128]{1,0:T(8,128)S(1)} %get-tuple-element.31), channel_id=1, source_target_pairs={{0,16},{1,17},{2,18},{3,19},{4,20},{5,21},{6,22},{7,23},{8,24},{9,... | collective-permute-start | bytes 798728 | tf_op jit(solution)/shard_map/ppermute | solution.py:268
  25.9 5.4 %collective-permute-done.3.refs_1_ = f32[520,128]{1,0:T(8,128)S(1)} collective-permute-done((f32[520,128]{1,0:T(8,128)S(1)}, f32[520,128]{1,0:T(8,128)S(1)}, u32[]{:S(2)}, u32[]{:S(2)}) %collective-permute-start.3) | collective-permute-done | bytes 266272 | tf_op jit(solution)/shard_map/ppermute | solution.py:268
  31.3 0.8 %collective-permute-start.5 = (f32[520,128]{1,0:T(8,128)S(1)}, f32[520,128]{1,0:T(8,128)S(1)}, u32[]{:S(2)}, u32[]{:S(2)}) collective-permute-start(f32[520,128]{1,0:T(8,128)S(1)} %get-tuple-element.32), channel_id=1, source_target_pairs={{0,24},{1,25},{2,26},{3,27},{4,28},{5,29},{6,30},{7,31},{8,0},{9,1... | collective-permute-start | bytes 798728 | tf_op jit(solution)/shard_map/ppermute | solution.py:268
  32.3 6.6 %collective-permute-done.5.refs_3_ = f32[520,128]{1,0:T(8,128)S(1)} collective-permute-done((f32[520,128]{1,0:T(8,128)S(1)}, f32[520,128]{1,0:T(8,128)S(1)}, u32[]{:S(2)}, u32[]{:S(2)}) %collective-permute-start.5) | collective-permute-done | bytes 266272 | tf_op jit(solution)/shard_map/ppermute | solution.py:268
  39.5 0.8 %collective-permute-start.9 = (f32[544,128]{1,0:T(8,128)S(1)}, f32[544,128]{1,0:T(8,128)S(1)}, u32[]{:S(2)}, u32[]{:S(2)}) collective-permute-start(f32[544,128]{1,0:T(8,128)S(1)} %get-tuple-element.38), channel_id=1, source_target_pairs={{0,32},{1,33},{2,34},{3,35},{4,36},{5,37},{6,38},{7,39},{8,40},{9,... | collective-permute-start | bytes 835592 | tf_op jit(solution)/shard_map/ppermute | solution.py:268
  40.3 2.5 %collective-permute-start.10 = (f32[544,128]{1,0:T(8,128)S(1)}, f32[544,128]{1,0:T(8,128)S(1)}, u32[]{:S(2)}, u32[]{:S(2)}) collective-permute-start(f32[544,128]{1,0:T(8,128)S(1)} %get-tuple-element.39), channel_id=1, source_target_pairs={{0,64},{1,65},{2,66},{3,67},{4,68},{5,69},{6,70},{7,71},{8,72},{9,... | collective-permute-start | bytes 835592 | tf_op jit(solution)/shard_map/ppermute | solution.py:268
  42.8 1.6 %collective-permute-start.11 = (f32[544,128]{1,0:T(8,128)S(1)}, f32[544,128]{1,0:T(8,128)S(1)}, u32[]{:S(2)}, u32[]{:S(2)}) collective-permute-start(f32[544,128]{1,0:T(8,128)S(1)} %get-tuple-element.40), channel_id=1, source_target_pairs={{0,96},{1,97},{2,98},{3,99},{4,100},{5,101},{6,102},{7,103},{8,104... | collective-permute-start | bytes 835592 | tf_op jit(solution)/shard_map/ppermute | solution.py:268
  44.3 1.3 %collective-permute-done.refs_1_ = f32[1544,128]{1,0:T(8,128)S(1)} collective-permute-done((f32[1544,128]{1,0:T(8,128)S(1)}, f32[1544,128]{1,0:T(8,128)S(1)}, u32[]{:S(2)}, u32[]{:S(2)}) %collective-permute-start) | collective-permute-done | bytes 790560 | tf_op jit(solution)/shard_map/ppermute | solution.py:268
  45.6 0.9 %merge_y.1 = (f32[392,128]{1,0:T(8,128)S(1)}, f32[392,128]{1,0:T(8,128)S(1)}, f32[392,128]{1,0:T(8,128)S(1)}, f32[392,128]{1,0:T(8,128)S(1)}) custom-call(s32[4]{0:T(128)S(1)} %pad_add_fusion.place, f32[1544,128]{1,0:T(8,128)S(1)} %get-tuple-element.26.refs_0_, f32[1544,128]{1,0:T(8,128)S(1)} %collective-permute-done.refs_1_, ...), custom_call_target="tpu_custom_call" | custom-call | flops 90000000 | bytes 1 | tf_op jit(solution)/shard_map/merge_y/pallas_call | solution.py:161
  47.0 2.4 %collective-permute-start.7 = (f32[392,128]{1,0:T(8,128)S(1)}, f32[392,128]{1,0:T(8,128)S(1)}, u32[]{:S(2)}, u32[]{:S(2)}) collective-permute-start(f32[392,128]{1,0:T(8,128)S(1)} %get-tuple-element.36), channel_id=1, source_target_pairs={{0,16},{1,17},{2,18},{3,19},{4,20},{5,21},{6,22},{7,23},{8,24},{9,... | collective-permute-start | bytes 602120 | tf_op jit(solution)/shard_map/ppermute | solution.py:268
  49.4 2.1 %collective-permute-done.9.refs_5_ = f32[544,128]{1,0:T(8,128)S(1)} collective-permute-done((f32[544,128]{1,0:T(8,128)S(1)}, f32[544,128]{1,0:T(8,128)S(1)}, u32[]{:S(2)}, u32[]{:S(2)}) %collective-permute-start.9) | collective-permute-done | bytes 278560 | tf_op jit(solution)/shard_map/ppermute | solution.py:268
  51.6 0.8 %collective-permute-start.8 = (f32[392,128]{1,0:T(8,128)S(1)}, f32[392,128]{1,0:T(8,128)S(1)}, u32[]{:S(2)}, u32[]{:S(2)}) collective-permute-start(f32[392,128]{1,0:T(8,128)S(1)} %get-tuple-element.37), channel_id=1, source_target_pairs={{0,24},{1,25},{2,26},{3,27},{4,28},{5,29},{6,30},{7,31},{8,0},{9,1... | collective-permute-start | bytes 602120 | tf_op jit(solution)/shard_map/ppermute | solution.py:268
  52.4 3.7 %collective-permute-done.10.refs_6_ = f32[544,128]{1,0:T(8,128)S(1)} collective-permute-done((f32[544,128]{1,0:T(8,128)S(1)}, f32[544,128]{1,0:T(8,128)S(1)}, u32[]{:S(2)}, u32[]{:S(2)}) %collective-permute-start.10) | collective-permute-done | bytes 278560 | tf_op jit(solution)/shard_map/ppermute | solution.py:268
  56.5 2.6 %collective-permute-done.8.refs_3_ = f32[392,128]{1,0:T(8,128)S(1)} collective-permute-done((f32[392,128]{1,0:T(8,128)S(1)}, f32[392,128]{1,0:T(8,128)S(1)}, u32[]{:S(2)}, u32[]{:S(2)}) %collective-permute-start.8) | collective-permute-done | bytes 200736 | tf_op jit(solution)/shard_map/ppermute | solution.py:268
  59.9 1.3 %collective-permute-done.12.other = f32[264,128]{1,0:T(8,128)S(1)} collective-permute-done((f32[264,128]{1,0:T(8,128)S(1)}, f32[264,128]{1,0:T(8,128)S(1)}, u32[]{:S(2)}, u32[]{:S(2)}) %collective-permute-start.12) | collective-permute-done | bytes 135200 | tf_op jit(solution)/shard_map/ppermute | solution.py:268
  61.9 2.0 %collective-permute-start.13 = (f32[64,128]{1,0:T(8,128)S(1)}, f32[64,128]{1,0:T(8,128)S(1)}, u32[]{:S(2)}, u32[]{:S(2)}) collective-permute-start(f32[64,128]{1,0:T(8,128)S(1)} %get-tuple-element.44), channel_id=1, source_target_pairs={{0,1},{1,2},{2,3},{3,0},{4,5},{5,6},{6,7},{7,4},{8,9},{9,10},{10,1... | collective-permute-start | bytes 98312 | tf_op jit(solution)/shard_map/ppermute | solution.py:268
  63.8 3.6 %collective-permute-start.14 = (f32[64,128]{1,0:T(8,128)S(1)}, f32[64,128]{1,0:T(8,128)S(1)}, u32[]{:S(2)}, u32[]{:S(2)}) collective-permute-start(f32[64,128]{1,0:T(8,128)S(1)} %get-tuple-element.45), channel_id=1, source_target_pairs={{0,2},{1,3},{2,0},{3,1},{4,6},{5,7},{6,4},{7,5},{8,10},{9,11},{10,... | collective-permute-start | bytes 98312 | tf_op jit(solution)/shard_map/ppermute | solution.py:268
  67.4 1.0 %collective-permute-start.15 = (f32[64,128]{1,0:T(8,128)S(1)}, f32[64,128]{1,0:T(8,128)S(1)}, u32[]{:S(2)}, u32[]{:S(2)}) collective-permute-start(f32[64,128]{1,0:T(8,128)S(1)} %get-tuple-element.46), channel_id=1, source_target_pairs={{0,3},{1,0},{2,1},{3,2},{4,7},{5,4},{6,5},{7,6},{8,11},{9,8},{10,9... | collective-permute-start | bytes 98312 | tf_op jit(solution)/shard_map/ppermute | solution.py:268
  68.4 1.2 %collective-permute-done.14.refs_2_ = f32[64,128]{1,0:T(8,128)S(1)} collective-permute-done((f32[64,128]{1,0:T(8,128)S(1)}, f32[64,128]{1,0:T(8,128)S(1)}, u32[]{:S(2)}, u32[]{:S(2)}) %collective-permute-start.14) | collective-permute-done | bytes 32800 | tf_op jit(solution)/shard_map/ppermute | solution.py:268
  69.7 1.7 %collective-permute-done.15.refs_3_ = f32[64,128]{1,0:T(8,128)S(1)} collective-permute-done((f32[64,128]{1,0:T(8,128)S(1)}, f32[64,128]{1,0:T(8,128)S(1)}, u32[]{:S(2)}, u32[]{:S(2)}) %collective-permute-start.15) | collective-permute-done | bytes 32800 | tf_op jit(solution)/shard_map/ppermute | solution.py:268
  71.3 1.2 %assemble.1 = f32[4,1,4,2048]{3,2,1,0:T(4,128)} custom-call(s32[4]{0:T(128)S(1)} %pad_add_fusion.place, f32[64,128]{1,0:T(8,128)S(1)} %get-tuple-element.43.refs_0_, f32[64,128]{1,0:T(8,128)S(1)} %collective-permute-done.13.refs_1_, f32[64,128]{1,0:T(8,128)S(1)} %collective-permute-done.14.refs_2_, f32[64,128]{1,0:T(8,128)S(1)} %collective-permute-done.15.refs_3_), custom_call_target="tpu_custom_call" | custom-call | flops 100000000 | bytes 1 | tf_op jit(solution)/shard_map/assemble/pallas_call | solution.py:244
  (18 shorter events, 5.6 us)
Async XLA Ops:
  6.2 36.6 %collective-permute-start.1 = (f32[1544,128]{1,0:T(8,128)S(1)}, f32[1544,128]{1,0:T(8,128)S(1)}, u32[]{:S(2)}, u32[]{:S(2)}) collective-permute-start(f32[1544,128]{1,0:T(8,128)S(1)} %march.2.refs_7_), channel_id=1, source_target_pairs={{0,64},{1,65},{2,66},{3,67},{4,68},{5,69},{6,70},{7,71},{8,72},{9,... | collective-permute-start | bytes 2371592 | tf_op jit(solution)/shard_map/ppermute | solution.py:268
  21.9 9.4 %collective-permute-start.3 = (f32[520,128]{1,0:T(8,128)S(1)}, f32[520,128]{1,0:T(8,128)S(1)}, u32[]{:S(2)}, u32[]{:S(2)}) collective-permute-start(f32[520,128]{1,0:T(8,128)S(1)} %get-tuple-element.30), channel_id=1, source_target_pairs={{0,8},{1,9},{2,10},{3,11},{4,12},{5,13},{6,14},{7,15},{8,16},{9,17... | collective-permute-start | bytes 798728 | tf_op jit(solution)/shard_map/ppermute | solution.py:268
  22.4 23.1 %collective-permute-start = (f32[1544,128]{1,0:T(8,128)S(1)}, f32[1544,128]{1,0:T(8,128)S(1)}, u32[]{:S(2)}, u32[]{:S(2)}) collective-permute-start(f32[1544,128]{1,0:T(8,128)S(1)} %get-tuple-element.27), channel_id=1, source_target_pairs={{0,32},{1,33},{2,34},{3,35},{4,36},{5,37},{6,38},{7,39},{8,40},{9,... | collective-permute-start | bytes 2371592 | tf_op jit(solution)/shard_map/ppermute | solution.py:268
  23.1 22.5 %collective-permute-start.2 = (f32[1544,128]{1,0:T(8,128)S(1)}, f32[1544,128]{1,0:T(8,128)S(1)}, u32[]{:S(2)}, u32[]{:S(2)}) collective-permute-start(f32[1544,128]{1,0:T(8,128)S(1)} %get-tuple-element.28), channel_id=1, source_target_pairs={{0,96},{1,97},{2,98},{3,99},{4,100},{5,101},{6,102},{7,103},{8,104... | collective-permute-start | bytes 2371592 | tf_op jit(solution)/shard_map/ppermute | solution.py:268
  23.5 8.8 %collective-permute-start.4 = (f32[520,128]{1,0:T(8,128)S(1)}, f32[520,128]{1,0:T(8,128)S(1)}, u32[]{:S(2)}, u32[]{:S(2)}) collective-permute-start(f32[520,128]{1,0:T(8,128)S(1)} %get-tuple-element.31), channel_id=1, source_target_pairs={{0,16},{1,17},{2,18},{3,19},{4,20},{5,21},{6,22},{7,23},{8,24},{9,... | collective-permute-start | bytes 798728 | tf_op jit(solution)/shard_map/ppermute | solution.py:268
  31.3 7.6 %collective-permute-start.5 = (f32[520,128]{1,0:T(8,128)S(1)}, f32[520,128]{1,0:T(8,128)S(1)}, u32[]{:S(2)}, u32[]{:S(2)}) collective-permute-start(f32[520,128]{1,0:T(8,128)S(1)} %get-tuple-element.32), channel_id=1, source_target_pairs={{0,24},{1,25},{2,26},{3,27},{4,28},{5,29},{6,30},{7,31},{8,0},{9,1... | collective-permute-start | bytes 798728 | tf_op jit(solution)/shard_map/ppermute | solution.py:268
  39.5 12.0 %collective-permute-start.9 = (f32[544,128]{1,0:T(8,128)S(1)}, f32[544,128]{1,0:T(8,128)S(1)}, u32[]{:S(2)}, u32[]{:S(2)}) collective-permute-start(f32[544,128]{1,0:T(8,128)S(1)} %get-tuple-element.38), channel_id=1, source_target_pairs={{0,32},{1,33},{2,34},{3,35},{4,36},{5,37},{6,38},{7,39},{8,40},{9,... | collective-permute-start | bytes 835592 | tf_op jit(solution)/shard_map/ppermute | solution.py:268
  40.3 15.8 %collective-permute-start.10 = (f32[544,128]{1,0:T(8,128)S(1)}, f32[544,128]{1,0:T(8,128)S(1)}, u32[]{:S(2)}, u32[]{:S(2)}) collective-permute-start(f32[544,128]{1,0:T(8,128)S(1)} %get-tuple-element.39), channel_id=1, source_target_pairs={{0,64},{1,65},{2,66},{3,67},{4,68},{5,69},{6,70},{7,71},{8,72},{9,... | collective-permute-start | bytes 835592 | tf_op jit(solution)/shard_map/ppermute | solution.py:268
  42.8 13.7 %collective-permute-start.11 = (f32[544,128]{1,0:T(8,128)S(1)}, f32[544,128]{1,0:T(8,128)S(1)}, u32[]{:S(2)}, u32[]{:S(2)}) collective-permute-start(f32[544,128]{1,0:T(8,128)S(1)} %get-tuple-element.40), channel_id=1, source_target_pairs={{0,96},{1,97},{2,98},{3,99},{4,100},{5,101},{6,102},{7,103},{8,104... | collective-permute-start | bytes 835592 | tf_op jit(solution)/shard_map/ppermute | solution.py:268
  46.5 10.0 %collective-permute-start.6 = (f32[392,128]{1,0:T(8,128)S(1)}, f32[392,128]{1,0:T(8,128)S(1)}, u32[]{:S(2)}, u32[]{:S(2)}) collective-permute-start(f32[392,128]{1,0:T(8,128)S(1)} %get-tuple-element.35), channel_id=1, source_target_pairs={{0,8},{1,9},{2,10},{3,11},{4,12},{5,13},{6,14},{7,15},{8,16},{9,17... | collective-permute-start | bytes 602120 | tf_op jit(solution)/shard_map/ppermute | solution.py:268
  47.0 9.5 %collective-permute-start.7 = (f32[392,128]{1,0:T(8,128)S(1)}, f32[392,128]{1,0:T(8,128)S(1)}, u32[]{:S(2)}, u32[]{:S(2)}) collective-permute-start(f32[392,128]{1,0:T(8,128)S(1)} %get-tuple-element.36), channel_id=1, source_target_pairs={{0,16},{1,17},{2,18},{3,19},{4,20},{5,21},{6,22},{7,23},{8,24},{9,... | collective-permute-start | bytes 602120 | tf_op jit(solution)/shard_map/ppermute | solution.py:268
  51.6 7.5 %collective-permute-start.8 = (f32[392,128]{1,0:T(8,128)S(1)}, f32[392,128]{1,0:T(8,128)S(1)}, u32[]{:S(2)}, u32[]{:S(2)}) collective-permute-start(f32[392,128]{1,0:T(8,128)S(1)} %get-tuple-element.37), channel_id=1, source_target_pairs={{0,24},{1,25},{2,26},{3,27},{4,28},{5,29},{6,30},{7,31},{8,0},{9,1... | collective-permute-start | bytes 602120 | tf_op jit(solution)/shard_map/ppermute | solution.py:268
  59.8 1.4 %collective-permute-start.12 = (f32[264,128]{1,0:T(8,128)S(1)}, f32[264,128]{1,0:T(8,128)S(1)}, u32[]{:S(2)}, u32[]{:S(2)}) collective-permute-start(f32[264,128]{1,0:T(8,128)S(1)} %get-tuple-element.42), channel_id=1, source_target_pairs={{0,4},{1,5},{2,6},{3,7},{4,0},{5,1},{6,2},{7,3},{8,12},{9,13},{10,... | collective-permute-start | bytes 405512 | tf_op jit(solution)/shard_map/ppermute | solution.py:268
  61.9 6.6 %collective-permute-start.13 = (f32[64,128]{1,0:T(8,128)S(1)}, f32[64,128]{1,0:T(8,128)S(1)}, u32[]{:S(2)}, u32[]{:S(2)}) collective-permute-start(f32[64,128]{1,0:T(8,128)S(1)} %get-tuple-element.44), channel_id=1, source_target_pairs={{0,1},{1,2},{2,3},{3,0},{4,5},{5,6},{6,7},{7,4},{8,9},{9,10},{10,1... | collective-permute-start | bytes 98312 | tf_op jit(solution)/shard_map/ppermute | solution.py:268
  63.8 5.8 %collective-permute-start.14 = (f32[64,128]{1,0:T(8,128)S(1)}, f32[64,128]{1,0:T(8,128)S(1)}, u32[]{:S(2)}, u32[]{:S(2)}) collective-permute-start(f32[64,128]{1,0:T(8,128)S(1)} %get-tuple-element.45), channel_id=1, source_target_pairs={{0,2},{1,3},{2,0},{3,1},{4,6},{5,7},{6,4},{7,5},{8,10},{9,11},{10,... | collective-permute-start | bytes 98312 | tf_op jit(solution)/shard_map/ppermute | solution.py:268
  67.4 3.9 %collective-permute-start.15 = (f32[64,128]{1,0:T(8,128)S(1)}, f32[64,128]{1,0:T(8,128)S(1)}, u32[]{:S(2)}, u32[]{:S(2)}) collective-permute-start(f32[64,128]{1,0:T(8,128)S(1)} %get-tuple-element.46), channel_id=1, source_target_pairs={{0,3},{1,0},{2,1},{3,2},{4,7},{5,4},{6,5},{7,6},{8,11},{9,8},{10,9... | collective-permute-start | bytes 98312 | tf_op jit(solution)/shard_map/ppermute | solution.py:268

commit v5 on v4

--- a/solution.py
+++ b/solution.py
@@ -16,6 +16,11 @@
 CORE_ROWS = 16
 EARLY = 3
 VMEM = 40 * 2**20
+
+
+def own_place():
+    depth = lax.axis_index("depth")
+    return depth >> 3, (depth >> 1) & 3, depth & 1, lax.axis_index("tile")
 
 
 def merge_two(a, b, a_in_front):
@@ -120,7 +125,8 @@
     )(place, *parameters, *([field] * len(parts)), *after)
 
 
-def turn_kernel(place, *refs):
+def turn_kernel(*refs):
+    place = own_place()
     inputs, outputs = refs[:N], refs[N:]
     for brick, message in enumerate(inputs):
         for step in range(N):
@@ -132,44 +138,71 @@
             outputs[step][pl.ds(N * CHANNELS * X_ROWS + brick * 8, 8), :] = rank
 
 
-def turn(place, messages):
+def turn(messages):
     return pl.pallas_call(
         turn_kernel,
-        in_specs=smem_specs(1) + vmem_specs(N),
+        in_specs=vmem_specs(N),
         out_specs=vmem_specs(N),
         out_shape=rows_of(*[N * (CHANNELS * X_ROWS + 8)] * N),
         compiler_params=pltpu.CompilerParams(vmem_limit_bytes=VMEM),
         cost_estimate=cost(0.8),
         name="turn",
-    )(place, *messages)
-
-
-def merge_y_kernel(place, *refs):
-    inputs, outputs = refs[:N], refs[-N:]
+    )(*messages)
+
+
+def merge_pair_kernel(mine, other, out):
+    slab = EARLY * X_ROWS
+    rank = mine[pl.ds(CHANNELS * N * slab, 8), :]
+    in_front = (rank < other[pl.ds(CHANNELS * N * slab, 8), :])[None]
+    for x in range(N):
+        starts = [(k * N + x) * slab for k in range(CHANNELS)]
+        merged = merge_two(*[[read(m, start, slab) for start in starts] for m in (mine, other)], in_front)
+        for start, value in zip(starts, merged):
+            write(out, start, value)
+    out[pl.ds(CHANNELS * N * slab, 8), :] = rank
+
+
+def merge_pair(mine, other):
+    return pl.pallas_call(
+        merge_pair_kernel,
+        in_specs=vmem_specs(2),
+        out_specs=pl.BlockSpec(memory_space=pltpu.VMEM),
+        out_shape=rows_of(CHANNELS * N * EARLY * X_ROWS + 8)[0],
+        compiler_params=pltpu.CompilerParams(vmem_limit_bytes=VMEM),
+        cost_estimate=cost(0.6),
+        name="merge_pair",
+    )(mine, other)
+
+
+def merge_y_kernel(*refs):
+    place = own_place()
+    inputs, outputs = refs[:3], refs[-N:]
     slab = EARLY * X_ROWS
     ranks = [m[pl.ds(CHANNELS * N * slab, 8), :] for m in inputs]
     for step in range(N):
         x = (place[1] + step) & 3
-        parts = [[read(m, (k * N + x) * slab, slab) for k in range(CHANNELS)] for m in inputs]
-        merged = merge_four(parts, ranks)
+        pair, *others = [[read(m, (k * N + x) * slab, slab) for k in range(CHANNELS)] for m in inputs]
+        odd = merge_two(*others, (ranks[1] < ranks[2])[None])
+        merged = merge_two(pair, odd, (ranks[0] < ranks[1])[None])
         for k in range(CHANNELS):
             write(outputs[step], k * slab, merged[k])
         outputs[step][pl.ds(CHANNELS * slab, 8), :] = ranks[0]
 
 
-def merge_y(place, messages, after=()):
+def merge_y(messages, after=()):
     return pl.pallas_call(
         merge_y_kernel,
-        in_specs=smem_specs(1) + vmem_specs(N) + [pl.BlockSpec(memory_space=pl.ANY)] * len(after),
+        in_specs=vmem_specs(3) + [pl.BlockSpec(memory_space=pl.ANY)] * len(after),
         out_specs=vmem_specs(N),
         out_shape=rows_of(*[CHANNELS * EARLY * X_ROWS + 8] * N),
         compiler_params=pltpu.CompilerParams(vmem_limit_bytes=VMEM),
         cost_estimate=cost(0.9),
         name="merge_y",
-    )(place, *messages, *after)
-
-
-def merge_x_kernel(place, *refs):
+    )(*messages, *after)
+
+
+def merge_x_kernel(*refs):
+    place = own_place()
     by_x, by_y, outputs = refs[:N], refs[N : 2 * N], refs[2 * N :]
     ranks = [m[pl.ds(CHANNELS * EARLY * X_ROWS, 8), :] for m in by_x]
     late_ranks = [[m[pl.ds(N * CHANNELS * X_ROWS + x * 8, 8), :] for m in by_y] for x in range(N)]
@@ -190,19 +223,20 @@
         outputs[flip][pl.ds(CHANNELS * N * CORE_ROWS, 8), :] = ranks[0]
 
 
-def merge_x(place, by_x, by_y):
+def merge_x(by_x, by_y):
     return pl.pallas_call(
         merge_x_kernel,
-        in_specs=smem_specs(1) + vmem_specs(2 * N),
+        in_specs=vmem_specs(2 * N),
         out_specs=vmem_specs(2),
         out_shape=rows_of(*[CHANNELS * N * CORE_ROWS + 8] * 2),
         compiler_params=pltpu.CompilerParams(vmem_limit_bytes=VMEM),
         cost_estimate=cost(0.5),
         name="merge_x",
-    )(place, *by_x, *by_y)
-
-
-def merge_core_kernel(place, mine, other, *targets):
+    )(*by_x, *by_y)
+
+
+def merge_core_kernel(mine, other, *targets):
+    place = own_place()
     where = CHANNELS * N * CORE_ROWS
     in_front = (mine[pl.ds(where, 8), :] < other[pl.ds(where, 8), :])[None]
     for block in range(N):
@@ -217,20 +251,21 @@
                 target[pl.ds((k * N + block) * 4, 4), :] = value[:4]
 
 
-def merge_core(place, mine, other):
+def merge_core(mine, other):
     rows = CHANNELS * N * 4
     return pl.pallas_call(
         merge_core_kernel,
-        in_specs=smem_specs(1) + vmem_specs(2),
+        in_specs=vmem_specs(2),
         out_specs=vmem_specs(N),
         out_shape=rows_of(*[rows] * N),
         compiler_params=pltpu.CompilerParams(vmem_limit_bytes=VMEM),
         cost_estimate=cost(0.5),
         name="merge_core",
-    )(place, mine, other)
-
-
-def assemble_kernel(place, *refs):
+    )(mine, other)
+
+
+def assemble_kernel(*refs):
+    place = own_place()
     sources, out = refs[:N], refs[N]
     for step, source in enumerate(sources):
         tile = (place[3] - step) & 3
@@ -240,16 +275,16 @@
                 out[k, 0, :, lanes] = source[pl.ds((k * N + block) * 4, 4), :]
 
 
-def assemble(place, pieces):
+def assemble(pieces):
     return pl.pallas_call(
         assemble_kernel,
-        in_specs=smem_specs(1) + vmem_specs(4),
+        in_specs=vmem_specs(4),
         out_specs=pl.BlockSpec(memory_space=pltpu.VMEM),
         out_shape=jax.ShapeDtypeStruct((CHANNELS, 1, 4, N * N * LANES), jnp.float32),
         compiler_params=pltpu.CompilerParams(vmem_limit_bytes=VMEM),
         cost_estimate=cost(1.0),
         name="assemble",
-    )(place, *pieces)
+    )(*pieces)
 
 
 def exchange(value, axis, step):
@@ -274,8 +309,7 @@
 
 
 def body(scalar_field, depth_rank, palette, extinction):
-    depth = lax.axis_index("depth")
-    place = jnp.stack([depth >> 3, (depth >> 1) & 3, depth & 1, lax.axis_index("tile")]).astype(jnp.int32)
+    place = jnp.stack(own_place()).astype(jnp.int32)
     which = lax.broadcasted_iota(jnp.int32, (2, 2, 3), 0)
     parameters = (jnp.where(which == 0, palette.T[None], extinction[None, :, None]), depth_rank)
     depth_total = scalar_field.shape[0] * lax.axis_size("depth")
@@ -283,11 +317,11 @@
     parts = [("y", step, 0, EARLY) for step in (0, 1, 3)] + [("x", step, EARLY, 1) for step in range(N)]
     own, *near = march(scalar_field, place, parameters, parts, depth_total, [far])
     early = all_steps([own, near[0], far, near[1]], "y", (2, 1, 3))
-    turned = turn(place, all_steps(near[2:], "x", (1, 2, 3)))
-    by_x = all_steps(merge_y(place, early, turned[:1]), "x", (1, 2, 3))
-    mine, send = merge_x(place, by_x, all_steps(turned, "y", (2, 1, 3)))
-    pieces = merge_core(place, mine, exchange(send, "core", 1))
-    return assemble(place, all_steps(pieces, "z", (2, 1, 3)))
+    turned = turn(all_steps(near[2:], "x", (1, 2, 3)))
+    by_x = all_steps(merge_y([merge_pair(early[0], early[2]), early[1], early[3]], turned[:1]), "x", (1, 2, 3))
+    mine, send = merge_x(by_x, all_steps(turned, "y", (2, 1, 3)))
+    pieces = merge_core(mine, exchange(send, "core", 1))
+    return assemble(all_steps(pieces, "z", (2, 1, 3)))
 
 
 def solution(mesh):

time: 72.7 us -> 70.6 us (0.971)
  Pallas kernels: 21.2 us -> 18.5 us
    pallas_call x5 -> x6, Pallas kernels: 4.08 us -> 1.35 us  [the longest x1 0.68 us: assemble(): pl.pallas_call(assemble_kernel, in_specs=vmem_specs(4), out_specs=pl.Bloc...]
  transfers between devices with their start and end apart: 16 -> 16, of which waited for: 11 -> 10; matrix products, arithmetic and copies ran while one was open for 0% -> 0% of each run, Pallas kernels for 19% -> 18%
where the time goes in v5:
time: 70.6 us; the launch traced here: 70.4 us
  waiting for transfers between devices  27.1 us (38%)
  starting transfers between devices  23.3 us (33%)
  Pallas kernels  18.5 us (26%)
  other arithmetic  0.84 us (1%)
  between operations  0.71 us (1%)
    ppermute x16, waiting for transfers between devices, exchange(): lax.ppermute(value, ('depth', 'tile'), [(i, target(i)) for i in range(2 *...  27.1 us
    ppermute x16, starting transfers between devices, exchange(): lax.ppermute(value, ('depth', 'tile'), [(i, target(i)) for i in range(2 *...  23.3 us
    pallas_call x2, Pallas kernels, march(): pl.pallas_call(functools.partial(march_kernel, sizes=sizes, depth_total=d...  17.1 us
  transfers between devices with their start and end apart: 16, of which 10 were waited for; matrix products, arithmetic and copies ran while one was open for 0% of the time, Pallas kernels for 18%

profile of v5, /device:TPU:6, one launch (start us, length us, event | category | flops | bytes accessed | tf_op | source)
XLA Modules:
  0.0 70.4 jit_solution(7964301772946194437)
XLA Ops:
  0.7 0.8 %broadcast_select_fusion.numbers = f32[2,2,3]{2,1,0:T(2,128)S(1)} fusion(pred[2]{0:T(512)(128)(4,1)S(1)} %iota_compare_fusion, f32[2,3]{1,0:T(2,128)} %bitcast.5, f32[2]{0:T(128)} %param.7), kind=kLoop, calls=%fused_computation | loop fusion | flops 12 | bytes 82 | tf_op jit(solution)/shard_map/jit(_where)/select_n | solution.py:314
  1.5 4.7 %march.2.refs_7_ = f32[1544,128]{1,0:T(8,128)S(1)} custom-call(s32[4]{0:T(128)S(1)} %pad_add_fusion.place, f32[2,2,3]{2,1,0:T(2,128)S(1)} %broadcast_select_fusion.numbers, s32[1,1]{1,0:T(1,128)S(6)} %copy.5.own_rank, f32[16,1,512,512]{3,2,1,0:T(8,128)} %refs_6_.1), custom_call_target="tpu_custom_call" | custom-call | flops 420000000 | bytes 1 | tf_op jit(solution)/shard_map/march/pallas_call | solution.py:109
  6.2 3.3 %collective-permute-start = (f32[1544,128]{1,0:T(8,128)S(1)}, f32[1544,128]{1,0:T(8,128)S(1)}, u32[]{:S(2)}, u32[]{:S(2)}) collective-permute-start(f32[1544,128]{1,0:T(8,128)S(1)} %march.2.refs_7_), channel_id=1, source_target_pairs={{0,64},{1,65},{2,66},{3,67},{4,68},{5,69},{6,70},{7,71},{8,72},{9,... | collective-permute-start | bytes 2371592 | tf_op jit(solution)/shard_map/ppermute | solution.py:303
  9.4 12.5 %march.3 = (f32[1544,128]{1,0:T(8,128)S(1)}, f32[1544,128]{1,0:T(8,128)S(1)}, f32[1544,128]{1,0:T(8,128)S(1)}, f32[520,128]{1,0:T(8,128)S(1)}, f32[520,128]{1,0:...) custom-call(s32[4]{0:T(128)S(1)} %pad_add_fusion.place, f32[2,2,3]{2,1,0:T(2,128)S(1)} %broadcast_select_fusion.numbers, ...), custom_call_target="tpu_custom_call" | custom-call | flops 1420000000 | bytes 1 | tf_op jit(solution)/shard_map/march/pallas_call | solution.py:109
  23.5 2.4 %collective-permute-start.4 = (f32[520,128]{1,0:T(8,128)S(1)}, f32[520,128]{1,0:T(8,128)S(1)}, u32[]{:S(2)}, u32[]{:S(2)}) collective-permute-start(f32[520,128]{1,0:T(8,128)S(1)} %get-tuple-element.31), channel_id=1, source_target_pairs={{0,16},{1,17},{2,18},{3,19},{4,20},{5,21},{6,22},{7,23},{8,24},{9,... | collective-permute-start | bytes 798728 | tf_op jit(solution)/shard_map/ppermute | solution.py:303
  25.9 5.4 %collective-permute-done.3.refs_1_ = f32[520,128]{1,0:T(8,128)S(1)} collective-permute-done((f32[520,128]{1,0:T(8,128)S(1)}, f32[520,128]{1,0:T(8,128)S(1)}, u32[]{:S(2)}, u32[]{:S(2)}) %collective-permute-start.3) | collective-permute-done | bytes 266272 | tf_op jit(solution)/shard_map/ppermute | solution.py:303
  31.3 0.8 %collective-permute-start.5 = (f32[520,128]{1,0:T(8,128)S(1)}, f32[520,128]{1,0:T(8,128)S(1)}, u32[]{:S(2)}, u32[]{:S(2)}) collective-permute-start(f32[520,128]{1,0:T(8,128)S(1)} %get-tuple-element.32), channel_id=1, source_target_pairs={{0,24},{1,25},{2,26},{3,27},{4,28},{5,29},{6,30},{7,31},{8,0},{9,1... | collective-permute-start | bytes 798728 | tf_op jit(solution)/shard_map/ppermute | solution.py:303
  32.3 6.6 %collective-permute-done.5.refs_3_ = f32[520,128]{1,0:T(8,128)S(1)} collective-permute-done((f32[520,128]{1,0:T(8,128)S(1)}, f32[520,128]{1,0:T(8,128)S(1)}, u32[]{:S(2)}, u32[]{:S(2)}) %collective-permute-start.5) | collective-permute-done | bytes 266272 | tf_op jit(solution)/shard_map/ppermute | solution.py:303
  39.0 0.8 %collective-permute-start.9 = (f32[544,128]{1,0:T(8,128)S(1)}, f32[544,128]{1,0:T(8,128)S(1)}, u32[]{:S(2)}, u32[]{:S(2)}) collective-permute-start(f32[544,128]{1,0:T(8,128)S(1)} %get-tuple-element.38), channel_id=1, source_target_pairs={{0,32},{1,33},{2,34},{3,35},{4,36},{5,37},{6,38},{7,39},{8,40},{9,... | collective-permute-start | bytes 835592 | tf_op jit(solution)/shard_map/ppermute | solution.py:303
  39.7 2.5 %collective-permute-start.10 = (f32[544,128]{1,0:T(8,128)S(1)}, f32[544,128]{1,0:T(8,128)S(1)}, u32[]{:S(2)}, u32[]{:S(2)}) collective-permute-start(f32[544,128]{1,0:T(8,128)S(1)} %get-tuple-element.39), channel_id=1, source_target_pairs={{0,64},{1,65},{2,66},{3,67},{4,68},{5,69},{6,70},{7,71},{8,72},{9,... | collective-permute-start | bytes 835592 | tf_op jit(solution)/shard_map/ppermute | solution.py:303
  42.2 1.6 %collective-permute-start.11 = (f32[544,128]{1,0:T(8,128)S(1)}, f32[544,128]{1,0:T(8,128)S(1)}, u32[]{:S(2)}, u32[]{:S(2)}) collective-permute-start(f32[544,128]{1,0:T(8,128)S(1)} %get-tuple-element.40), channel_id=1, source_target_pairs={{0,96},{1,97},{2,98},{3,99},{4,100},{5,101},{6,102},{7,103},{8,104... | collective-permute-start | bytes 835592 | tf_op jit(solution)/shard_map/ppermute | solution.py:303
  43.9 1.7 %collective-permute-done.1.refs_1_ = f32[1544,128]{1,0:T(8,128)S(1)} collective-permute-done((f32[1544,128]{1,0:T(8,128)S(1)}, f32[1544,128]{1,0:T(8,128)S(1)}, u32[]{:S(2)}, u32[]{:S(2)}) %collective-permute-start.1) | collective-permute-done | bytes 790560 | tf_op jit(solution)/shard_map/ppermute | solution.py:303
  46.3 2.4 %collective-permute-start.7 = (f32[392,128]{1,0:T(8,128)S(1)}, f32[392,128]{1,0:T(8,128)S(1)}, u32[]{:S(2)}, u32[]{:S(2)}) collective-permute-start(f32[392,128]{1,0:T(8,128)S(1)} %get-tuple-element.36), channel_id=1, source_target_pairs={{0,16},{1,17},{2,18},{3,19},{4,20},{5,21},{6,22},{7,23},{8,24},{9,... | collective-permute-start | bytes 602120 | tf_op jit(solution)/shard_map/ppermute | solution.py:303
  48.8 2.8 %collective-permute-done.9.refs_5_ = f32[544,128]{1,0:T(8,128)S(1)} collective-permute-done((f32[544,128]{1,0:T(8,128)S(1)}, f32[544,128]{1,0:T(8,128)S(1)}, u32[]{:S(2)}, u32[]{:S(2)}) %collective-permute-start.9) | collective-permute-done | bytes 278560 | tf_op jit(solution)/shard_map/ppermute | solution.py:303
  51.6 0.8 %collective-permute-start.8 = (f32[392,128]{1,0:T(8,128)S(1)}, f32[392,128]{1,0:T(8,128)S(1)}, u32[]{:S(2)}, u32[]{:S(2)}) collective-permute-start(f32[392,128]{1,0:T(8,128)S(1)} %get-tuple-element.37), channel_id=1, source_target_pairs={{0,24},{1,25},{2,26},{3,27},{4,28},{5,29},{6,30},{7,31},{8,0},{9,1... | collective-permute-start | bytes 602120 | tf_op jit(solution)/shard_map/ppermute | solution.py:303
  52.4 3.6 %collective-permute-done.10.refs_6_ = f32[544,128]{1,0:T(8,128)S(1)} collective-permute-done((f32[544,128]{1,0:T(8,128)S(1)}, f32[544,128]{1,0:T(8,128)S(1)}, u32[]{:S(2)}, u32[]{:S(2)}) %collective-permute-start.10) | collective-permute-done | bytes 278560 | tf_op jit(solution)/shard_map/ppermute | solution.py:303
  56.0 2.6 %collective-permute-done.8.refs_3_ = f32[392,128]{1,0:T(8,128)S(1)} collective-permute-done((f32[392,128]{1,0:T(8,128)S(1)}, f32[392,128]{1,0:T(8,128)S(1)}, u32[]{:S(2)}, u32[]{:S(2)}) %collective-permute-start.8) | collective-permute-done | bytes 200736 | tf_op jit(solution)/shard_map/ppermute | solution.py:303
  58.9 1.3 %collective-permute-done.12.other = f32[264,128]{1,0:T(8,128)S(1)} collective-permute-done((f32[264,128]{1,0:T(8,128)S(1)}, f32[264,128]{1,0:T(8,128)S(1)}, u32[]{:S(2)}, u32[]{:S(2)}) %collective-permute-start.12) | collective-permute-done | bytes 135200 | tf_op jit(solution)/shard_map/ppermute | solution.py:303
  60.3 2.0 %collective-permute-start.13 = (f32[64,128]{1,0:T(8,128)S(1)}, f32[64,128]{1,0:T(8,128)S(1)}, u32[]{:S(2)}, u32[]{:S(2)}) collective-permute-start(f32[64,128]{1,0:T(8,128)S(1)} %get-tuple-element.44), channel_id=1, source_target_pairs={{0,1},{1,2},{2,3},{3,0},{4,5},{5,6},{6,7},{7,4},{8,9},{9,10},{10,1... | collective-permute-start | bytes 98312 | tf_op jit(solution)/shard_map/ppermute | solution.py:303
  62.2 3.6 %collective-permute-start.14 = (f32[64,128]{1,0:T(8,128)S(1)}, f32[64,128]{1,0:T(8,128)S(1)}, u32[]{:S(2)}, u32[]{:S(2)}) collective-permute-start(f32[64,128]{1,0:T(8,128)S(1)} %get-tuple-element.45), channel_id=1, source_target_pairs={{0,2},{1,3},{2,0},{3,1},{4,6},{5,7},{6,4},{7,5},{8,10},{9,11},{10,... | collective-permute-start | bytes 98312 | tf_op jit(solution)/shard_map/ppermute | solution.py:303
  65.8 1.0 %collective-permute-start.15 = (f32[64,128]{1,0:T(8,128)S(1)}, f32[64,128]{1,0:T(8,128)S(1)}, u32[]{:S(2)}, u32[]{:S(2)}) collective-permute-start(f32[64,128]{1,0:T(8,128)S(1)} %get-tuple-element.46), channel_id=1, source_target_pairs={{0,3},{1,0},{2,1},{3,2},{4,7},{5,4},{6,5},{7,6},{8,11},{9,8},{10,9... | collective-permute-start | bytes 98312 | tf_op jit(solution)/shard_map/ppermute | solution.py:303
  66.8 1.2 %collective-permute-done.14.refs_2_ = f32[64,128]{1,0:T(8,128)S(1)} collective-permute-done((f32[64,128]{1,0:T(8,128)S(1)}, f32[64,128]{1,0:T(8,128)S(1)}, u32[]{:S(2)}, u32[]{:S(2)}) %collective-permute-start.14) | collective-permute-done | bytes 32800 | tf_op jit(solution)/shard_map/ppermute | solution.py:303
  68.1 1.7 %collective-permute-done.15.refs_3_ = f32[64,128]{1,0:T(8,128)S(1)} collective-permute-done((f32[64,128]{1,0:T(8,128)S(1)}, f32[64,128]{1,0:T(8,128)S(1)}, u32[]{:S(2)}, u32[]{:S(2)}) %collective-permute-start.15) | collective-permute-done | bytes 32800 | tf_op jit(solution)/shard_map/ppermute | solution.py:303
  69.7 0.7 assemble.1
  (19 shorter events, 3.2 us)
Async XLA Ops:
  6.2 36.1 %collective-permute-start = (f32[1544,128]{1,0:T(8,128)S(1)}, f32[1544,128]{1,0:T(8,128)S(1)}, u32[]{:S(2)}, u32[]{:S(2)}) collective-permute-start(f32[1544,128]{1,0:T(8,128)S(1)} %march.2.refs_7_), channel_id=1, source_target_pairs={{0,64},{1,65},{2,66},{3,67},{4,68},{5,69},{6,70},{7,71},{8,72},{9,... | collective-permute-start | bytes 2371592 | tf_op jit(solution)/shard_map/ppermute | solution.py:303
  21.9 9.4 %collective-permute-start.3 = (f32[520,128]{1,0:T(8,128)S(1)}, f32[520,128]{1,0:T(8,128)S(1)}, u32[]{:S(2)}, u32[]{:S(2)}) collective-permute-start(f32[520,128]{1,0:T(8,128)S(1)} %get-tuple-element.30), channel_id=1, source_target_pairs={{0,8},{1,9},{2,10},{3,11},{4,12},{5,13},{6,14},{7,15},{8,16},{9,17... | collective-permute-start | bytes 798728 | tf_op jit(solution)/shard_map/ppermute | solution.py:303
  22.4 23.1 %collective-permute-start.1 = (f32[1544,128]{1,0:T(8,128)S(1)}, f32[1544,128]{1,0:T(8,128)S(1)}, u32[]{:S(2)}, u32[]{:S(2)}) collective-permute-start(f32[1544,128]{1,0:T(8,128)S(1)} %get-tuple-element.27), channel_id=1, source_target_pairs={{0,32},{1,33},{2,34},{3,35},{4,36},{5,37},{6,38},{7,39},{8,40},{9,... | collective-permute-start | bytes 2371592 | tf_op jit(solution)/shard_map/ppermute | solution.py:303
  23.1 22.5 %collective-permute-start.2 = (f32[1544,128]{1,0:T(8,128)S(1)}, f32[1544,128]{1,0:T(8,128)S(1)}, u32[]{:S(2)}, u32[]{:S(2)}) collective-permute-start(f32[1544,128]{1,0:T(8,128)S(1)} %get-tuple-element.28), channel_id=1, source_target_pairs={{0,96},{1,97},{2,98},{3,99},{4,100},{5,101},{6,102},{7,103},{8,104... | collective-permute-start | bytes 2371592 | tf_op jit(solution)/shard_map/ppermute | solution.py:303
  23.5 8.8 %collective-permute-start.4 = (f32[520,128]{1,0:T(8,128)S(1)}, f32[520,128]{1,0:T(8,128)S(1)}, u32[]{:S(2)}, u32[]{:S(2)}) collective-permute-start(f32[520,128]{1,0:T(8,128)S(1)} %get-tuple-element.31), channel_id=1, source_target_pairs={{0,16},{1,17},{2,18},{3,19},{4,20},{5,21},{6,22},{7,23},{8,24},{9,... | collective-permute-start | bytes 798728 | tf_op jit(solution)/shard_map/ppermute | solution.py:303
  31.3 7.6 %collective-permute-start.5 = (f32[520,128]{1,0:T(8,128)S(1)}, f32[520,128]{1,0:T(8,128)S(1)}, u32[]{:S(2)}, u32[]{:S(2)}) collective-permute-start(f32[520,128]{1,0:T(8,128)S(1)} %get-tuple-element.32), channel_id=1, source_target_pairs={{0,24},{1,25},{2,26},{3,27},{4,28},{5,29},{6,30},{7,31},{8,0},{9,1... | collective-permute-start | bytes 798728 | tf_op jit(solution)/shard_map/ppermute | solution.py:303
  39.0 12.6 %collective-permute-start.9 = (f32[544,128]{1,0:T(8,128)S(1)}, f32[544,128]{1,0:T(8,128)S(1)}, u32[]{:S(2)}, u32[]{:S(2)}) collective-permute-start(f32[544,128]{1,0:T(8,128)S(1)} %get-tuple-element.38), channel_id=1, source_target_pairs={{0,32},{1,33},{2,34},{3,35},{4,36},{5,37},{6,38},{7,39},{8,40},{9,... | collective-permute-start | bytes 835592 | tf_op jit(solution)/shard_map/ppermute | solution.py:303
  39.7 16.2 %collective-permute-start.10 = (f32[544,128]{1,0:T(8,128)S(1)}, f32[544,128]{1,0:T(8,128)S(1)}, u32[]{:S(2)}, u32[]{:S(2)}) collective-permute-start(f32[544,128]{1,0:T(8,128)S(1)} %get-tuple-element.39), channel_id=1, source_target_pairs={{0,64},{1,65},{2,66},{3,67},{4,68},{5,69},{6,70},{7,71},{8,72},{9,... | collective-permute-start | bytes 835592 | tf_op jit(solution)/shard_map/ppermute | solution.py:303
  42.2 13.8 %collective-permute-start.11 = (f32[544,128]{1,0:T(8,128)S(1)}, f32[544,128]{1,0:T(8,128)S(1)}, u32[]{:S(2)}, u32[]{:S(2)}) collective-permute-start(f32[544,128]{1,0:T(8,128)S(1)} %get-tuple-element.40), channel_id=1, source_target_pairs={{0,96},{1,97},{2,98},{3,99},{4,100},{5,101},{6,102},{7,103},{8,104... | collective-permute-start | bytes 835592 | tf_op jit(solution)/shard_map/ppermute | solution.py:303
  45.8 10.2 %collective-permute-start.6 = (f32[392,128]{1,0:T(8,128)S(1)}, f32[392,128]{1,0:T(8,128)S(1)}, u32[]{:S(2)}, u32[]{:S(2)}) collective-permute-start(f32[392,128]{1,0:T(8,128)S(1)} %get-tuple-element.35), channel_id=1, source_target_pairs={{0,8},{1,9},{2,10},{3,11},{4,12},{5,13},{6,14},{7,15},{8,16},{9,17... | collective-permute-start | bytes 602120 | tf_op jit(solution)/shard_map/ppermute | solution.py:303
  46.3 9.7 %collective-permute-start.7 = (f32[392,128]{1,0:T(8,128)S(1)}, f32[392,128]{1,0:T(8,128)S(1)}, u32[]{:S(2)}, u32[]{:S(2)}) collective-permute-start(f32[392,128]{1,0:T(8,128)S(1)} %get-tuple-element.36), channel_id=1, source_target_pairs={{0,16},{1,17},{2,18},{3,19},{4,20},{5,21},{6,22},{7,23},{8,24},{9,... | collective-permute-start | bytes 602120 | tf_op jit(solution)/shard_map/ppermute | solution.py:303
  51.6 7.0 %collective-permute-start.8 = (f32[392,128]{1,0:T(8,128)S(1)}, f32[392,128]{1,0:T(8,128)S(1)}, u32[]{:S(2)}, u32[]{:S(2)}) collective-permute-start(f32[392,128]{1,0:T(8,128)S(1)} %get-tuple-element.37), channel_id=1, source_target_pairs={{0,24},{1,25},{2,26},{3,27},{4,28},{5,29},{6,30},{7,31},{8,0},{9,1... | collective-permute-start | bytes 602120 | tf_op jit(solution)/shard_map/ppermute | solution.py:303
  58.8 1.4 %collective-permute-start.12 = (f32[264,128]{1,0:T(8,128)S(1)}, f32[264,128]{1,0:T(8,128)S(1)}, u32[]{:S(2)}, u32[]{:S(2)}) collective-permute-start(f32[264,128]{1,0:T(8,128)S(1)} %get-tuple-element.42), channel_id=1, source_target_pairs={{0,4},{1,5},{2,6},{3,7},{4,0},{5,1},{6,2},{7,3},{8,12},{9,13},{10,... | collective-permute-start | bytes 405512 | tf_op jit(solution)/shard_map/ppermute | solution.py:303
  60.3 6.6 %collective-permute-start.13 = (f32[64,128]{1,0:T(8,128)S(1)}, f32[64,128]{1,0:T(8,128)S(1)}, u32[]{:S(2)}, u32[]{:S(2)}) collective-permute-start(f32[64,128]{1,0:T(8,128)S(1)} %get-tuple-element.44), channel_id=1, source_target_pairs={{0,1},{1,2},{2,3},{3,0},{4,5},{5,6},{6,7},{7,4},{8,9},{9,10},{10,1... | collective-permute-start | bytes 98312 | tf_op jit(solution)/shard_map/ppermute | solution.py:303
  62.2 5.8 %collective-permute-start.14 = (f32[64,128]{1,0:T(8,128)S(1)}, f32[64,128]{1,0:T(8,128)S(1)}, u32[]{:S(2)}, u32[]{:S(2)}) collective-permute-start(f32[64,128]{1,0:T(8,128)S(1)} %get-tuple-element.45), channel_id=1, source_target_pairs={{0,2},{1,3},{2,0},{3,1},{4,6},{5,7},{6,4},{7,5},{8,10},{9,11},{10,... | collective-permute-start | bytes 98312 | tf_op jit(solution)/shard_map/ppermute | solution.py:303
  65.8 3.9 %collective-permute-start.15 = (f32[64,128]{1,0:T(8,128)S(1)}, f32[64,128]{1,0:T(8,128)S(1)}, u32[]{:S(2)}, u32[]{:S(2)}) collective-permute-start(f32[64,128]{1,0:T(8,128)S(1)} %get-tuple-element.46), channel_id=1, source_target_pairs={{0,3},{1,0},{2,1},{3,2},{4,7},{5,4},{6,5},{7,6},{8,11},{9,8},{10,9... | collective-permute-start | bytes 98312 | tf_op jit(solution)/shard_map/ppermute | solution.py:303
